TPU v7x, 128 devices: a whole 4x4x4 slice. The times are simulated.
128 devices in a mesh: band: 32 (over z, x, core), tile: 4 (over y).
Axes of the slice: x: 4, y: 4, z: 4, core: 2. Of those that a mesh axis runs over, the one named last changes fastest.
Arguments:
- source: bfloat16 [40, 1048576], P(None, ('band', 'tile')), may hold values from -6 to 6
- regrid_weights: bfloat16 [8192, 4, 128, 128], P(('band', 'tile')), may hold values from -0.5 to 0.5
- dest_group: int32 [8192, 4], P(('band', 'tile')), may hold values from 0 to 127, all different within a row; in each aligned block of 64 rows (0 to 63, 64 to 127, ...) at most 6 rows name the same one
- dest_block: int32 [8192, 4], P(('band', 'tile')), may hold values from 0 to 191
- seam_table: int32 [12, 4, 3], replicated, may hold values from 0 to 11, as said below
- conv1_weight: bfloat16 [9, 128, 40], replicated, may hold values from -0.3125 to 0.3125
- conv1_bias: float32 [128], replicated, may hold values from -3 to 3
- conv2_weight: bfloat16 [9, 128, 128], replicated, may hold values from -0.1875 to 0.1875
- conv2_bias: float32 [128], replicated, may hold values from -3 to 3
Outputs:
- features: bfloat16 [128, 12, 512, 512], P(None, None, 'band', 'tile')
Inputs may be any that keep to these rules, and one draw needn't show every extreme that they name: `dest_group`: within the rows of one device (aligned blocks of 64 rows) no value appears more than 6 times, and a row's 4 values differ. `seam_table`: entries 0 and 1 name a face and a side (0 to 3). Joins are symmetric: if side s of face f is joined to side s2 of face g, side s2 of face g is joined to side s of face f with the same reversal entry. No side is joined to itself. Entry 2 is 0 or 1.
All inputs are finite; a program needn't handle non-finite values.
Results may differ from a plain program's by a relative error of at most 0.0058.
Values may be sent and summed in bfloat16 or wider, within the bound.
No kernel may reach another device: no remote copies, remote signals or barrier semaphores. Data moves between devices by JAX's collectives and lax.ppermute only.
A program may use at most 320 MiB of HBM per device.

v0:
```python
import functools

import jax
import jax.numpy as jnp
import numpy as np
from jax import lax
from jax.experimental import pallas as pl
from jax.experimental.pallas import tpu as pltpu
from jax.sharding import PartitionSpec as P

BF = jnp.bfloat16
F32 = jnp.float32
AXES = ("band", "tile")
VMEM_LIMIT = 56 * 1024 * 1024


def regrid_kernel(pos_ref, src_ref, w_ref, out_ref, *, blocks, top, length):
    step = pl.program_id(0)
    for s in range(blocks):
        lhs = src_ref[:, s * length : (s + 1) * length]
        rhs = jnp.concatenate([w_ref[s, k] for k in range(top)], axis=1)
        val = jnp.dot(lhs, rhs, preferred_element_type=F32).astype(BF)
        for k in range(top):
            where = pos_ref[(step * blocks + s) * top + k]
            out_ref[where] = val[:, k * length : (k + 1) * length]


def regrid(source, weights, position, slots):
    fields = source.shape[0]
    count, top, length = weights.shape[0], weights.shape[1], weights.shape[2]
    blocks = 8
    return pl.pallas_call(
        functools.partial(regrid_kernel, blocks=blocks, top=top, length=length),
        grid_spec=pltpu.PrefetchScalarGridSpec(
            num_scalar_prefetch=1,
            grid=(count // blocks,),
            in_specs=[
                pl.BlockSpec((fields, blocks * length), lambda i, p: (0, i)),
                pl.BlockSpec((blocks, top, length, length), lambda i, p: (i, 0, 0, 0)),
            ],
            out_specs=pl.BlockSpec((slots, fields, length), lambda i, p: (0, 0, 0)),
        ),
        out_shape=jax.ShapeDtypeStruct((slots, fields, length), BF),
        compiler_params=pltpu.CompilerParams(vmem_limit_bytes=VMEM_LIMIT),
        cost_estimate=pl.CostEstimate(
            flops=2 * count * top * length * length * fields, bytes_accessed=17_000_000, transcendentals=0
        ),
    )(position, source, weights)


def edge_columns(piece, lane, at, low, high):
    cols = piece.shape[1]
    here = lane == at
    low = jnp.where(here, pltpu.roll(piece, at, 1) if at else piece, low)
    high = jnp.where(here, pltpu.roll(piece, (at + 1) % cols, 1), high)
    return low, high


def place_kernel(slot_ref, in_ref, out_ref, low_ref, high_ref, acc_ref, *, chunk):
    step = pl.program_id(0)

    @pl.when(step == 0)
    def _():
        acc_ref[...] = jnp.zeros_like(acc_ref)

    def body(i, carry):
        where = slot_ref[step * chunk + i]
        acc_ref[where] += in_ref[i].astype(F32)
        return carry

    lax.fori_loop(0, chunk, body, 0, unroll=8)

    @pl.when(step == pl.num_programs(0) - 1)
    def _():
        count, chans, cols = out_ref.shape
        lane = lax.broadcasted_iota(jnp.int32, (chans, cols), 1)
        for half in range(2):
            low = high = jnp.zeros((chans, cols), F32)
            for at in range(min(cols, count - half * cols)):
                piece = acc_ref[half * cols + at]
                out_ref[half * cols + at] = piece.astype(BF)
                low, high = edge_columns(piece, lane, at, low, high)
            low_ref[:, half * cols : (half + 1) * cols] = low.astype(BF)
            high_ref[:, half * cols : (half + 1) * cols] = high.astype(BF)


def place(arrived, slots, count):
    items, fields, length = arrived.shape
    chunk = 96
    return pl.pallas_call(
        functools.partial(place_kernel, chunk=chunk),
        grid_spec=pltpu.PrefetchScalarGridSpec(
            num_scalar_prefetch=1,
            grid=(items // chunk,),
            in_specs=[pl.BlockSpec((chunk, fields, length), lambda i, p: (i, 0, 0))],
            out_specs=[
                pl.BlockSpec((count, fields, length), lambda i, p: (0, 0, 0)),
                pl.BlockSpec((fields, 2 * length), lambda i, p: (0, 0)),
                pl.BlockSpec((fields, 2 * length), lambda i, p: (0, 0)),
            ],
            scratch_shapes=[pltpu.VMEM((count + 1, fields, length), F32)],
        ),
        out_shape=[
            jax.ShapeDtypeStruct((count, fields, length), BF),
            jax.ShapeDtypeStruct((fields, 2 * length), BF),
            jax.ShapeDtypeStruct((fields, 2 * length), BF),
        ],
        compiler_params=pltpu.CompilerParams(vmem_limit_bytes=VMEM_LIMIT),
    )(slots, arrived)


def gelu(v):
    return 0.5 * v * (1.0 + lax.erf(v * np.float32(1.0 / np.sqrt(2.0))))


def conv_kernel(w_ref, b_ref, x_ref, top_ref, bot_ref, l_ref, r_ref, *refs, last):
    if last:
        o_ref, p_ref, s_ref = refs
    else:
        o_ref, low_ref, high_ref, p_ref = refs
    faces, rows, chans, cols = x_ref.shape
    depth = p_ref.shape[1]
    hid = b_ref.shape[0] // 2
    step = pl.program_id(0)
    lane = lax.broadcasted_iota(jnp.int32, (chans, cols), 1)
    spare = depth - 3 * chans
    span = rows + 2
    group = pl.ds(pl.multiple_of((step // 3) * cols, cols), cols)
    back = lax.rem(cols - lax.rem(step, 3) * (faces * span), cols)
    left = pltpu.roll(l_ref[:, group].astype(F32), back, 1)
    right = pltpu.roll(r_ref[:, group].astype(F32), back, 1)
    for f in range(faces):
        for r in range(span):
            row = top_ref[f] if r == 0 else bot_ref[f] if r == rows + 1 else x_ref[f, r - 1]
            mid = row.astype(F32)
            at = f * span + r
            lo = jnp.where(lane == 0, left[:, at : at + 1], pltpu.roll(mid, 1, 1))
            hi = jnp.where(lane == cols - 1, right[:, at : at + 1], pltpu.roll(mid, cols - 1, 1))
            parts = [lo, mid, hi]
            if spare:
                parts.append(jnp.zeros((spare, cols), F32))
            p_ref[r, :, f * cols : (f + 1) * cols] = jnp.concatenate(parts, axis=0).astype(BF)
    bias = b_ref[...]
    out_lane = lax.broadcasted_iota(jnp.int32, (hid, cols), 1)
    low = high = jnp.zeros((hid, cols), F32)
    for rp in range(rows // 2):
        patch = p_ref[2 * rp : 2 * rp + 4].reshape(4 * depth, faces * cols)
        acc = jnp.dot(w_ref[...], patch, preferred_element_type=F32) + bias
        acc = gelu(acc)
        for d in range(2):
            for f in range(faces):
                piece = acc[d * hid : (d + 1) * hid, f * cols : (f + 1) * cols]
                if last:
                    s_ref[f, (2 * rp + d) * hid : (2 * rp + d + 1) * hid, :] = piece
                else:
                    o_ref[f, 2 * rp + d] = piece.astype(BF)
                    low, high = edge_columns(piece, out_lane, f * rows + 2 * rp + d, low, high)
    if last:
        for f in range(faces):
            for o in range(hid):
                o_ref[o, f] = s_ref[f, pl.ds(o, rows, stride=hid), :].astype(BF)
    else:
        per = cols // (faces * rows)
        ahead = lax.rem(step, per) * (faces * rows)
        half = pl.ds(pl.multiple_of((step // per) * cols, cols), cols)
        fresh = lax.rem(step, per) == 0
        for ref, value in ((low_ref, low), (high_ref, high)):
            value = pltpu.roll(value, ahead, 1).astype(BF)

            @pl.when(fresh)
            def _(ref=ref, value=value):
                ref[:, half] = value

            @pl.when(jnp.logical_not(fresh))
            def _(ref=ref, value=value):
                ref[:, half] += value


def conv(x, top, bottom, left, right, weight, bias, last):
    face_count, rows, chans, cols = x.shape
    depth = weight.shape[1] // 4
    hid = weight.shape[0] // 2
    faces = 2
    scratch = [pltpu.VMEM((rows + 2, depth, faces * cols), BF)]
    if last:
        out_shape = jax.ShapeDtypeStruct((hid, face_count, rows, cols), BF)
        out_spec = pl.BlockSpec((hid, faces, rows, cols), lambda i: (0, i, 0, 0))
        scratch.append(pltpu.VMEM((faces, rows * hid, cols), F32))
    else:
        out_shape = [jax.ShapeDtypeStruct((face_count, rows, hid, cols), BF)]
        out_shape += [jax.ShapeDtypeStruct((hid, 2 * cols), BF)] * 2
        out_spec = [pl.BlockSpec((faces, rows, hid, cols), lambda i: (i, 0, 0, 0))]
        out_spec += [pl.BlockSpec((hid, 2 * cols), lambda i: (0, 0))] * 2
    return pl.pallas_call(
        functools.partial(conv_kernel, last=last),
        grid=(face_count // faces,),
        in_specs=[
            pl.BlockSpec(weight.shape, lambda i: (0, 0)),
            pl.BlockSpec(bias.shape, lambda i: (0, 0)),
            pl.BlockSpec((faces, rows, chans, cols), lambda i: (i, 0, 0, 0)),
            pl.BlockSpec((faces, chans, cols), lambda i: (i, 0, 0)),
            pl.BlockSpec((faces, chans, cols), lambda i: (i, 0, 0)),
            pl.BlockSpec(left.shape, lambda i: (0, 0)),
            pl.BlockSpec(right.shape, lambda i: (0, 0)),
        ],
        out_specs=out_spec,
        out_shape=out_shape,
        scratch_shapes=scratch,
        compiler_params=pltpu.CompilerParams(vmem_limit_bytes=VMEM_LIMIT),
    )(weight, bias, x, top, bottom, left, right)


def wide_weight(weight, depth):
    taps, hid, chans = weight.shape
    rows = weight.reshape(3, 3, hid, chans).transpose(2, 0, 1, 3).reshape(hid, 3, 3 * chans)
    rows = jnp.pad(rows, ((0, 0), (0, 0), (0, depth - 3 * chans)))
    first = jnp.pad(rows, ((0, 0), (0, 1), (0, 0)))
    second = jnp.pad(rows, ((0, 0), (1, 0), (0, 0)))
    return jnp.stack([first, second]).reshape(2 * hid, 4 * depth)


class Plan:
    def __init__(self, bands, tiles):
        self.bands, self.tiles = bands, tiles
        self.per = bands // tiles
        per, last = self.per, bands - 1
        rounds = per + 1
        count = bands * tiles
        self.pairs = [[] for _ in range(rounds)]
        self.sends_row = np.zeros((rounds, count), np.int32)
        self.unit = np.zeros((rounds, count), np.int32)
        self.row_round = np.full((count, per), rounds, np.int32)
        self.col_round = np.full((count,), rounds, np.int32)

        def join(r, row_dev, col_dev, j):
            if row_dev == col_dev:
                self.sends_row[r, row_dev] = 1
                return
            self.pairs[r] += [(row_dev, col_dev), (col_dev, row_dev)]
            self.sends_row[r, row_dev] = 1
            self.unit[r, row_dev] = j
            self.row_round[row_dev, j] = r
            self.col_round[col_dev] = r

        for j in range(per):
            for t in range(tiles):
                join(per if (t, j) == (tiles - 1, 0) else j, t, (per * t + j) * tiles, j)
                join(
                    per if (t, j) == (0, per - 1) else j,
                    last * tiles + t,
                    (per * t + j) * tiles + tiles - 1,
                    j,
                )
        for pairs in self.pairs:
            assert len({a for a, _ in pairs}) == len(pairs) == len({b for _, b in pairs})
        self.flip_row = [
            (b * tiles + t, b * tiles + tiles - 1 - t) for b in (0, last) for t in range(tiles)
        ]
        self.flip_col = [(b * tiles + t, (last - b) * tiles + t) for b in range(bands) for t in (0, tiles - 1)]


def lane18(f, p, span, width):
    return (f // 6) * width + (f % 6) * span + p


def fixed_maps(faces, rows, cols):
    span = rows + 2
    own = np.zeros((3 * cols, 2 * cols), np.float32)
    wrap = np.zeros((4 * cols, 2 * cols), np.float32)
    widen = np.zeros((2 * cols, 2 * cols), np.float32)
    ends = np.zeros((2, 2 * cols, 2 * cols), np.float32)
    corner = np.zeros((2, 4 * cols, cols), np.float32)
    unit_ends = np.zeros((2, 2 * cols, 4 * cols), np.float32)
    for f in range(faces):
        for r in range(rows):
            to = lane18(f, r + 1, span, cols)
            own[f * rows + r, to] = wrap[f * rows + r, to] = widen[f * rows + r, to] = 1
        for which, p in ((0, 0), (1, span - 1)):
            to = lane18(f, p, span, cols)
            own[2 * cols + 16 * which + f, to] = 1
            wrap[(2 + which) * cols + 2 * f, to] = 1
            for side in range(2):
                ends[side, which * cols + 2 * f + side, to] = 1
        for which, r in ((0, 0), (1, rows - 1)):
            for side in range(2):
                corner[which, side * 2 * cols + f * rows + r, 2 * f + side] = 1
        for which, p in ((0, 0), (1, span - 1)):
            for pair in range(2):
                to = pair * 2 * cols + lane18(f, p, span, cols)
                unit_ends[which, pair * cols + 2 * f + which, to] = 1
    back = np.eye(cols)[::-1].copy()
    return [jnp.asarray(m, BF) for m in (own, wrap, widen, ends, corner, unit_ends, back)]


def seam_tables(seam_table, plan, rows, cols):
    band, tile = lax.axis_index("band"), lax.axis_index("tile")
    me = band * plan.tiles + tile
    faces = seam_table.shape[0]
    span = rows + 2
    per, rounds = plan.per, plan.per + 1
    last_band, last_tile = plan.bands - 1, plan.tiles - 1
    static = np.concatenate(
        [
            plan.col_round[:, None],
            np.where(plan.row_round[:, :1] == 0, 0, np.where(plan.row_round[:, :1] == per, 1, 2)),
            np.where(plan.row_round[:, -1:] == per - 1, 0, np.where(plan.row_round[:, -1:] == per, 1, 2)),
            plan.sends_row.T + plan.sends_row.T * (plan.unit.T > 0) * (np.arange(rounds) == per),
        ],
        axis=1,
    ).astype(np.int32)
    static = lax.dynamic_slice_in_dim(jnp.asarray(static), me, 1, 0)[0]
    row = jnp.where(band == 0, seam_table[:, 0], seam_table[:, 1])
    col = jnp.where(tile == 0, seam_table[:, 2], seam_table[:, 3])
    scalars = jnp.concatenate(
        [jnp.stack([band, tile]).astype(jnp.int32), static, row[:, 1], row[:, 0], row[:, 2], jnp.zeros((4,), jnp.int32)]
    )
    lanes = np.full((2, 2 * cols), -1, np.int32)
    for f in range(faces):
        for p in range(span):
            lanes[:, lane18(f, p, span, cols)] = f, p
    face, place = lanes
    line_in = np.concatenate([np.where(face >= 0, face + faces * side, -1) for side in range(4)])
    place_in = np.tile(place, 4)
    col_line = col[:, 1] * faces + col[:, 0]
    hot = jnp.asarray(face[:, None] == np.arange(faces)[None, :])
    want = jnp.sum(jnp.where(hot, col_line[None, :], 0), axis=1)
    turned = jnp.sum(jnp.where(hot, col[:, 2][None, :], 0), axis=1)
    pick = (jnp.asarray(line_in)[:, None] == want[None, :]) & jnp.asarray(
        (place_in[:, None] == place[None, :]) & (face >= 0)[None, :]
    )
    corner = ((band == 0) & jnp.asarray(place == 0)) | ((band == last_band) & jnp.asarray(place == span - 1))
    same_face = (face[:, None] == face[None, :]) & (face >= 0)[None, :]
    keep = jnp.asarray(same_face & (place[:, None] == place[None, :])) & (turned == 0)[None, :]
    flip = jnp.asarray(same_face & (place[:, None] == span - 1 - place[None, :])) & (turned == 1)[None, :]
    join = jnp.concatenate([keep, flip]) & jnp.logical_not(corner)[None, :]
    at = np.arange(cols)
    end_face, end_side = np.where(at < 2 * faces, at // 2, -1), at % 2
    end_turned = jnp.sum(jnp.where(jnp.asarray(end_face[:, None] == np.arange(faces)[None, :]), row[:, 2][None, :], 0), axis=1)
    outer = ((tile == 0) & jnp.asarray(end_side == 0)) | ((tile == last_tile) & jnp.asarray(end_side == 1))
    same_end = (end_face[:, None] == end_face[None, :]) & (end_face >= 0)[None, :]
    keep_end = jnp.asarray(same_end & (end_side[:, None] == end_side[None, :])) & (end_turned == 0)[None, :]
    flip_end = jnp.asarray(same_end & (end_side[:, None] != end_side[None, :])) & (end_turned == 1)[None, :]
    join_end = jnp.concatenate([keep_end, flip_end]) & jnp.logical_not(outer)[None, :]
    return scalars, pick.astype(BF), join.astype(BF), join_end.astype(BF), fixed_maps(faces, rows, cols)


BAND, TILE, COL_ROUND, FIRST_FROM, LAST_FROM, SENDS = 0, 1, 2, 3, 4, 5


def whole(kernel, out_shape, scratch, scalars, *args):
    return pl.pallas_call(
        kernel,
        in_specs=[pl.BlockSpec(memory_space=pltpu.SMEM)] + [pl.BlockSpec(memory_space=pltpu.VMEM)] * len(args),
        out_specs=[pl.BlockSpec(memory_space=pltpu.VMEM)] * len(out_shape),
        out_shape=[jax.ShapeDtypeStruct(s, BF) for s in out_shape],
        scratch_shapes=scratch,
        compiler_params=pltpu.CompilerParams(vmem_limit_bytes=VMEM_LIMIT),
    )(scalars, *args)


def pick2(cond, a, b):
    return lax.select_n(cond, b, a)


def side_by_side(*parts):
    return jnp.concatenate(parts, axis=1)


def move(x, matrix):
    return jnp.dot(x, matrix, preferred_element_type=F32)


def rows_kernel(first_ref, last_ref, left_ref, right_ref, corner_ref, up_ref, down_ref):
    faces = first_ref.shape[0]
    both = side_by_side(left_ref[...], right_ref[...])
    for which, (src, out) in enumerate(((first_ref, up_ref), (last_ref, down_ref))):
        for f in range(faces):
            out[f] = src[f, 0]
        out[faces] = move(both, corner_ref[which]).astype(BF)


def rows_call(x, left, right, corner):
    faces, rows, chans, cols = x.shape
    full = lambda a: pl.BlockSpec(a.shape, lambda i: (0,) * a.ndim)
    out = jax.ShapeDtypeStruct((faces + 1, chans, cols), BF)
    return pl.pallas_call(
        rows_kernel,
        grid=(1,),
        in_specs=[
            pl.BlockSpec((faces, 1, chans, cols), lambda i: (0, 0, 0, 0)),
            pl.BlockSpec((faces, 1, chans, cols), lambda i: (0, rows - 1, 0, 0)),
            full(left),
            full(right),
            full(corner),
        ],
        out_specs=[pl.BlockSpec(out.shape, lambda i: (0, 0, 0))] * 2,
        out_shape=[out] * 2,
        compiler_params=pltpu.CompilerParams(vmem_limit_bytes=VMEM_LIMIT),
    )(x, x, left, right, corner)


def lines_kernel(s_ref, up_ref, down_ref, top_ref, bot_ref, low_ref, high_ref, left_ref, right_ref, own_ref, wrap_ref, ue_ref, *outs, bands, rows):
    messages, cl_ref = outs[:-1], outs[-1]
    per = len(messages) - 1
    faces, (chans, cols) = up_ref.shape[0] - 1, up_ref.shape[1:]
    span = rows + 2
    first_band, first_tile = s_ref[BAND] == 0, s_ref[TILE] == 0
    lane = lax.broadcasted_iota(jnp.int32, (chans, cols), 1)
    top_edge = jnp.zeros((chans, cols), F32)
    for which, ref in enumerate((top_ref, bot_ref)):
        for f in range(faces):
            at = 16 * which + f
            row = ref[f].astype(F32)
            value = pltpu.roll(row, pick2(first_tile, jnp.int32(at), jnp.int32(at + 1)), 1)
            top_edge = jnp.where(lane == at, value, top_edge)
    mine = pick2(first_tile, low_ref[...], high_ref[...])
    theirs = pick2(first_tile, left_ref[...], right_ref[...])
    turn = pick2(first_tile, jnp.int32(0), jnp.int32(cols - 1))
    tc = pltpu.roll(top_ref[faces].astype(F32), turn, 1).astype(BF)
    bc = pltpu.roll(bot_ref[faces].astype(F32), turn, 1).astype(BF)
    own = move(side_by_side(mine, top_edge.astype(BF)), own_ref[...]).astype(BF)
    wrap = move(side_by_side(theirs, tc, bc), wrap_ref[...]).astype(BF)
    cl_ref[...] = side_by_side(pick2(first_tile, own, wrap), pick2(first_tile, wrap, own))
    on_row = jnp.logical_or(first_band, s_ref[BAND] == bands - 1)
    for m in range(per + 1):

        @pl.when(s_ref[SENDS + m] == 0)
        def _(m=m):
            messages[m][...] = cl_ref[...]

    @pl.when(on_row)
    def _():
        ends = side_by_side(pick2(first_band, up_ref[faces], bot_ref[faces]), pick2(first_band, top_ref[faces], down_ref[faces]))
        for g in range(4):
            pieces = [jnp.zeros((chans, cols), F32) for _ in range(per)]
            for i in range(6):
                pair, f = divmod(6 * g + i, faces)
                line = pick2(first_band, up_ref[f], bot_ref[f]) if pair == 0 else pick2(first_band, top_ref[f], down_ref[f])
                line = line.astype(F32)
                for j in range(per):
                    low = i * span + (1 if j == 0 else 0)
                    high = i * span + span - (1 if j == per - 1 else 0)
                    value = pltpu.roll(line, (i * span + 1 - rows * j) % cols, 1)
                    pieces[j] = jnp.where((lane >= low) & (lane < high), value, pieces[j])
            where = slice(g * cols, (g + 1) * cols)
            for j in (0, per - 1):
                pieces[j] = pieces[j] + move(ends, ue_ref[0 if j == 0 else 1, :, where])
            for j in range(per):

                @pl.when(s_ref[SENDS + j] == 1)
                def _(j=j, piece=pieces[j]):
                    messages[j][:, where] = piece.astype(BF)

            @pl.when(s_ref[SENDS + per] == 1)
            def _(piece=pieces[0]):
                messages[per][:, where] = piece.astype(BF)

            @pl.when(s_ref[SENDS + per] == 2)
            def _(piece=pieces[per - 1]):
                messages[per][:, where] = piece.astype(BF)


def seams_kernel(s_ref, *refs, rounds, rows, bands):
    got, refs = refs[:rounds], refs[rounds:]
    first_msg, last_msg, cl_ref, up_ref, down_ref, top_ref, bot_ref, pick_ref, srow_ref, scol_ref = refs[:10]
    rows_ref, unit0_ref, unit7_ref, other_ref, corner_ref = refs[10:]
    faces, (chans, cols) = up_ref.shape[0] - 1, up_ref.shape[1:]
    per = rounds - 1
    span = rows + 2
    first_band = s_ref[BAND] == 0
    lane = lax.broadcasted_iota(jnp.int32, (chans, cols), 1)
    for r in range(rounds):

        @pl.when(s_ref[COL_ROUND] == r)
        def _(r=r):
            other_ref[...] = got[r][...]

    @pl.when((s_ref[COL_ROUND] == rounds) & first_band)
    def _():
        other_ref[...] = first_msg[...]

    @pl.when((s_ref[COL_ROUND] == rounds) & jnp.logical_not(first_band))
    def _():
        other_ref[...] = last_msg[...]

    scol_ref[...] = move(side_by_side(other_ref[...], cl_ref[...]), pick_ref[...]).astype(BF)

    on_row = jnp.logical_or(first_band, s_ref[BAND] == bands - 1)
    table = SENDS + rounds

    @pl.when(on_row)
    def _():
        for code, to, normal in ((FIRST_FROM, unit0_ref, got[0]), (LAST_FROM, unit7_ref, got[per - 1])):
            for value, src in enumerate((normal, got[per], cl_ref)):

                @pl.when(s_ref[code] == value)
                def _(to=to, src=src):
                    to[...] = src[...]

        for f in range(faces + 1):
            rows_ref[f] = pick2(first_band, up_ref[f], bot_ref[f])
            rows_ref[faces + 1 + f] = pick2(first_band, top_ref[f], down_ref[f])
        units = [unit0_ref, *got[1 : per - 1], unit7_ref]
        corner_ref[...] = jnp.zeros_like(corner_ref)
        for f in range(faces):
            side, face = s_ref[table + f], s_ref[table + faces + f]

            @pl.when(side < 2)
            def _(f=f, side=side, face=face):
                srow_ref[f] = rows_ref[side * (faces + 1) + face]
                ends = rows_ref[side * (faces + 1) + faces].astype(F32)
                ends = pltpu.roll(ends, lax.rem(2 * f + 2 * cols - 2 * face, cols), 1)
                corner_ref[...] = jnp.where((lane == 2 * f) | (lane == 2 * f + 1), ends, corner_ref[...])

            @pl.when(side >= 2)
            def _(f=f, side=side, face=face):
                group = pl.ds(pl.multiple_of(((side - 2) * 2 + face // 6) * cols, cols), cols)
                q = lax.rem(face, 6) * span
                line = jnp.zeros((chans, cols), F32)
                ends = corner_ref[...]
                for j in range(per):
                    value = units[j][:, group].astype(F32)
                    line = jnp.where(lane // rows == j, pltpu.roll(value, lax.rem(rows * j + 2 * cols - 1 - q, cols), 1), line)
                    if j == 0:
                        ends = jnp.where(lane == 2 * f, pltpu.roll(value, lax.rem(2 * f + 2 * cols - q, cols), 1), ends)
                    if j == per - 1:
                        shift = lax.rem(2 * f + 1 + 2 * cols - q - (span - 1), cols)
                        ends = jnp.where(lane == 2 * f + 1, pltpu.roll(value, shift, 1), ends)
                srow_ref[f] = line.astype(BF)
                corner_ref[...] = ends

        srow_ref[faces] = corner_ref[...].astype(BF)

    @pl.when(jnp.logical_not(on_row))
    def _():
        srow_ref[...] = jnp.zeros_like(srow_ref)


def halo_kernel(s_ref, srow_ref, rrow_ref, scol_ref, rcol_ref, top_ref, bot_ref, left_ref, right_ref, join_ref, joinend_ref, back_ref, widen_ref, ends_ref, t_out, b_out, l_out, r_out, *, bands, tiles, rounds):
    faces, (chans, cols) = top_ref.shape[0] - 1, top_ref.shape[1:]
    first_band, last_band = s_ref[BAND] == 0, s_ref[BAND] == bands - 1
    first_tile, last_tile = s_ref[TILE] == 0, s_ref[TILE] == tiles - 1
    table = SENDS + rounds + 2 * faces
    for cond, out, ref in ((first_band, t_out, top_ref), (last_band, b_out, bot_ref)):

        @pl.when(cond)
        def _(out=out):
            for f in range(faces):
                turned = move(rrow_ref[f], back_ref[...]).astype(BF)
                out[f] = pick2(s_ref[table + f] == 1, turned, srow_ref[f])

        @pl.when(jnp.logical_not(cond))
        def _(out=out, ref=ref):
            for f in range(faces):
                out[f] = ref[f]

    ends = move(side_by_side(srow_ref[faces], rrow_ref[faces]), joinend_ref[...]).astype(BF)
    top_end = pick2(first_band, ends, top_ref[faces])
    bot_end = pick2(last_band, ends, bot_ref[faces])
    none = jnp.zeros_like(top_end)
    seam = move(side_by_side(scol_ref[...], rcol_ref[...]), join_ref[...])
    for side, (at_edge, src, out) in enumerate(((first_tile, left_ref, l_out), (last_tile, right_ref, r_out))):
        use_top = jnp.logical_or(first_band, jnp.logical_not(at_edge))
        use_bot = jnp.logical_or(last_band, jnp.logical_not(at_edge))
        both = side_by_side(pick2(use_top, top_end, none), pick2(use_bot, bot_end, none))
        base = pick2(at_edge, seam, move(src[...], widen_ref[...]))
        out[...] = (base + move(both, ends_ref[side])).astype(BF)


def exchange(x, low, high, plan, tables):
    scalars, pick, join, join_end, (own, wrap, widen, ends, corner, unit_ends, back) = tables
    faces, rows, chans, cols = x.shape
    bands, tiles = plan.bands, plan.tiles
    rounds = len(plan.pairs)
    across = [(i, (i + 1) % tiles) for i in range(tiles)]
    left = lax.ppermute(high, "tile", across)
    right = lax.ppermute(low, "tile", [(j, i) for i, j in across])
    up, down = rows_call(x, left, right, corner)
    around = [(i, (i + 1) % bands) for i in range(bands)]
    top = lax.ppermute(down, "band", around)
    bottom = lax.ppermute(up, "band", [(j, i) for i, j in around])
    outs = whole(
        functools.partial(lines_kernel, bands=bands, rows=rows),
        [(chans, 4 * cols)] * (rounds + 1),
        [],
        scalars, up, down, top, bottom, low, high, left, right, own, wrap, unit_ends,
    )
    messages, col_lines = outs[:-1], outs[-1]
    got = [lax.ppermute(m, AXES, pairs) for m, pairs in zip(messages, plan.pairs)]
    line = (faces + 1, chans, cols)
    srow, scol = whole(
        functools.partial(seams_kernel, rounds=rounds, rows=rows, bands=bands),
        [line, (chans, 2 * cols)],
        [
            pltpu.VMEM((2 * (faces + 1), chans, cols), BF),
            pltpu.VMEM((chans, 4 * cols), BF),
            pltpu.VMEM((chans, 4 * cols), BF),
            pltpu.VMEM((chans, 4 * cols), BF),
            pltpu.VMEM((chans, cols), F32),
        ],
        scalars, *got, messages[0], messages[plan.per - 1], col_lines, up, down, top, bottom, pick,
    )
    rrow = lax.ppermute(srow, AXES, plan.flip_row)
    rcol = lax.ppermute(scol, AXES, plan.flip_col)
    rim = (faces, chans, cols)
    return whole(
        functools.partial(halo_kernel, bands=bands, tiles=tiles, rounds=rounds),
        [rim, rim, (chans, 2 * cols), (chans, 2 * cols)],
        [],
        scalars, srow, rrow, scol, rcol, top, bottom, left, right, join, join_end, back, widen, ends,
    )


def local(
    source,
    regrid_weights,
    dest_group,
    dest_block,
    seam_table,
    conv1_weight,
    conv1_bias,
    conv2_weight,
    conv2_bias,
):
    bands, tiles = lax.axis_size("band"), lax.axis_size("tile")
    devices = bands * tiles
    src_count, top_count, block_len = regrid_weights.shape[:3]
    capacity = 3 * src_count * top_count // devices
    rows = block_len * tiles // bands
    faces = seam_table.shape[0]
    slots_dev = faces * rows
    fields = source.shape[0]
    hid = conv1_weight.shape[1]
    items = src_count * top_count
    total = devices * capacity

    target = dest_group.reshape(items)
    order = jnp.arange(items)
    same = (target[:, None] == target[None, :]) & (order[None, :] < order[:, None])
    position = target * capacity + jnp.sum(same.astype(jnp.int32), axis=1)
    hit = position[:, None] == jnp.arange(total)[None, :]
    out_slots = slots_dev + jnp.sum(
        jnp.where(hit, (dest_block.reshape(items) - slots_dev)[:, None], 0), axis=0
    )
    slots = lax.all_to_all(out_slots.reshape(devices, capacity), AXES, split_axis=0, concat_axis=0, tiled=True)
    outgoing = regrid(source, regrid_weights, position, total)
    arrived = lax.all_to_all(
        outgoing.reshape(devices, capacity, fields, block_len), AXES, split_axis=0, concat_axis=0, tiled=True
    )
    regridded, low, high = place(arrived.reshape(total, fields, block_len), slots.reshape(total), slots_dev)
    regridded = regridded.reshape(faces, rows, fields, block_len)

    plan = Plan(bands, tiles)
    tables = seam_tables(seam_table, plan, rows, block_len)
    depth1 = -(-3 * fields // 128) * 128
    weight1 = wide_weight(conv1_weight, depth1)
    weight2 = wide_weight(conv2_weight, 3 * hid)
    bias1 = jnp.concatenate([conv1_bias, conv1_bias])[:, None]
    bias2 = jnp.concatenate([conv2_bias, conv2_bias])[:, None]
    halo = exchange(regridded, low, high, plan, tables)
    hidden, low, high = conv(regridded, *halo, weight1, bias1, False)
    halo = exchange(hidden, low, high, plan, tables)
    return conv(hidden, *halo, weight2, bias2, True)


def solution(mesh):
    return jax.shard_map(
        local,
        mesh=mesh,
        in_specs=(
            P(None, AXES),
            P(AXES, None, None, None),
            P(AXES, None),
            P(AXES, None),
            P(),
            P(),
            P(),
            P(),
            P(),
        ),
        out_specs=P(None, None, "band", "tile"),
        check_vma=False,
    )
```

profile of v0, /device:TPU:0, one launch (start us, length us, event | category | flops | bytes accessed | tf_op | source)
XLA Modules:
  0.0 350.0 jit_solution(1656057236522795795)
XLA Ops:
  2.9 11.1 %all-to-all-start = ((s32[128,1,6]{2,1,0:T(1,128)}), s32[128,1,6]{2,1,0:T(1,128)S(1)}, u32[]{:S(2)}, u32[]{:S(2)}) async-start(s32[128,1,6]{2,1,0:T(1,128)} %bitcast.14), calls=%async_computation | async-start | bytes 131072 | tf_op jit(solution)/shard_map/all_to_all | solution.py:645
  14.1 10.5 %shard_map.271 = bf16[768,40,128]{2,1,0:T(8,128)(2,1)} custom-call(s32[256]{0:T(256)} %copy-done.37, bf16[40,8192]{1,0:T(8,128)(2,1)} %src_ref.1, bf16[64,4,128,128]{3,2,1,0:T(8,128)(2,1)} %w_ref.1), custom_call_target="tpu_custom_call" | custom-call | flops 335544320 | bytes 17000000 | tf_op jit(solution)/shard_map/pallas_call | solution.py:32
  24.7 10.2 %all-to-all-start.1 = ((bf16[128,6,40,128]{3,2,1,0:T(8,128)(2,1)}), bf16[128,6,40,128]{3,2,1,0:T(8,128)(2,1)}, u32[]{:S(2)}, u32[]{:S(2)}) async-start(bf16[128,6,40,128]{3,2,1,0:T(8,128)(2,1)} %bitcast.50), calls=%async_computation.1 | async-start | bytes 15728640 | tf_op jit(solution)/shard_map/all_to_all | solution.py:647
  39.4 89.8 %all-to-all-done.1 = bf16[128,6,40,128]{3,2,1,0:T(8,128)(2,1)} async-done(((bf16[128,6,40,128]{3,2,1,0:T(8,128)(2,1)}), bf16[128,6,40,128]{3,2,1,0:T(8,128)(2,1)}, u32[]{:S(2)}, u32[]{:S(2)}) %all-to-all-start.1) | async-done | bytes 7864352 | tf_op jit(solution)/shard_map/all_to_all | solution.py:647
  129.2 11.3 %shard_map.272 = (bf16[192,40,128]{2,1,0:T(8,128)(2,1)}, bf16[40,256]{1,0:T(8,128)(2,1)}, bf16[40,256]{1,0:T(8,128)(2,1)}) custom-call(s32[768]{0:T(1024)} %reshape.110.slot_ref, bf16[768,40,128]{2,1,0:T(8,128)(2,1)} %bitcast.16.in_ref), custom_call_target="tpu_custom_call" | custom-call | tf_op jit(solution)/shard_map/pallas_call | solution.py:90
  140.5 3.2 collective-permute-start.1
  146.3 2.0 shard_map.273
  148.2 5.1 %collective-permute-start.3 = (bf16[13,40,128]{2,1,0:T(8,128)(2,1)}, bf16[13,40,128]{2,1,0:T(8,128)(2,1)S(1)}, u32[]{:S(2)}, u32[]{:S(2)}) collective-permute-start(bf16[13,40,128]{2,1,0:T(8,128)(2,1)} %get-tuple-element.50.up_ref.refs_12_), channel_id=1, source_target_pairs={{4,0},{8,4},{12,8},{16,12},{20,16},{24,20},{28,24},{32,28},{36,32}... | collective-permute-start | bytes 399368 | tf_op jit(solution)/shard_map/ppermute | solution.py:581
  153.3 2.9 collective-permute-done.2.top_ref.refs_14_
  157.5 3.8 %shard_map.274 = (bf16[40,512]{1,0:T(8,128)(2,1)}, bf16[40,512]{1,0:T(8,128)(2,1)}, bf16[40,512]{1,0:T(8,128)(2,1)}, bf16[40,512]{1,0:T(8,128)(2,1)}, bf16[40,51...) custom-call(s32[54]{0:T(128)} %concatenate.17.s_ref, ...), custom_call_target="tpu_custom_call" | custom-call | tf_op jit(solution)/shard_map/pallas_call | solution.py:351
  163.1 1.9 collective-permute-start.11
  167.1 1.9 collective-permute-start.5
  169.0 1.9 collective-permute-start.6
  171.0 1.9 collective-permute-start.7
  176.9 3.6 %collective-permute-done.8.refs_4_ = bf16[40,512]{1,0:T(8,128)(2,1)S(1)} collective-permute-done((bf16[40,512]{1,0:T(8,128)(2,1)}, bf16[40,512]{1,0:T(8,128)(2,1)S(1)}, u32[]{:S(2)}, u32[]{:S(2)}) %collective-permute-start.8) | collective-permute-done | bytes 40992 | tf_op jit(solution)/shard_map/ppermute | solution.py:589
  182.5 3.6 %shard_map.275 = (bf16[13,40,128]{2,1,0:T(8,128)(2,1)}, bf16[40,256]{1,0:T(8,128)(2,1)}) custom-call(s32[54]{0:T(128)} %concatenate.17.s_ref, bf16[40,512]{1,0:T(8,128)(2,1)} %copy-done.28, bf16[40,512]{1,0:T(8,128)(2,1)} %copy-done.29, bf16[40,512]{1,0:T(8,128)(2,1)} %copy-done.30, bf16[40,512]{1,0:T(8,128)(2,1)} %copy-done.31, bf16[40,512]{1,0:T(8,128)(2,1)} %copy-done.32, ...), custom_call_target="tpu_custom_call" | custom-call | tf_op jit(solution)/shard_map/pallas_call | solution.py:351
  186.1 19.0 %collective-permute-start.13 = (bf16[13,40,128]{2,1,0:T(8,128)(2,1)}, bf16[13,40,128]{2,1,0:T(8,128)(2,1)S(1)}, u32[]{:S(2)}, u32[]{:S(2)}) collective-permute-start(bf16[13,40,128]{2,1,0:T(8,128)(2,1)} %get-tuple-element.62.srow_ref), channel_id=1, source_target_pairs={{0,3},{1,2},{2,1},{3,0},{124,127},{125,126},{126,125},{127,124}} | collective-permute-start | bytes 399368 | tf_op jit(solution)/shard_map/ppermute | solution.py:603
  208.9 4.9 %collective-permute-done.14.rcol_ref = bf16[40,256]{1,0:T(8,128)(2,1)S(1)} collective-permute-done((bf16[40,256]{1,0:T(8,128)(2,1)}, bf16[40,256]{1,0:T(8,128)(2,1)S(1)}, u32[]{:S(2)}, u32[]{:S(2)}) %collective-permute-start.14) | collective-permute-done | bytes 20512 | tf_op jit(solution)/shard_map/ppermute | solution.py:604
  215.1 2.8 shard_map.276
  217.8 13.7 %shard_map.277 = (bf16[12,16,128,128]{3,2,1,0:T(8,128)(2,1)}, bf16[128,256]{1,0:T(8,128)(2,1)}, bf16[128,256]{1,0:T(8,128)(2,1)}) custom-call(bf16[256,512]{1,0:T(8,128)(2,1)} %bitcast.57, f32[256,1]{1,0:T(8,128)} %copy.53.b_ref, bf16[12,16,40,128]{3,2,1,0:T(8,128)(2,1)} %bitcast.53, bf16[12,40,128]{2,1,0:T(8,128)(2,1)} %get-tuple-element.64.top_ref, ...), custom_call_target="tpu_custom_call" | custom-call | tf_op jit(solution)/shard_map/pallas_call | solution.py:194
  231.7 3.2 collective-permute-start.16
  234.9 2.4 collective-permute-done.15.left_ref
  238.0 2.4 shard_map.278
  240.3 5.1 %collective-permute-start.18 = (bf16[13,128,128]{2,1,0:T(8,128)(2,1)}, bf16[13,128,128]{2,1,0:T(8,128)(2,1)S(1)}, u32[]{:S(2)}, u32[]{:S(2)}) collective-permute-start(bf16[13,128,128]{2,1,0:T(8,128)(2,1)} %get-tuple-element.71.up_ref.refs_12_), channel_id=1, source_target_pairs={{4,0},{8,4},{12,8},{16,12},{20,16},{24,20},{28,24},{32,28},{36,32}... | collective-permute-start | bytes 1277960 | tf_op jit(solution)/shard_map/ppermute | solution.py:581
  245.4 6.0 %collective-permute-done.17.top_ref.refs_14_ = bf16[13,128,128]{2,1,0:T(8,128)(2,1)S(1)} collective-permute-done((bf16[13,128,128]{2,1,0:T(8,128)(2,1)}, bf16[13,128,128]{2,1,0:T(8,128)(2,1)S(1)}, u32[]{:S(2)}, u32[]{:S(2)}) %collective-permute-start.17) | collective-permute-done | bytes 426016 | tf_op jit(solution)/shard_map/ppermute | solution.py:580
  253.1 5.7 %shard_map.279 = (bf16[128,512]{1,0:T(8,128)(2,1)}, bf16[128,512]{1,0:T(8,128)(2,1)}, bf16[128,512]{1,0:T(8,128)(2,1)}, bf16[128,512]{1,0:T(8,128)(2,1)}, bf16[1...) custom-call(s32[54]{0:T(128)} %concatenate.17.s_ref, ...), custom_call_target="tpu_custom_call" | custom-call | tf_op jit(solution)/shard_map/pallas_call | solution.py:351
  275.2 2.2 collective-permute-done.25.refs_6_
  279.5 4.9 %shard_map.280 = (bf16[13,128,128]{2,1,0:T(8,128)(2,1)}, bf16[128,256]{1,0:T(8,128)(2,1)}) custom-call(s32[54]{0:T(128)} %concatenate.17.s_ref, bf16[128,512]{1,0:T(8,128)(2,1)} %copy-done.12, bf16[128,512]{1,0:T(8,128)(2,1)} %copy-done.13, bf16[128,512]{1,0:T(8,128)(2,1)} %copy-done.14, bf16[128,512]{1,0:T(8,128)(2,1)} %copy-done.15, ...), custom_call_target="tpu_custom_call" | custom-call | tf_op jit(solution)/shard_map/pallas_call | solution.py:351
  284.4 21.8 %collective-permute-start.28 = (bf16[13,128,128]{2,1,0:T(8,128)(2,1)}, bf16[13,128,128]{2,1,0:T(8,128)(2,1)S(1)}, u32[]{:S(2)}, u32[]{:S(2)}) collective-permute-start(bf16[13,128,128]{2,1,0:T(8,128)(2,1)} %get-tuple-element.83.srow_ref), channel_id=1, source_target_pairs={{0,3},{1,2},{2,1},{3,0},{124,127},{125,126},{126,125},{127,124}} | collective-permute-start | bytes 1277960 | tf_op jit(solution)/shard_map/ppermute | solution.py:603
  311.1 6.4 %collective-permute-done.29.rcol_ref = bf16[128,256]{1,0:T(8,128)(2,1)S(1)} collective-permute-done((bf16[128,256]{1,0:T(8,128)(2,1)}, bf16[128,256]{1,0:T(8,128)(2,1)S(1)}, u32[]{:S(2)}, u32[]{:S(2)}) %collective-permute-start.29) | collective-permute-done | bytes 65568 | tf_op jit(solution)/shard_map/ppermute | solution.py:604
  318.8 3.2 shard_map.281
  322.0 28.0 %shard_map.282 = bf16[128,12,16,128]{3,2,1,0:T(8,128)(2,1)} custom-call(bf16[256,1536]{1,0:T(8,128)(2,1)} %bitcast.54, f32[256,1]{1,0:T(8,128)} %copy.54.b_ref, bf16[12,16,128,128]{3,2,1,0:T(8,128)(2,1)} %get-tuple-element.68.first_ref.last_ref.x_ref, bf16[12,128,128]{2,1,0:T(8,128)(2,1)} %get-tuple-element.85.top_ref, ...), custom_call_target="tpu_custom_call" | custom-call | tf_op jit(solution)/shard_map/pallas_call | solution.py:194
  (187 shorter events, 52.6 us)
Async XLA Ops:
  2.9 21.7 %all-to-all-start = ((s32[128,1,6]{2,1,0:T(1,128)}), s32[128,1,6]{2,1,0:T(1,128)S(1)}, u32[]{:S(2)}, u32[]{:S(2)}) async-start(s32[128,1,6]{2,1,0:T(1,128)} %bitcast.14), calls=%async_computation | async-start | bytes 131072 | tf_op jit(solution)/shard_map/all_to_all | solution.py:645
  24.7 104.4 %all-to-all-start.1 = ((bf16[128,6,40,128]{3,2,1,0:T(8,128)(2,1)}), bf16[128,6,40,128]{3,2,1,0:T(8,128)(2,1)}, u32[]{:S(2)}, u32[]{:S(2)}) async-start(bf16[128,6,40,128]{3,2,1,0:T(8,128)(2,1)} %bitcast.50), calls=%async_computation.1 | async-start | bytes 15728640 | tf_op jit(solution)/shard_map/all_to_all | solution.py:647
  140.4 5.2 %collective-permute-start = (bf16[40,256]{1,0:T(8,128)(2,1)}, bf16[40,256]{1,0:T(8,128)(2,1)S(1)}, u32[]{:S(2)}, u32[]{:S(2)}) collective-permute-start(bf16[40,256]{1,0:T(8,128)(2,1)} %get-tuple-element.48.high_ref), channel_id=1, source_target_pairs={{0,1},{1,2},{2,3},{3,0},{4,5},{5,6},{6,7},{7,4},{8,9},{9,10},{10,1... | collective-permute-start | bytes 61448 | tf_op jit(solution)/shard_map/ppermute | solution.py:576
  140.5 5.2 %collective-permute-start.1 = (bf16[40,256]{1,0:T(8,128)(2,1)}, bf16[40,256]{1,0:T(8,128)(2,1)S(1)}, u32[]{:S(2)}, u32[]{:S(2)}) collective-permute-start(bf16[40,256]{1,0:T(8,128)(2,1)} %get-tuple-element.49.low_ref), channel_id=1, source_target_pairs={{1,0},{2,1},{3,2},{0,3},{5,4},{6,5},{7,6},{4,7},{9,8},{10,9},{11,1... | collective-permute-start | bytes 61448 | tf_op jit(solution)/shard_map/ppermute | solution.py:577
  148.2 7.9 %collective-permute-start.2 = (bf16[13,40,128]{2,1,0:T(8,128)(2,1)}, bf16[13,40,128]{2,1,0:T(8,128)(2,1)S(1)}, u32[]{:S(2)}, u32[]{:S(2)}) collective-permute-start(bf16[13,40,128]{2,1,0:T(8,128)(2,1)} %get-tuple-element.51.down_ref.refs_13_), channel_id=1, source_target_pairs={{0,4},{4,8},{8,12},{12,16},{16,20},{20,24},{24,28},{28,32},{32,36}... | collective-permute-start | bytes 399368 | tf_op jit(solution)/shard_map/ppermute | solution.py:580
  148.2 7.9 %collective-permute-start.3 = (bf16[13,40,128]{2,1,0:T(8,128)(2,1)}, bf16[13,40,128]{2,1,0:T(8,128)(2,1)S(1)}, u32[]{:S(2)}, u32[]{:S(2)}) collective-permute-start(bf16[13,40,128]{2,1,0:T(8,128)(2,1)} %get-tuple-element.50.up_ref.refs_12_), channel_id=1, source_target_pairs={{4,0},{8,4},{12,8},{16,12},{20,16},{24,20},{28,24},{32,28},{36,32}... | collective-permute-start | bytes 399368 | tf_op jit(solution)/shard_map/ppermute | solution.py:581
  161.2 7.8 %collective-permute-start.10 = (bf16[40,512]{1,0:T(8,128)(2,1)}, bf16[40,512]{1,0:T(8,128)(2,1)S(1)}, u32[]{:S(2)}, u32[]{:S(2)}) collective-permute-start(bf16[40,512]{1,0:T(8,128)(2,1)} %get-tuple-element.58), channel_id=1, source_target_pairs={{0,24},{24,0},{124,27},{27,124},{1,56},{56,1},{125,59},{59,125},{2... | collective-permute-start | bytes 122888 | tf_op jit(solution)/shard_map/ppermute | solution.py:589
  163.1 7.8 %collective-permute-start.11 = (bf16[40,512]{1,0:T(8,128)(2,1)}, bf16[40,512]{1,0:T(8,128)(2,1)S(1)}, u32[]{:S(2)}, u32[]{:S(2)}) collective-permute-start(bf16[40,512]{1,0:T(8,128)(2,1)} %get-tuple-element.59.refs_10_), channel_id=1, source_target_pairs={{0,28},{28,0},{1,60},{60,1},{125,63},{63,125},{2,92},{92,2},{126,9... | collective-permute-start | bytes 122888 | tf_op jit(solution)/shard_map/ppermute | solution.py:589
  165.1 7.8 %collective-permute-start.12 = (bf16[40,512]{1,0:T(8,128)(2,1)}, bf16[40,512]{1,0:T(8,128)(2,1)S(1)}, u32[]{:S(2)}, u32[]{:S(2)}) collective-permute-start(bf16[40,512]{1,0:T(8,128)(2,1)} %get-tuple-element.60), channel_id=1, source_target_pairs={{3,96},{96,3},{124,31},{31,124}} | collective-permute-start | bytes 122888 | tf_op jit(solution)/shard_map/ppermute | solution.py:589
  165.7 9.1 %collective-permute-start.4 = (bf16[40,512]{1,0:T(8,128)(2,1)}, bf16[40,512]{1,0:T(8,128)(2,1)S(1)}, u32[]{:S(2)}, u32[]{:S(2)}) collective-permute-start(bf16[40,512]{1,0:T(8,128)(2,1)} %get-tuple-element.52.refs_9_), channel_id=1, source_target_pairs={{124,3},{3,124},{1,32},{32,1},{125,35},{35,125},{2,64},{64,2},{126... | collective-permute-start | bytes 122888 | tf_op jit(solution)/shard_map/ppermute | solution.py:589
  167.1 9.8 %collective-permute-start.5 = (bf16[40,512]{1,0:T(8,128)(2,1)}, bf16[40,512]{1,0:T(8,128)(2,1)S(1)}, u32[]{:S(2)}, u32[]{:S(2)}) collective-permute-start(bf16[40,512]{1,0:T(8,128)(2,1)} %get-tuple-element.53), channel_id=1, source_target_pairs={{0,4},{4,0},{124,7},{7,124},{1,36},{36,1},{125,39},{39,125},{2,68}... | collective-permute-start | bytes 122888 | tf_op jit(solution)/shard_map/ppermute | solution.py:589
  169.0 7.8 %collective-permute-start.6 = (bf16[40,512]{1,0:T(8,128)(2,1)}, bf16[40,512]{1,0:T(8,128)(2,1)S(1)}, u32[]{:S(2)}, u32[]{:S(2)}) collective-permute-start(bf16[40,512]{1,0:T(8,128)(2,1)} %get-tuple-element.54), channel_id=1, source_target_pairs={{0,8},{8,0},{124,11},{11,124},{1,40},{40,1},{125,43},{43,125},{2,7... | collective-permute-start | bytes 122888 | tf_op jit(solution)/shard_map/ppermute | solution.py:589
  171.0 5.9 %collective-permute-start.7 = (bf16[40,512]{1,0:T(8,128)(2,1)}, bf16[40,512]{1,0:T(8,128)(2,1)S(1)}, u32[]{:S(2)}, u32[]{:S(2)}) collective-permute-start(bf16[40,512]{1,0:T(8,128)(2,1)} %get-tuple-element.55), channel_id=1, source_target_pairs={{0,12},{12,0},{124,15},{15,124},{1,44},{44,1},{125,47},{47,125},{2... | collective-permute-start | bytes 122888 | tf_op jit(solution)/shard_map/ppermute | solution.py:589
  172.9 7.6 %collective-permute-start.8 = (bf16[40,512]{1,0:T(8,128)(2,1)}, bf16[40,512]{1,0:T(8,128)(2,1)S(1)}, u32[]{:S(2)}, u32[]{:S(2)}) collective-permute-start(bf16[40,512]{1,0:T(8,128)(2,1)} %get-tuple-element.56), channel_id=1, source_target_pairs={{0,16},{16,0},{124,19},{19,124},{1,48},{48,1},{125,51},{51,125},{2... | collective-permute-start | bytes 122888 | tf_op jit(solution)/shard_map/ppermute | solution.py:589
  174.9 7.0 %collective-permute-start.9 = (bf16[40,512]{1,0:T(8,128)(2,1)}, bf16[40,512]{1,0:T(8,128)(2,1)S(1)}, u32[]{:S(2)}, u32[]{:S(2)}) collective-permute-start(bf16[40,512]{1,0:T(8,128)(2,1)} %get-tuple-element.57), channel_id=1, source_target_pairs={{0,20},{20,0},{124,23},{23,124},{1,52},{52,1},{125,55},{55,125},{2... | collective-permute-start | bytes 122888 | tf_op jit(solution)/shard_map/ppermute | solution.py:589
  186.1 27.7 %collective-permute-start.13 = (bf16[13,40,128]{2,1,0:T(8,128)(2,1)}, bf16[13,40,128]{2,1,0:T(8,128)(2,1)S(1)}, u32[]{:S(2)}, u32[]{:S(2)}) collective-permute-start(bf16[13,40,128]{2,1,0:T(8,128)(2,1)} %get-tuple-element.62.srow_ref), channel_id=1, source_target_pairs={{0,3},{1,2},{2,1},{3,0},{124,127},{125,126},{126,125},{127,124}} | collective-permute-start | bytes 399368 | tf_op jit(solution)/shard_map/ppermute | solution.py:603
  205.2 8.6 %collective-permute-start.14 = (bf16[40,256]{1,0:T(8,128)(2,1)}, bf16[40,256]{1,0:T(8,128)(2,1)S(1)}, u32[]{:S(2)}, u32[]{:S(2)}) collective-permute-start(bf16[40,256]{1,0:T(8,128)(2,1)} %get-tuple-element.63.scol_ref), channel_id=1, source_target_pairs={{0,124},{3,127},{4,120},{7,123},{8,116},{11,119},{12,112},{15,115}... | collective-permute-start | bytes 61448 | tf_op jit(solution)/shard_map/ppermute | solution.py:604
  231.6 5.7 %collective-permute-start.15 = (bf16[128,256]{1,0:T(8,128)(2,1)}, bf16[128,256]{1,0:T(8,128)(2,1)S(1)}, u32[]{:S(2)}, u32[]{:S(2)}) collective-permute-start(bf16[128,256]{1,0:T(8,128)(2,1)} %get-tuple-element.69.high_ref), channel_id=1, source_target_pairs={{0,1},{1,2},{2,3},{3,0},{4,5},{5,6},{6,7},{7,4},{8,9},{9,10},{10,1... | collective-permute-start | bytes 196616 | tf_op jit(solution)/shard_map/ppermute | solution.py:576
  231.7 5.7 %collective-permute-start.16 = (bf16[128,256]{1,0:T(8,128)(2,1)}, bf16[128,256]{1,0:T(8,128)(2,1)S(1)}, u32[]{:S(2)}, u32[]{:S(2)}) collective-permute-start(bf16[128,256]{1,0:T(8,128)(2,1)} %get-tuple-element.70.low_ref), channel_id=1, source_target_pairs={{1,0},{2,1},{3,2},{0,3},{5,4},{6,5},{7,6},{4,7},{9,8},{10,9},{11,1... | collective-permute-start | bytes 196616 | tf_op jit(solution)/shard_map/ppermute | solution.py:577
  240.3 11.1 %collective-permute-start.17 = (bf16[13,128,128]{2,1,0:T(8,128)(2,1)}, bf16[13,128,128]{2,1,0:T(8,128)(2,1)S(1)}, u32[]{:S(2)}, u32[]{:S(2)}) collective-permute-start(bf16[13,128,128]{2,1,0:T(8,128)(2,1)} %get-tuple-element.72.down_ref.refs_13_), channel_id=1, source_target_pairs={{0,4},{4,8},{8,12},{12,16},{16,20},{20,24},{24,28},{28,32},{32,36}... | collective-permute-start | bytes 1277960 | tf_op jit(solution)/shard_map/ppermute | solution.py:580
  240.3 11.1 %collective-permute-start.18 = (bf16[13,128,128]{2,1,0:T(8,128)(2,1)}, bf16[13,128,128]{2,1,0:T(8,128)(2,1)S(1)}, u32[]{:S(2)}, u32[]{:S(2)}) collective-permute-start(bf16[13,128,128]{2,1,0:T(8,128)(2,1)} %get-tuple-element.71.up_ref.refs_12_), channel_id=1, source_target_pairs={{4,0},{8,4},{12,8},{16,12},{20,16},{24,20},{28,24},{32,28},{36,32}... | collective-permute-start | bytes 1277960 | tf_op jit(solution)/shard_map/ppermute | solution.py:581
  258.8 8.4 %collective-permute-start.19 = (bf16[128,512]{1,0:T(8,128)(2,1)}, bf16[128,512]{1,0:T(8,128)(2,1)S(1)}, u32[]{:S(2)}, u32[]{:S(2)}) collective-permute-start(bf16[128,512]{1,0:T(8,128)(2,1)} %get-tuple-element.73.refs_9_), channel_id=1, source_target_pairs={{124,3},{3,124},{1,32},{32,1},{125,35},{35,125},{2,64},{64,2},{126... | collective-permute-start | bytes 393224 | tf_op jit(solution)/shard_map/ppermute | solution.py:589
  259.4 9.7 %collective-permute-start.20 = (bf16[128,512]{1,0:T(8,128)(2,1)}, bf16[128,512]{1,0:T(8,128)(2,1)S(1)}, u32[]{:S(2)}, u32[]{:S(2)}) collective-permute-start(bf16[128,512]{1,0:T(8,128)(2,1)} %get-tuple-element.74), channel_id=1, source_target_pairs={{0,4},{4,0},{124,7},{7,124},{1,36},{36,1},{125,39},{39,125},{2,68}... | collective-permute-start | bytes 393224 | tf_op jit(solution)/shard_map/ppermute | solution.py:589
  261.4 9.7 %collective-permute-start.21 = (bf16[128,512]{1,0:T(8,128)(2,1)}, bf16[128,512]{1,0:T(8,128)(2,1)S(1)}, u32[]{:S(2)}, u32[]{:S(2)}) collective-permute-start(bf16[128,512]{1,0:T(8,128)(2,1)} %get-tuple-element.75), channel_id=1, source_target_pairs={{0,8},{8,0},{124,11},{11,124},{1,40},{40,1},{125,43},{43,125},{2,7... | collective-permute-start | bytes 393224 | tf_op jit(solution)/shard_map/ppermute | solution.py:589
  263.3 9.7 %collective-permute-start.22 = (bf16[128,512]{1,0:T(8,128)(2,1)}, bf16[128,512]{1,0:T(8,128)(2,1)S(1)}, u32[]{:S(2)}, u32[]{:S(2)}) collective-permute-start(bf16[128,512]{1,0:T(8,128)(2,1)} %get-tuple-element.76), channel_id=1, source_target_pairs={{0,12},{12,0},{124,15},{15,124},{1,44},{44,1},{125,47},{47,125},{2... | collective-permute-start | bytes 393224 | tf_op jit(solution)/shard_map/ppermute | solution.py:589
  265.2 8.6 %collective-permute-start.23 = (bf16[128,512]{1,0:T(8,128)(2,1)}, bf16[128,512]{1,0:T(8,128)(2,1)S(1)}, u32[]{:S(2)}, u32[]{:S(2)}) collective-permute-start(bf16[128,512]{1,0:T(8,128)(2,1)} %get-tuple-element.77), channel_id=1, source_target_pairs={{0,16},{16,0},{124,19},{19,124},{1,48},{48,1},{125,51},{51,125},{2... | collective-permute-start | bytes 393224 | tf_op jit(solution)/shard_map/ppermute | solution.py:589
  267.2 8.0 %collective-permute-start.24 = (bf16[128,512]{1,0:T(8,128)(2,1)}, bf16[128,512]{1,0:T(8,128)(2,1)S(1)}, u32[]{:S(2)}, u32[]{:S(2)}) collective-permute-start(bf16[128,512]{1,0:T(8,128)(2,1)} %get-tuple-element.78), channel_id=1, source_target_pairs={{0,20},{20,0},{124,23},{23,124},{1,52},{52,1},{125,55},{55,125},{2... | collective-permute-start | bytes 393224 | tf_op jit(solution)/shard_map/ppermute | solution.py:589
  269.1 8.3 %collective-permute-start.25 = (bf16[128,512]{1,0:T(8,128)(2,1)}, bf16[128,512]{1,0:T(8,128)(2,1)S(1)}, u32[]{:S(2)}, u32[]{:S(2)}) collective-permute-start(bf16[128,512]{1,0:T(8,128)(2,1)} %get-tuple-element.79), channel_id=1, source_target_pairs={{0,24},{24,0},{124,27},{27,124},{1,56},{56,1},{125,59},{59,125},{2... | collective-permute-start | bytes 393224 | tf_op jit(solution)/shard_map/ppermute | solution.py:589
  271.1 7.7 %collective-permute-start.26 = (bf16[128,512]{1,0:T(8,128)(2,1)}, bf16[128,512]{1,0:T(8,128)(2,1)S(1)}, u32[]{:S(2)}, u32[]{:S(2)}) collective-permute-start(bf16[128,512]{1,0:T(8,128)(2,1)} %get-tuple-element.80.refs_10_), channel_id=1, source_target_pairs={{0,28},{28,0},{1,60},{60,1},{125,63},{63,125},{2,92},{92,2},{126,9... | collective-permute-start | bytes 393224 | tf_op jit(solution)/shard_map/ppermute | solution.py:589
  273.0 5.8 %collective-permute-start.27 = (bf16[128,512]{1,0:T(8,128)(2,1)}, bf16[128,512]{1,0:T(8,128)(2,1)S(1)}, u32[]{:S(2)}, u32[]{:S(2)}) collective-permute-start(bf16[128,512]{1,0:T(8,128)(2,1)} %get-tuple-element.81), channel_id=1, source_target_pairs={{3,96},{96,3},{124,31},{31,124}} | collective-permute-start | bytes 393224 | tf_op jit(solution)/shard_map/ppermute | solution.py:589
  284.4 33.0 %collective-permute-start.28 = (bf16[13,128,128]{2,1,0:T(8,128)(2,1)}, bf16[13,128,128]{2,1,0:T(8,128)(2,1)S(1)}, u32[]{:S(2)}, u32[]{:S(2)}) collective-permute-start(bf16[13,128,128]{2,1,0:T(8,128)(2,1)} %get-tuple-element.83.srow_ref), channel_id=1, source_target_pairs={{0,3},{1,2},{2,1},{3,0},{124,127},{125,126},{126,125},{127,124}} | collective-permute-start | bytes 1277960 | tf_op jit(solution)/shard_map/ppermute | solution.py:603
  308.3 9.1 %collective-permute-start.29 = (bf16[128,256]{1,0:T(8,128)(2,1)}, bf16[128,256]{1,0:T(8,128)(2,1)S(1)}, u32[]{:S(2)}, u32[]{:S(2)}) collective-permute-start(bf16[128,256]{1,0:T(8,128)(2,1)} %get-tuple-element.84.scol_ref), channel_id=1, source_target_pairs={{0,124},{3,127},{4,120},{7,123},{8,116},{11,119},{12,112},{15,115}... | collective-permute-start | bytes 196616 | tf_op jit(solution)/shard_map/ppermute | solution.py:604
  (48 other events, 828.2 us)
where the time goes:
time: 351 us; the launch traced here: 350 us
  waiting for transfers between devices  123 us (35%)
  starting transfers between devices  112 us (32%)
  Pallas kernels  91.9 us (26%)
  local copies, waits for them, and re-layouts  17.1 us (5%)
  other arithmetic  4.74 us (1%)
    all_to_all x1, waiting for transfers between devices, local(): lax.all_to_all(outgoing.reshape(devices, capacity, fields, block_len), AX...  89.8 us
    pallas_call x2, Pallas kernels, conv(): pl.pallas_call(functools.partial(conv_kernel, last=last), grid=(face_coun...  41.8 us
    ppermute x2, starting transfers between devices, exchange(): rrow = lax.ppermute(srow, AXES, plan.flip_row)  40.8 us
    ppermute x18, starting transfers between devices, exchange(): lax.ppermute(m, AXES, pairs)  29.5 us
    pallas_call x6, Pallas kernels, whole(): pl.pallas_call(kernel, in_specs=[pl.BlockSpec(memory_space=pltpu.SMEM)] +...  24 us
    ppermute x2, waiting for transfers between devices, exchange(): rcol = lax.ppermute(scol, AXES, plan.flip_col)  11.3 us
    pallas_call x1, Pallas kernels, place(): pl.pallas_call(functools.partial(place_kernel, chunk=chunk), grid_spec=pl...  11.3 us
    all_to_all x1, starting transfers between devices, local(): lax.all_to_all(out_slots.reshape(devices, capacity), AXES, split_axis=0,...  11.1 us
  transfers between devices with their start and end apart: 32, of which 13 were waited for; matrix products, arithmetic and copies ran while one was open for 3% of the time, Pallas kernels for 3%

commit v1 on v0

--- a/solution.py
+++ b/solution.py
@@ -114,6 +114,8 @@
 
 
 def conv_kernel(w_ref, b_ref, x_ref, top_ref, bot_ref, l_ref, r_ref, *refs, last):
+    if not last:
+        edge_ref, refs = refs[0], refs[1:]
     if last:
         o_ref, p_ref, s_ref = refs
     else:
@@ -121,18 +123,20 @@
     faces, rows, chans, cols = x_ref.shape
     depth = p_ref.shape[1]
     hid = b_ref.shape[0] // 2
+    pitch = hid + 8
     step = pl.program_id(0)
     lane = lax.broadcasted_iota(jnp.int32, (chans, cols), 1)
     spare = depth - 3 * chans
     span = rows + 2
     group = pl.ds(pl.multiple_of((step // 3) * cols, cols), cols)
     back = lax.rem(cols - lax.rem(step, 3) * (faces * span), cols)
-    left = pltpu.roll(l_ref[:, group].astype(F32), back, 1)
-    right = pltpu.roll(r_ref[:, group].astype(F32), back, 1)
+    kind = F32 if chans % 16 else BF
+    left = pltpu.roll(l_ref[:, group].astype(F32), back, 1).astype(kind)
+    right = pltpu.roll(r_ref[:, group].astype(F32), back, 1).astype(kind)
     for f in range(faces):
         for r in range(span):
             row = top_ref[f] if r == 0 else bot_ref[f] if r == rows + 1 else x_ref[f, r - 1]
-            mid = row.astype(F32)
+            mid = row.astype(kind)
             at = f * span + r
             lo = jnp.where(lane == 0, left[:, at : at + 1], pltpu.roll(mid, 1, 1))
             hi = jnp.where(lane == cols - 1, right[:, at : at + 1], pltpu.roll(mid, cols - 1, 1))
@@ -141,30 +145,32 @@
                 parts.append(jnp.zeros((spare, cols), F32))
             p_ref[r, :, f * cols : (f + 1) * cols] = jnp.concatenate(parts, axis=0).astype(BF)
     bias = b_ref[...]
-    out_lane = lax.broadcasted_iota(jnp.int32, (hid, cols), 1)
-    low = high = jnp.zeros((hid, cols), F32)
+    edges = jnp.zeros((2 * hid, 2 * cols), F32)
     for rp in range(rows // 2):
         patch = p_ref[2 * rp : 2 * rp + 4].reshape(4 * depth, faces * cols)
         acc = jnp.dot(w_ref[...], patch, preferred_element_type=F32) + bias
         acc = gelu(acc)
+        if not last:
+            acc = acc.astype(BF)
+            edges += jnp.dot(acc, edge_ref[rp], preferred_element_type=F32)
         for d in range(2):
             for f in range(faces):
                 piece = acc[d * hid : (d + 1) * hid, f * cols : (f + 1) * cols]
                 if last:
-                    s_ref[f, (2 * rp + d) * hid : (2 * rp + d + 1) * hid, :] = piece
+                    s_ref[f, (2 * rp + d) * pitch : (2 * rp + d) * pitch + hid, :] = piece
                 else:
-                    o_ref[f, 2 * rp + d] = piece.astype(BF)
-                    low, high = edge_columns(piece, out_lane, f * rows + 2 * rp + d, low, high)
+                    o_ref[f, 2 * rp + d] = piece
     if last:
         for f in range(faces):
             for o in range(hid):
-                o_ref[o, f] = s_ref[f, pl.ds(o, rows, stride=hid), :].astype(BF)
+                o_ref[o, f] = s_ref[f, pl.ds(o, rows, stride=pitch), :].astype(BF)
     else:
         per = cols // (faces * rows)
         ahead = lax.rem(step, per) * (faces * rows)
         half = pl.ds(pl.multiple_of((step // per) * cols, cols), cols)
         fresh = lax.rem(step, per) == 0
-        for ref, value in ((low_ref, low), (high_ref, high)):
+        for i, ref in enumerate((low_ref, high_ref)):
+            value = edges[:hid, i * cols : (i + 1) * cols] + pltpu.roll(edges[hid:, i * cols : (i + 1) * cols], 1, 1)
             value = pltpu.roll(value, ahead, 1).astype(BF)
 
             @pl.when(fresh)
@@ -174,6 +180,15 @@
             @pl.when(jnp.logical_not(fresh))
             def _(ref=ref, value=value):
                 ref[:, half] += value
+
+
+def edge_maps(faces, rows, cols):
+    maps = np.zeros((rows // 2, faces * cols, 2 * cols), np.float32)
+    for rp in range(rows // 2):
+        for f in range(faces):
+            maps[rp, f * cols, f * rows + 2 * rp] = 1
+            maps[rp, f * cols + cols - 1, cols + f * rows + 2 * rp] = 1
+    return jnp.asarray(maps, BF)
 
 
 def conv(x, top, bottom, left, right, weight, bias, last):
@@ -185,7 +200,7 @@
     if last:
         out_shape = jax.ShapeDtypeStruct((hid, face_count, rows, cols), BF)
         out_spec = pl.BlockSpec((hid, faces, rows, cols), lambda i: (0, i, 0, 0))
-        scratch.append(pltpu.VMEM((faces, rows * hid, cols), F32))
+        scratch.append(pltpu.VMEM((faces, rows * (hid + 8), cols), F32))
     else:
         out_shape = [jax.ShapeDtypeStruct((face_count, rows, hid, cols), BF)]
         out_shape += [jax.ShapeDtypeStruct((hid, 2 * cols), BF)] * 2
@@ -202,12 +217,13 @@
             pl.BlockSpec((faces, chans, cols), lambda i: (i, 0, 0)),
             pl.BlockSpec(left.shape, lambda i: (0, 0)),
             pl.BlockSpec(right.shape, lambda i: (0, 0)),
-        ],
+        ]
+        + ([] if last else [pl.BlockSpec((rows // 2, faces * cols, 2 * cols), lambda i: (0, 0, 0))]),
         out_specs=out_spec,
         out_shape=out_shape,
         scratch_shapes=scratch,
         compiler_params=pltpu.CompilerParams(vmem_limit_bytes=VMEM_LIMIT),
-    )(weight, bias, x, top, bottom, left, right)
+    )(weight, bias, x, top, bottom, left, right, *([] if last else [edge_maps(faces, rows, cols)]))
 
 
 def wide_weight(weight, depth):
@@ -227,30 +243,28 @@
         rounds = per + 1
         count = bands * tiles
         self.pairs = [[] for _ in range(rounds)]
-        self.sends_row = np.zeros((rounds, count), np.int32)
-        self.unit = np.zeros((rounds, count), np.int32)
-        self.row_round = np.full((count, per), rounds, np.int32)
+        self.sends = np.zeros((rounds, count), np.int32)
+        self.row_from = np.full((count, per), 2, np.int32)
         self.col_round = np.full((count,), rounds, np.int32)
-
-        def join(r, row_dev, col_dev, j):
-            if row_dev == col_dev:
-                self.sends_row[r, row_dev] = 1
+        corners = (tiles - 1, last * tiles)
+        self.pairs[per] = [corners, corners[::-1]]
+
+        def join(row_dev, col_dev, j):
+            if row_dev in corners and col_dev in corners:
+                self.sends[per, row_dev] = 1 if j == 0 else 2
+                self.row_from[row_dev, j] = 1
+                self.col_round[col_dev] = per
                 return
-            self.pairs[r] += [(row_dev, col_dev), (col_dev, row_dev)]
-            self.sends_row[r, row_dev] = 1
-            self.unit[r, row_dev] = j
-            self.row_round[row_dev, j] = r
-            self.col_round[col_dev] = r
+            self.sends[j, row_dev] = 1
+            if row_dev != col_dev:
+                self.pairs[j] += [(row_dev, col_dev), (col_dev, row_dev)]
+                self.row_from[row_dev, j] = 0
+                self.col_round[col_dev] = j
 
         for j in range(per):
             for t in range(tiles):
-                join(per if (t, j) == (tiles - 1, 0) else j, t, (per * t + j) * tiles, j)
-                join(
-                    per if (t, j) == (0, per - 1) else j,
-                    last * tiles + t,
-                    (per * t + j) * tiles + tiles - 1,
-                    j,
-                )
+                join(t, (per * t + j) * tiles, j)
+                join(last * tiles + t, (per * t + j) * tiles + tiles - 1, j)
         for pairs in self.pairs:
             assert len({a for a, _ in pairs}) == len(pairs) == len({b for _, b in pairs})
         self.flip_row = [
@@ -302,9 +316,9 @@
     static = np.concatenate(
         [
             plan.col_round[:, None],
-            np.where(plan.row_round[:, :1] == 0, 0, np.where(plan.row_round[:, :1] == per, 1, 2)),
-            np.where(plan.row_round[:, -1:] == per - 1, 0, np.where(plan.row_round[:, -1:] == per, 1, 2)),
-            plan.sends_row.T + plan.sends_row.T * (plan.unit.T > 0) * (np.arange(rounds) == per),
+            plan.row_from[:, :1],
+            plan.row_from[:, -1:],
+            plan.sends.T,
         ],
         axis=1,
     ).astype(np.int32)
@@ -400,8 +414,8 @@
 
 
 def lines_kernel(s_ref, up_ref, down_ref, top_ref, bot_ref, low_ref, high_ref, left_ref, right_ref, own_ref, wrap_ref, ue_ref, *outs, bands, rows):
-    messages, cl_ref = outs[:-1], outs[-1]
-    per = len(messages) - 1
+    messages, both_ref, cl_ref = outs[:-2], outs[-2], outs[-1]
+    per = len(messages)
     faces, (chans, cols) = up_ref.shape[0] - 1, up_ref.shape[1:]
     span = rows + 2
     first_band, first_tile = s_ref[BAND] == 0, s_ref[TILE] == 0
@@ -422,7 +436,9 @@
     wrap = move(side_by_side(theirs, tc, bc), wrap_ref[...]).astype(BF)
     cl_ref[...] = side_by_side(pick2(first_tile, own, wrap), pick2(first_tile, wrap, own))
     on_row = jnp.logical_or(first_band, s_ref[BAND] == bands - 1)
-    for m in range(per + 1):
+    both_ref[:, : 4 * cols] = cl_ref[...]
+    both_ref[:, 4 * cols :] = jnp.zeros((chans, 4 * cols), BF)
+    for m in range(per):
 
         @pl.when(s_ref[SENDS + m] == 0)
         def _(m=m):
@@ -451,13 +467,12 @@
                 def _(j=j, piece=pieces[j]):
                     messages[j][:, where] = piece.astype(BF)
 
-            @pl.when(s_ref[SENDS + per] == 1)
-            def _(piece=pieces[0]):
-                messages[per][:, where] = piece.astype(BF)
-
-            @pl.when(s_ref[SENDS + per] == 2)
-            def _(piece=pieces[per - 1]):
-                messages[per][:, where] = piece.astype(BF)
+            second = slice((4 + g) * cols, (5 + g) * cols)
+            for code, j in ((1, 0), (2, per - 1)):
+
+                @pl.when(s_ref[SENDS + per] == code)
+                def _(piece=pieces[j]):
+                    both_ref[:, second] = piece.astype(BF)
 
 
 def seams_kernel(s_ref, *refs, rounds, rows, bands):
@@ -473,7 +488,7 @@
 
         @pl.when(s_ref[COL_ROUND] == r)
         def _(r=r):
-            other_ref[...] = got[r][...]
+            other_ref[...] = got[r][:, got[r].shape[1] - 4 * cols :]
 
     @pl.when((s_ref[COL_ROUND] == rounds) & first_band)
     def _():
@@ -495,7 +510,7 @@
 
                 @pl.when(s_ref[code] == value)
                 def _(to=to, src=src):
-                    to[...] = src[...]
+                    to[...] = src[:, : 4 * cols]
 
         for f in range(faces + 1):
             rows_ref[f] = pick2(first_band, up_ref[f], bot_ref[f])
@@ -581,7 +596,7 @@
     bottom = lax.ppermute(up, "band", [(j, i) for i, j in around])
     outs = whole(
         functools.partial(lines_kernel, bands=bands, rows=rows),
-        [(chans, 4 * cols)] * (rounds + 1),
+        [(chans, 4 * cols)] * plan.per + [(chans, 8 * cols), (chans, 4 * cols)],
         [],
         scalars, up, down, top, bottom, low, high, left, right, own, wrap, unit_ends,
     )
@@ -638,11 +653,13 @@
     order = jnp.arange(items)
     same = (target[:, None] == target[None, :]) & (order[None, :] < order[:, None])
     position = target * capacity + jnp.sum(same.astype(jnp.int32), axis=1)
-    hit = position[:, None] == jnp.arange(total)[None, :]
-    out_slots = slots_dev + jnp.sum(
-        jnp.where(hit, (dest_block.reshape(items) - slots_dev)[:, None], 0), axis=0
-    )
-    slots = lax.all_to_all(out_slots.reshape(devices, capacity), AXES, split_axis=0, concat_axis=0, tiled=True)
+    base = 1 << slots_dev.bit_length()
+    codes = lax.all_gather(target * base + dest_block.reshape(items), AXES)
+    mine = codes // base == lax.axis_index(AXES)
+    earlier = jnp.asarray(np.triu(np.ones((items, items), np.float32), 1), BF)
+    rank = jnp.dot(mine.astype(BF), earlier, preferred_element_type=F32).astype(jnp.int32)
+    hit = mine[:, None, :] & (rank[:, None, :] == jnp.arange(capacity)[None, :, None])
+    slots = slots_dev + jnp.sum(jnp.where(hit, (codes % base - slots_dev)[:, None, :], 0), axis=2)
     outgoing = regrid(source, regrid_weights, position, total)
     arrived = lax.all_to_all(
         outgoing.reshape(devices, capacity, fields, block_len), AXES, split_axis=0, concat_axis=0, tiled=True

time: 351 us -> 364 us (1.037)
  blocking collectives: 0 us -> 134 us
  waiting for transfers between devices: 123 us -> 31.6 us
  starting transfers between devices: 112 us -> 92.1 us
  Pallas kernels: 91.9 us -> 83.1 us
    all_gather x0 -> x1, blocking collectives: none -> 134 us  [local(): codes = lax.all_gather(target * base + dest_block.reshape(items), AXES)]
    all_to_all x1, waiting for transfers between devices: 89.8 us -> 0.01 us  [local(): lax.all_to_all(outgoing.reshape(devices, capacity, fields, block_len), AX...]
    ppermute x2, starting transfers between devices: 40.8 us -> 27.8 us  [exchange(): rrow = lax.ppermute(srow, AXES, plan.flip_row)]
    all_to_all x1 -> x0, starting transfers between devices: 11.1 us -> none  [local(): lax.all_to_all(out_slots.reshape(devices, capacity), AXES, split_axis=0,...]
    pallas_call x2, Pallas kernels: 41.8 us -> 32.3 us  [conv(): pl.pallas_call(functools.partial(conv_kernel, last=last), grid=(face_coun...]
    unnamed x101 -> x106, local copies, waits for them, and re-layouts: 10.9 us -> 11.1 us
  transfers between devices with their start and end apart: 32 -> 31, of which waited for: 13 -> 12; matrix products, arithmetic and copies ran while one was open for 3% -> 3% of each run, Pallas kernels for 3% -> 0%
where the time goes in v1:
time: 364 us; the launch traced here: 362 us
  blocking collectives  134 us (37%)
  starting transfers between devices  92.1 us (25%)
  Pallas kernels  83.1 us (23%)
  waiting for transfers between devices  31.6 us (9%)
  local copies, waits for them, and re-layouts  16 us (4%)
  other arithmetic  4.05 us (1%)
    all_gather x1, blocking collectives, local(): codes = lax.all_gather(target * base + dest_block.reshape(items), AXES)  134 us
    pallas_call x2, Pallas kernels, conv(): pl.pallas_call(functools.partial(conv_kernel, last=last), grid=(face_coun...  32.3 us
    ppermute x18, starting transfers between devices, exchange(): lax.ppermute(m, AXES, pairs)  29.5 us
    ppermute x2, starting transfers between devices, exchange(): rrow = lax.ppermute(srow, AXES, plan.flip_row)  27.8 us
    pallas_call x6, Pallas kernels, whole(): pl.pallas_call(kernel, in_specs=[pl.BlockSpec(memory_space=pltpu.SMEM)] +...  24.7 us
    all_to_all x1, starting transfers between devices, local(): lax.all_to_all(outgoing.reshape(devices, capacity, fields, block_len), AX...  11.6 us
    pallas_call x1, Pallas kernels, place(): pl.pallas_call(functools.partial(place_kernel, chunk=chunk), grid_spec=pl...  11.3 us
    unnamed x106, local copies, waits for them, and re-layouts  11.1 us
  transfers between devices with their start and end apart: 31, of which 12 were waited for; matrix products, arithmetic and copies ran while one was open for 3% of the time, Pallas kernels for 0%

profile of v1, /device:TPU:0, one launch (start us, length us, event | category | flops | bytes accessed | tf_op | source)
XLA Modules:
  0.0 362.4 jit_solution(8326853203054553898)
XLA Ops:
  1.6 10.5 %shard_map.289 = bf16[768,40,128]{2,1,0:T(8,128)(2,1)} custom-call(s32[256]{0:T(256)} %multiply_add_fusion.1.pos_ref, bf16[40,8192]{1,0:T(8,128)(2,1)} %src_ref.1, bf16[64,4,128,128]{3,2,1,0:T(8,128)(2,1)} %w_ref.1), custom_call_target="tpu_custom_call" | custom-call | flops 335544320 | bytes 17000000 | tf_op jit(solution)/shard_map/pallas_call | solution.py:32
  12.3 11.6 %all-to-all-start = ((bf16[128,6,40,128]{3,2,1,0:T(8,128)(2,1)}), bf16[128,6,40,128]{3,2,1,0:T(8,128)(2,1)}, u32[]{:S(2)}, u32[]{:S(2)}) async-start(bf16[128,6,40,128]{3,2,1,0:T(8,128)(2,1)} %bitcast.77), calls=%async_computation | async-start | bytes 15728640 | tf_op jit(solution)/shard_map/all_to_all | solution.py:664
  24.2 134.4 %all-gather = s32[128,1,256]{2,1,0:T(1,128)S(1)} all-gather(s32[1,1,256]{2,1,0:T(1,128)S(1)} %reshape.108), channel_id=1, replica_groups=mesh['band'=32,'tile'=4] {'band','tile'}, dimensions={0}, use_global_device_ids=true | all-gather | bytes 132096 | tf_op jit(solution)/shard_map/all_gather | solution.py:657
  162.3 11.3 %shard_map.290 = (bf16[192,40,128]{2,1,0:T(8,128)(2,1)}, bf16[40,256]{1,0:T(8,128)(2,1)}, bf16[40,256]{1,0:T(8,128)(2,1)}) custom-call(s32[768]{0:T(1024)} %add.67.slot_ref, bf16[768,40,128]{2,1,0:T(8,128)(2,1)} %bitcast.15.in_ref), custom_call_target="tpu_custom_call" | custom-call | tf_op jit(solution)/shard_map/pallas_call | solution.py:90
  173.6 3.2 collective-permute-start.1
  179.4 2.0 shard_map.291
  181.4 5.1 %collective-permute-start.3 = (bf16[13,40,128]{2,1,0:T(8,128)(2,1)}, bf16[13,40,128]{2,1,0:T(8,128)(2,1)S(1)}, u32[]{:S(2)}, u32[]{:S(2)}) collective-permute-start(bf16[13,40,128]{2,1,0:T(8,128)(2,1)} %get-tuple-element.50.up_ref.refs_12_), channel_id=1, source_target_pairs={{4,0},{8,4},{12,8},{16,12},{20,16},{24,20},{28,24},{32,28},{36,32}... | collective-permute-start | bytes 399368 | tf_op jit(solution)/shard_map/ppermute | solution.py:596
  186.5 2.9 collective-permute-done.2.top_ref.refs_14_
  190.7 3.8 %shard_map.292 = (bf16[40,512]{1,0:T(8,128)(2,1)}, bf16[40,512]{1,0:T(8,128)(2,1)}, bf16[40,512]{1,0:T(8,128)(2,1)}, bf16[40,512]{1,0:T(8,128)(2,1)}, bf16[40,51...) custom-call(s32[54]{0:T(128)} %concatenate.17.s_ref, ...), custom_call_target="tpu_custom_call" | custom-call | tf_op jit(solution)/shard_map/pallas_call | solution.py:365
  196.4 1.9 collective-permute-start.11
  199.0 1.9 collective-permute-start.5
  202.2 1.9 collective-permute-start.6
  204.2 1.9 collective-permute-start.7
  210.1 3.6 %collective-permute-done.8.refs_4_ = bf16[40,512]{1,0:T(8,128)(2,1)S(1)} collective-permute-done((bf16[40,512]{1,0:T(8,128)(2,1)}, bf16[40,512]{1,0:T(8,128)(2,1)S(1)}, u32[]{:S(2)}, u32[]{:S(2)}) %collective-permute-start.8) | collective-permute-done | bytes 40992 | tf_op jit(solution)/shard_map/ppermute | solution.py:604
  215.8 3.9 %shard_map.293 = (bf16[13,40,128]{2,1,0:T(8,128)(2,1)}, bf16[40,256]{1,0:T(8,128)(2,1)}) custom-call(s32[54]{0:T(128)} %concatenate.17.s_ref, bf16[40,512]{1,0:T(8,128)(2,1)} %copy-done.29, bf16[40,512]{1,0:T(8,128)(2,1)} %copy-done.30, bf16[40,512]{1,0:T(8,128)(2,1)} %copy-done.31, bf16[40,512]{1,0:T(8,128)(2,1)} %copy-done.32, bf16[40,512]{1,0:T(8,128)(2,1)} %copy-done.33, ...), custom_call_target="tpu_custom_call" | custom-call | tf_op jit(solution)/shard_map/pallas_call | solution.py:365
  219.7 14.4 %collective-permute-start.13 = (bf16[13,40,128]{2,1,0:T(8,128)(2,1)}, bf16[13,40,128]{2,1,0:T(8,128)(2,1)S(1)}, u32[]{:S(2)}, u32[]{:S(2)}) collective-permute-start(bf16[13,40,128]{2,1,0:T(8,128)(2,1)} %get-tuple-element.62.srow_ref), channel_id=1, source_target_pairs={{0,3},{1,2},{2,1},{3,0},{124,127},{125,126},{126,125},{127,124}} | collective-permute-start | bytes 399368 | tf_op jit(solution)/shard_map/ppermute | solution.py:618
  237.8 4.9 %collective-permute-done.14.rcol_ref = bf16[40,256]{1,0:T(8,128)(2,1)S(1)} collective-permute-done((bf16[40,256]{1,0:T(8,128)(2,1)}, bf16[40,256]{1,0:T(8,128)(2,1)S(1)}, u32[]{:S(2)}, u32[]{:S(2)}) %collective-permute-start.14) | collective-permute-done | bytes 20512 | tf_op jit(solution)/shard_map/ppermute | solution.py:619
  244.0 2.6 shard_map.294
  246.6 13.6 %shard_map.295 = (bf16[12,16,128,128]{3,2,1,0:T(8,128)(2,1)}, bf16[128,256]{1,0:T(8,128)(2,1)}, bf16[128,256]{1,0:T(8,128)(2,1)}) custom-call(bf16[256,512]{1,0:T(8,128)(2,1)} %bitcast.84, f32[256,1]{1,0:T(8,128)} %copy.54.b_ref, bf16[12,16,40,128]{3,2,1,0:T(8,128)(2,1)} %bitcast.80, bf16[12,40,128]{2,1,0:T(8,128)(2,1)} %get-tuple-element.64.top_ref, ...), custom_call_target="tpu_custom_call" | custom-call | tf_op jit(solution)/shard_map/pallas_call | solution.py:209
  260.4 3.2 collective-permute-start.16
  263.6 2.4 collective-permute-done.15.left_ref
  266.7 2.4 shard_map.296
  269.1 5.1 %collective-permute-start.18 = (bf16[13,128,128]{2,1,0:T(8,128)(2,1)}, bf16[13,128,128]{2,1,0:T(8,128)(2,1)S(1)}, u32[]{:S(2)}, u32[]{:S(2)}) collective-permute-start(bf16[13,128,128]{2,1,0:T(8,128)(2,1)} %get-tuple-element.71.up_ref.refs_12_), channel_id=1, source_target_pairs={{4,0},{8,4},{12,8},{16,12},{20,16},{24,20},{28,24},{32,28},{36,32}... | collective-permute-start | bytes 1277960 | tf_op jit(solution)/shard_map/ppermute | solution.py:596
  274.2 6.0 %collective-permute-done.17.top_ref.refs_14_ = bf16[13,128,128]{2,1,0:T(8,128)(2,1)S(1)} collective-permute-done((bf16[13,128,128]{2,1,0:T(8,128)(2,1)}, bf16[13,128,128]{2,1,0:T(8,128)(2,1)S(1)}, u32[]{:S(2)}, u32[]{:S(2)}) %collective-permute-start.17) | collective-permute-done | bytes 426016 | tf_op jit(solution)/shard_map/ppermute | solution.py:595
  281.8 5.8 %shard_map.297 = (bf16[128,512]{1,0:T(8,128)(2,1)}, bf16[128,512]{1,0:T(8,128)(2,1)}, bf16[128,512]{1,0:T(8,128)(2,1)}, bf16[128,512]{1,0:T(8,128)(2,1)}, bf16[1...) custom-call(s32[54]{0:T(128)} %concatenate.17.s_ref, ...), custom_call_target="tpu_custom_call" | custom-call | tf_op jit(solution)/shard_map/pallas_call | solution.py:365
  304.7 2.2 collective-permute-done.25.refs_6_
  309.1 5.5 %shard_map.298 = (bf16[13,128,128]{2,1,0:T(8,128)(2,1)}, bf16[128,256]{1,0:T(8,128)(2,1)}) custom-call(s32[54]{0:T(128)} %concatenate.17.s_ref, bf16[128,512]{1,0:T(8,128)(2,1)} %copy-done.13, bf16[128,512]{1,0:T(8,128)(2,1)} %copy-done.14, bf16[128,512]{1,0:T(8,128)(2,1)} %copy-done.15, bf16[128,512]{1,0:T(8,128)(2,1)} %copy-done.16, ...), custom_call_target="tpu_custom_call" | custom-call | tf_op jit(solution)/shard_map/pallas_call | solution.py:365
  314.5 13.4 %collective-permute-start.28 = (bf16[13,128,128]{2,1,0:T(8,128)(2,1)}, bf16[13,128,128]{2,1,0:T(8,128)(2,1)S(1)}, u32[]{:S(2)}, u32[]{:S(2)}) collective-permute-start(bf16[13,128,128]{2,1,0:T(8,128)(2,1)} %get-tuple-element.83.srow_ref), channel_id=1, source_target_pairs={{0,3},{1,2},{2,1},{3,0},{124,127},{125,126},{126,125},{127,124}} | collective-permute-start | bytes 1277960 | tf_op jit(solution)/shard_map/ppermute | solution.py:618
  330.0 4.4 %collective-permute-start.29 = (bf16[128,256]{1,0:T(8,128)(2,1)}, bf16[128,256]{1,0:T(8,128)(2,1)S(1)}, u32[]{:S(2)}, u32[]{:S(2)}) collective-permute-start(bf16[128,256]{1,0:T(8,128)(2,1)} %get-tuple-element.84.scol_ref), channel_id=1, source_target_pairs={{0,124},{3,127},{4,120},{7,123},{8,116},{11,119},{12,112},{15,115}... | collective-permute-start | bytes 196616 | tf_op jit(solution)/shard_map/ppermute | solution.py:619
  335.2 3.8 %collective-permute-done.29.rcol_ref = bf16[128,256]{1,0:T(8,128)(2,1)S(1)} collective-permute-done((bf16[128,256]{1,0:T(8,128)(2,1)}, bf16[128,256]{1,0:T(8,128)(2,1)S(1)}, u32[]{:S(2)}, u32[]{:S(2)}) %collective-permute-start.29) | collective-permute-done | bytes 65568 | tf_op jit(solution)/shard_map/ppermute | solution.py:619
  340.5 3.2 shard_map.299
  343.7 18.7 %shard_map.300 = bf16[128,12,16,128]{3,2,1,0:T(8,128)(2,1)} custom-call(bf16[256,1536]{1,0:T(8,128)(2,1)} %bitcast.81, f32[256,1]{1,0:T(8,128)} %copy.55.b_ref, bf16[12,16,128,128]{3,2,1,0:T(8,128)(2,1)} %get-tuple-element.68.first_ref.last_ref.x_ref, bf16[12,128,128]{2,1,0:T(8,128)(2,1)} %get-tuple-element.85.top_ref, ...), custom_call_target="tpu_custom_call" | custom-call | tf_op jit(solution)/shard_map/pallas_call | solution.py:209
  (191 shorter events, 49.9 us)
Async XLA Ops:
  12.3 150.0 %all-to-all-start = ((bf16[128,6,40,128]{3,2,1,0:T(8,128)(2,1)}), bf16[128,6,40,128]{3,2,1,0:T(8,128)(2,1)}, u32[]{:S(2)}, u32[]{:S(2)}) async-start(bf16[128,6,40,128]{3,2,1,0:T(8,128)(2,1)} %bitcast.77), calls=%async_computation | async-start | bytes 15728640 | tf_op jit(solution)/shard_map/all_to_all | solution.py:664
  23.9 162.5 %copy-start.44 = (pred[128]{0:T(512)(128)(4,1)S(1)}, pred[128]{0:T(512)(128)(4,1)}, u32[]{:S(2)}) copy-start(pred[128]{0:T(512)(128)(4,1)} %constant.117.clone) | copy-start | bytes 388
  173.6 5.2 %collective-permute-start = (bf16[40,256]{1,0:T(8,128)(2,1)}, bf16[40,256]{1,0:T(8,128)(2,1)S(1)}, u32[]{:S(2)}, u32[]{:S(2)}) collective-permute-start(bf16[40,256]{1,0:T(8,128)(2,1)} %get-tuple-element.48.high_ref), channel_id=1, source_target_pairs={{0,1},{1,2},{2,3},{3,0},{4,5},{5,6},{6,7},{7,4},{8,9},{9,10},{10,1... | collective-permute-start | bytes 61448 | tf_op jit(solution)/shard_map/ppermute | solution.py:591
  173.6 5.2 %collective-permute-start.1 = (bf16[40,256]{1,0:T(8,128)(2,1)}, bf16[40,256]{1,0:T(8,128)(2,1)S(1)}, u32[]{:S(2)}, u32[]{:S(2)}) collective-permute-start(bf16[40,256]{1,0:T(8,128)(2,1)} %get-tuple-element.49.low_ref), channel_id=1, source_target_pairs={{1,0},{2,1},{3,2},{0,3},{5,4},{6,5},{7,6},{4,7},{9,8},{10,9},{11,1... | collective-permute-start | bytes 61448 | tf_op jit(solution)/shard_map/ppermute | solution.py:592
  181.4 7.9 %collective-permute-start.2 = (bf16[13,40,128]{2,1,0:T(8,128)(2,1)}, bf16[13,40,128]{2,1,0:T(8,128)(2,1)S(1)}, u32[]{:S(2)}, u32[]{:S(2)}) collective-permute-start(bf16[13,40,128]{2,1,0:T(8,128)(2,1)} %get-tuple-element.51.down_ref.refs_13_), channel_id=1, source_target_pairs={{0,4},{4,8},{8,12},{12,16},{16,20},{20,24},{24,28},{28,32},{32,36}... | collective-permute-start | bytes 399368 | tf_op jit(solution)/shard_map/ppermute | solution.py:595
  181.4 7.9 %collective-permute-start.3 = (bf16[13,40,128]{2,1,0:T(8,128)(2,1)}, bf16[13,40,128]{2,1,0:T(8,128)(2,1)S(1)}, u32[]{:S(2)}, u32[]{:S(2)}) collective-permute-start(bf16[13,40,128]{2,1,0:T(8,128)(2,1)} %get-tuple-element.50.up_ref.refs_12_), channel_id=1, source_target_pairs={{4,0},{8,4},{12,8},{16,12},{20,16},{24,20},{28,24},{32,28},{36,32}... | collective-permute-start | bytes 399368 | tf_op jit(solution)/shard_map/ppermute | solution.py:596
  194.4 7.8 %collective-permute-start.10 = (bf16[40,512]{1,0:T(8,128)(2,1)}, bf16[40,512]{1,0:T(8,128)(2,1)S(1)}, u32[]{:S(2)}, u32[]{:S(2)}) collective-permute-start(bf16[40,512]{1,0:T(8,128)(2,1)} %get-tuple-element.58), channel_id=1, source_target_pairs={{0,24},{24,0},{124,27},{27,124},{1,56},{56,1},{125,59},{59,125},{2... | collective-permute-start | bytes 122888 | tf_op jit(solution)/shard_map/ppermute | solution.py:604
  196.4 7.8 %collective-permute-start.11 = (bf16[40,512]{1,0:T(8,128)(2,1)}, bf16[40,512]{1,0:T(8,128)(2,1)S(1)}, u32[]{:S(2)}, u32[]{:S(2)}) collective-permute-start(bf16[40,512]{1,0:T(8,128)(2,1)} %get-tuple-element.59.refs_10_), channel_id=1, source_target_pairs={{0,28},{28,0},{124,31},{31,124},{1,60},{60,1},{125,63},{63,125},{2... | collective-permute-start | bytes 122888 | tf_op jit(solution)/shard_map/ppermute | solution.py:604
  198.3 7.8 %collective-permute-start.4 = (bf16[40,512]{1,0:T(8,128)(2,1)}, bf16[40,512]{1,0:T(8,128)(2,1)S(1)}, u32[]{:S(2)}, u32[]{:S(2)}) collective-permute-start(bf16[40,512]{1,0:T(8,128)(2,1)} %get-tuple-element.52.refs_9_), channel_id=1, source_target_pairs={{1,32},{32,1},{125,35},{35,125},{2,64},{64,2},{126,67},{67,126},{3... | collective-permute-start | bytes 122888 | tf_op jit(solution)/shard_map/ppermute | solution.py:604
  199.0 9.1 %collective-permute-start.5 = (bf16[40,512]{1,0:T(8,128)(2,1)}, bf16[40,512]{1,0:T(8,128)(2,1)S(1)}, u32[]{:S(2)}, u32[]{:S(2)}) collective-permute-start(bf16[40,512]{1,0:T(8,128)(2,1)} %get-tuple-element.53), channel_id=1, source_target_pairs={{0,4},{4,0},{124,7},{7,124},{1,36},{36,1},{125,39},{39,125},{2,68}... | collective-permute-start | bytes 122888 | tf_op jit(solution)/shard_map/ppermute | solution.py:604
  201.5 13.6 %collective-permute-start.12 = (bf16[40,1024]{1,0:T(8,128)(2,1)}, bf16[40,1024]{1,0:T(8,128)(2,1)S(1)}, u32[]{:S(2)}, u32[]{:S(2)}) collective-permute-start(bf16[40,1024]{1,0:T(8,128)(2,1)} %get-tuple-element.60), channel_id=1, source_target_pairs={{3,124},{124,3}} | collective-permute-start | bytes 245768 | tf_op jit(solution)/shard_map/ppermute | solution.py:604
  202.2 7.8 %collective-permute-start.6 = (bf16[40,512]{1,0:T(8,128)(2,1)}, bf16[40,512]{1,0:T(8,128)(2,1)S(1)}, u32[]{:S(2)}, u32[]{:S(2)}) collective-permute-start(bf16[40,512]{1,0:T(8,128)(2,1)} %get-tuple-element.54), channel_id=1, source_target_pairs={{0,8},{8,0},{124,11},{11,124},{1,40},{40,1},{125,43},{43,125},{2,7... | collective-permute-start | bytes 122888 | tf_op jit(solution)/shard_map/ppermute | solution.py:604
  204.2 5.9 %collective-permute-start.7 = (bf16[40,512]{1,0:T(8,128)(2,1)}, bf16[40,512]{1,0:T(8,128)(2,1)S(1)}, u32[]{:S(2)}, u32[]{:S(2)}) collective-permute-start(bf16[40,512]{1,0:T(8,128)(2,1)} %get-tuple-element.55), channel_id=1, source_target_pairs={{0,12},{12,0},{124,15},{15,124},{1,44},{44,1},{125,47},{47,125},{2... | collective-permute-start | bytes 122888 | tf_op jit(solution)/shard_map/ppermute | solution.py:604
  206.1 7.6 %collective-permute-start.8 = (bf16[40,512]{1,0:T(8,128)(2,1)}, bf16[40,512]{1,0:T(8,128)(2,1)S(1)}, u32[]{:S(2)}, u32[]{:S(2)}) collective-permute-start(bf16[40,512]{1,0:T(8,128)(2,1)} %get-tuple-element.56), channel_id=1, source_target_pairs={{0,16},{16,0},{124,19},{19,124},{1,48},{48,1},{125,51},{51,125},{2... | collective-permute-start | bytes 122888 | tf_op jit(solution)/shard_map/ppermute | solution.py:604
  208.1 7.0 %collective-permute-start.9 = (bf16[40,512]{1,0:T(8,128)(2,1)}, bf16[40,512]{1,0:T(8,128)(2,1)S(1)}, u32[]{:S(2)}, u32[]{:S(2)}) collective-permute-start(bf16[40,512]{1,0:T(8,128)(2,1)} %get-tuple-element.57), channel_id=1, source_target_pairs={{0,20},{20,0},{124,23},{23,124},{1,52},{52,1},{125,55},{55,125},{2... | collective-permute-start | bytes 122888 | tf_op jit(solution)/shard_map/ppermute | solution.py:604
  219.7 23.1 %collective-permute-start.13 = (bf16[13,40,128]{2,1,0:T(8,128)(2,1)}, bf16[13,40,128]{2,1,0:T(8,128)(2,1)S(1)}, u32[]{:S(2)}, u32[]{:S(2)}) collective-permute-start(bf16[13,40,128]{2,1,0:T(8,128)(2,1)} %get-tuple-element.62.srow_ref), channel_id=1, source_target_pairs={{0,3},{1,2},{2,1},{3,0},{124,127},{125,126},{126,125},{127,124}} | collective-permute-start | bytes 399368 | tf_op jit(solution)/shard_map/ppermute | solution.py:618
  234.1 8.6 %collective-permute-start.14 = (bf16[40,256]{1,0:T(8,128)(2,1)}, bf16[40,256]{1,0:T(8,128)(2,1)S(1)}, u32[]{:S(2)}, u32[]{:S(2)}) collective-permute-start(bf16[40,256]{1,0:T(8,128)(2,1)} %get-tuple-element.63.scol_ref), channel_id=1, source_target_pairs={{0,124},{3,127},{4,120},{7,123},{8,116},{11,119},{12,112},{15,115}... | collective-permute-start | bytes 61448 | tf_op jit(solution)/shard_map/ppermute | solution.py:619
  260.2 5.9 %collective-permute-start.15 = (bf16[128,256]{1,0:T(8,128)(2,1)}, bf16[128,256]{1,0:T(8,128)(2,1)S(1)}, u32[]{:S(2)}, u32[]{:S(2)}) collective-permute-start(bf16[128,256]{1,0:T(8,128)(2,1)} %get-tuple-element.69.high_ref), channel_id=1, source_target_pairs={{0,1},{1,2},{2,3},{3,0},{4,5},{5,6},{6,7},{7,4},{8,9},{9,10},{10,1... | collective-permute-start | bytes 196616 | tf_op jit(solution)/shard_map/ppermute | solution.py:591
  260.4 5.7 %collective-permute-start.16 = (bf16[128,256]{1,0:T(8,128)(2,1)}, bf16[128,256]{1,0:T(8,128)(2,1)S(1)}, u32[]{:S(2)}, u32[]{:S(2)}) collective-permute-start(bf16[128,256]{1,0:T(8,128)(2,1)} %get-tuple-element.70.low_ref), channel_id=1, source_target_pairs={{1,0},{2,1},{3,2},{0,3},{5,4},{6,5},{7,6},{4,7},{9,8},{10,9},{11,1... | collective-permute-start | bytes 196616 | tf_op jit(solution)/shard_map/ppermute | solution.py:592
  269.1 11.1 %collective-permute-start.17 = (bf16[13,128,128]{2,1,0:T(8,128)(2,1)}, bf16[13,128,128]{2,1,0:T(8,128)(2,1)S(1)}, u32[]{:S(2)}, u32[]{:S(2)}) collective-permute-start(bf16[13,128,128]{2,1,0:T(8,128)(2,1)} %get-tuple-element.72.down_ref.refs_13_), channel_id=1, source_target_pairs={{0,4},{4,8},{8,12},{12,16},{16,20},{20,24},{24,28},{28,32},{32,36}... | collective-permute-start | bytes 1277960 | tf_op jit(solution)/shard_map/ppermute | solution.py:595
  269.1 11.1 %collective-permute-start.18 = (bf16[13,128,128]{2,1,0:T(8,128)(2,1)}, bf16[13,128,128]{2,1,0:T(8,128)(2,1)S(1)}, u32[]{:S(2)}, u32[]{:S(2)}) collective-permute-start(bf16[13,128,128]{2,1,0:T(8,128)(2,1)} %get-tuple-element.71.up_ref.refs_12_), channel_id=1, source_target_pairs={{4,0},{8,4},{12,8},{16,12},{20,16},{24,20},{28,24},{32,28},{36,32}... | collective-permute-start | bytes 1277960 | tf_op jit(solution)/shard_map/ppermute | solution.py:596
  287.6 7.1 %collective-permute-start.19 = (bf16[128,512]{1,0:T(8,128)(2,1)}, bf16[128,512]{1,0:T(8,128)(2,1)S(1)}, u32[]{:S(2)}, u32[]{:S(2)}) collective-permute-start(bf16[128,512]{1,0:T(8,128)(2,1)} %get-tuple-element.73.refs_9_), channel_id=1, source_target_pairs={{1,32},{32,1},{125,35},{35,125},{2,64},{64,2},{126,67},{67,126},{3... | collective-permute-start | bytes 393224 | tf_op jit(solution)/shard_map/ppermute | solution.py:604
  288.2 8.4 %collective-permute-start.20 = (bf16[128,512]{1,0:T(8,128)(2,1)}, bf16[128,512]{1,0:T(8,128)(2,1)S(1)}, u32[]{:S(2)}, u32[]{:S(2)}) collective-permute-start(bf16[128,512]{1,0:T(8,128)(2,1)} %get-tuple-element.74), channel_id=1, source_target_pairs={{0,4},{4,0},{124,7},{7,124},{1,36},{36,1},{125,39},{39,125},{2,68}... | collective-permute-start | bytes 393224 | tf_op jit(solution)/shard_map/ppermute | solution.py:604
  290.2 8.4 %collective-permute-start.21 = (bf16[128,512]{1,0:T(8,128)(2,1)}, bf16[128,512]{1,0:T(8,128)(2,1)S(1)}, u32[]{:S(2)}, u32[]{:S(2)}) collective-permute-start(bf16[128,512]{1,0:T(8,128)(2,1)} %get-tuple-element.75), channel_id=1, source_target_pairs={{0,8},{8,0},{124,11},{11,124},{1,40},{40,1},{125,43},{43,125},{2,7... | collective-permute-start | bytes 393224 | tf_op jit(solution)/shard_map/ppermute | solution.py:604
  292.1 8.5 %collective-permute-start.22 = (bf16[128,512]{1,0:T(8,128)(2,1)}, bf16[128,512]{1,0:T(8,128)(2,1)S(1)}, u32[]{:S(2)}, u32[]{:S(2)}) collective-permute-start(bf16[128,512]{1,0:T(8,128)(2,1)} %get-tuple-element.76), channel_id=1, source_target_pairs={{0,12},{12,0},{124,15},{15,124},{1,44},{44,1},{125,47},{47,125},{2... | collective-permute-start | bytes 393224 | tf_op jit(solution)/shard_map/ppermute | solution.py:604
  294.0 14.3 %collective-permute-start.27 = (bf16[128,1024]{1,0:T(8,128)(2,1)}, bf16[128,1024]{1,0:T(8,128)(2,1)S(1)}, u32[]{:S(2)}, u32[]{:S(2)}) collective-permute-start(bf16[128,1024]{1,0:T(8,128)(2,1)} %get-tuple-element.81), channel_id=1, source_target_pairs={{3,124},{124,3}} | collective-permute-start | bytes 786440 | tf_op jit(solution)/shard_map/ppermute | solution.py:604
  294.7 8.6 %collective-permute-start.23 = (bf16[128,512]{1,0:T(8,128)(2,1)}, bf16[128,512]{1,0:T(8,128)(2,1)S(1)}, u32[]{:S(2)}, u32[]{:S(2)}) collective-permute-start(bf16[128,512]{1,0:T(8,128)(2,1)} %get-tuple-element.77), channel_id=1, source_target_pairs={{0,16},{16,0},{124,19},{19,124},{1,48},{48,1},{125,51},{51,125},{2... | collective-permute-start | bytes 393224 | tf_op jit(solution)/shard_map/ppermute | solution.py:604
  296.7 8.0 %collective-permute-start.24 = (bf16[128,512]{1,0:T(8,128)(2,1)}, bf16[128,512]{1,0:T(8,128)(2,1)S(1)}, u32[]{:S(2)}, u32[]{:S(2)}) collective-permute-start(bf16[128,512]{1,0:T(8,128)(2,1)} %get-tuple-element.78), channel_id=1, source_target_pairs={{0,20},{20,0},{124,23},{23,124},{1,52},{52,1},{125,55},{55,125},{2... | collective-permute-start | bytes 393224 | tf_op jit(solution)/shard_map/ppermute | solution.py:604
  298.6 8.3 %collective-permute-start.25 = (bf16[128,512]{1,0:T(8,128)(2,1)}, bf16[128,512]{1,0:T(8,128)(2,1)S(1)}, u32[]{:S(2)}, u32[]{:S(2)}) collective-permute-start(bf16[128,512]{1,0:T(8,128)(2,1)} %get-tuple-element.79), channel_id=1, source_target_pairs={{0,24},{24,0},{124,27},{27,124},{1,56},{56,1},{125,59},{59,125},{2... | collective-permute-start | bytes 393224 | tf_op jit(solution)/shard_map/ppermute | solution.py:604
  300.6 7.7 %collective-permute-start.26 = (bf16[128,512]{1,0:T(8,128)(2,1)}, bf16[128,512]{1,0:T(8,128)(2,1)S(1)}, u32[]{:S(2)}, u32[]{:S(2)}) collective-permute-start(bf16[128,512]{1,0:T(8,128)(2,1)} %get-tuple-element.80.refs_10_), channel_id=1, source_target_pairs={{0,28},{28,0},{124,31},{31,124},{1,60},{60,1},{125,63},{63,125},{2... | collective-permute-start | bytes 393224 | tf_op jit(solution)/shard_map/ppermute | solution.py:604
  314.5 24.6 %collective-permute-start.28 = (bf16[13,128,128]{2,1,0:T(8,128)(2,1)}, bf16[13,128,128]{2,1,0:T(8,128)(2,1)S(1)}, u32[]{:S(2)}, u32[]{:S(2)}) collective-permute-start(bf16[13,128,128]{2,1,0:T(8,128)(2,1)} %get-tuple-element.83.srow_ref), channel_id=1, source_target_pairs={{0,3},{1,2},{2,1},{3,0},{124,127},{125,126},{126,125},{127,124}} | collective-permute-start | bytes 1277960 | tf_op jit(solution)/shard_map/ppermute | solution.py:618
  330.0 9.1 %collective-permute-start.29 = (bf16[128,256]{1,0:T(8,128)(2,1)}, bf16[128,256]{1,0:T(8,128)(2,1)S(1)}, u32[]{:S(2)}, u32[]{:S(2)}) collective-permute-start(bf16[128,256]{1,0:T(8,128)(2,1)} %get-tuple-element.84.scol_ref), channel_id=1, source_target_pairs={{0,124},{3,127},{4,120},{7,123},{8,116},{11,119},{12,112},{15,115}... | collective-permute-start | bytes 196616 | tf_op jit(solution)/shard_map/ppermute | solution.py:619
  (49 other events, 2321.1 us)

commit v2 on v1

--- a/solution.py
+++ b/solution.py
@@ -56,19 +56,21 @@
     return low, high
 
 
-def place_kernel(slot_ref, in_ref, out_ref, low_ref, high_ref, acc_ref, *, chunk):
+def place_kernel(slot_ref, in_ref, out_ref, low_ref, high_ref, acc_ref, acc2_ref, *, chunk):
     step = pl.program_id(0)
 
     @pl.when(step == 0)
     def _():
         acc_ref[...] = jnp.zeros_like(acc_ref)
+        acc2_ref[...] = jnp.zeros_like(acc2_ref)
 
     def body(i, carry):
-        where = slot_ref[step * chunk + i]
-        acc_ref[where] += in_ref[i].astype(F32)
+        for j, ref in ((2 * i, acc_ref), (2 * i + 1, acc2_ref)):
+            where = slot_ref[step * chunk + j]
+            ref[where] += in_ref[j].astype(F32)
         return carry
 
-    lax.fori_loop(0, chunk, body, 0, unroll=8)
+    lax.fori_loop(0, chunk // 2, body, 0, unroll=8)
 
     @pl.when(step == pl.num_programs(0) - 1)
     def _():
@@ -77,7 +79,7 @@
         for half in range(2):
             low = high = jnp.zeros((chans, cols), F32)
             for at in range(min(cols, count - half * cols)):
-                piece = acc_ref[half * cols + at]
+                piece = acc_ref[half * cols + at] + acc2_ref[half * cols + at]
                 out_ref[half * cols + at] = piece.astype(BF)
                 low, high = edge_columns(piece, lane, at, low, high)
             low_ref[:, half * cols : (half + 1) * cols] = low.astype(BF)
@@ -98,7 +100,7 @@
                 pl.BlockSpec((fields, 2 * length), lambda i, p: (0, 0)),
                 pl.BlockSpec((fields, 2 * length), lambda i, p: (0, 0)),
             ],
-            scratch_shapes=[pltpu.VMEM((count + 1, fields, length), F32)],
+            scratch_shapes=[pltpu.VMEM((count + 1, fields, length), F32)] * 2,
         ),
         out_shape=[
             jax.ShapeDtypeStruct((count, fields, length), BF),
@@ -418,6 +420,7 @@
     per = len(messages)
     faces, (chans, cols) = up_ref.shape[0] - 1, up_ref.shape[1:]
     span = rows + 2
+    kind = F32 if chans % 16 else BF
     first_band, first_tile = s_ref[BAND] == 0, s_ref[TILE] == 0
     lane = lax.broadcasted_iota(jnp.int32, (chans, cols), 1)
     top_edge = jnp.zeros((chans, cols), F32)
@@ -448,11 +451,11 @@
     def _():
         ends = side_by_side(pick2(first_band, up_ref[faces], bot_ref[faces]), pick2(first_band, top_ref[faces], down_ref[faces]))
         for g in range(4):
-            pieces = [jnp.zeros((chans, cols), F32) for _ in range(per)]
+            pieces = [jnp.zeros((chans, cols), kind) for _ in range(per)]
             for i in range(6):
                 pair, f = divmod(6 * g + i, faces)
                 line = pick2(first_band, up_ref[f], bot_ref[f]) if pair == 0 else pick2(first_band, top_ref[f], down_ref[f])
-                line = line.astype(F32)
+                line = line.astype(kind)
                 for j in range(per):
                     low = i * span + (1 if j == 0 else 0)
                     high = i * span + span - (1 if j == per - 1 else 0)
@@ -460,7 +463,7 @@
                     pieces[j] = jnp.where((lane >= low) & (lane < high), value, pieces[j])
             where = slice(g * cols, (g + 1) * cols)
             for j in (0, per - 1):
-                pieces[j] = pieces[j] + move(ends, ue_ref[0 if j == 0 else 1, :, where])
+                pieces[j] = pieces[j] + move(ends, ue_ref[0 if j == 0 else 1, :, where]).astype(kind)
             for j in range(per):
 
                 @pl.when(s_ref[SENDS + j] == 1)
@@ -483,6 +486,7 @@
     per = rounds - 1
     span = rows + 2
     first_band = s_ref[BAND] == 0
+    kind = F32 if chans % 16 else BF
     lane = lax.broadcasted_iota(jnp.int32, (chans, cols), 1)
     for r in range(rounds):
 
@@ -531,16 +535,16 @@
             def _(f=f, side=side, face=face):
                 group = pl.ds(pl.multiple_of(((side - 2) * 2 + face // 6) * cols, cols), cols)
                 q = lax.rem(face, 6) * span
-                line = jnp.zeros((chans, cols), F32)
+                line = jnp.zeros((chans, cols), kind)
                 ends = corner_ref[...]
                 for j in range(per):
-                    value = units[j][:, group].astype(F32)
+                    value = units[j][:, group].astype(kind)
                     line = jnp.where(lane // rows == j, pltpu.roll(value, lax.rem(rows * j + 2 * cols - 1 - q, cols), 1), line)
                     if j == 0:
-                        ends = jnp.where(lane == 2 * f, pltpu.roll(value, lax.rem(2 * f + 2 * cols - q, cols), 1), ends)
+                        ends = jnp.where(lane == 2 * f, pltpu.roll(value.astype(F32), lax.rem(2 * f + 2 * cols - q, cols), 1), ends)
                     if j == per - 1:
                         shift = lax.rem(2 * f + 1 + 2 * cols - q - (span - 1), cols)
-                        ends = jnp.where(lane == 2 * f + 1, pltpu.roll(value, shift, 1), ends)
+                        ends = jnp.where(lane == 2 * f + 1, pltpu.roll(value.astype(F32), shift, 1), ends)
                 srow_ref[f] = line.astype(BF)
                 corner_ref[...] = ends
 
@@ -653,13 +657,11 @@
     order = jnp.arange(items)
     same = (target[:, None] == target[None, :]) & (order[None, :] < order[:, None])
     position = target * capacity + jnp.sum(same.astype(jnp.int32), axis=1)
-    base = 1 << slots_dev.bit_length()
-    codes = lax.all_gather(target * base + dest_block.reshape(items), AXES)
-    mine = codes // base == lax.axis_index(AXES)
-    earlier = jnp.asarray(np.triu(np.ones((items, items), np.float32), 1), BF)
-    rank = jnp.dot(mine.astype(BF), earlier, preferred_element_type=F32).astype(jnp.int32)
-    hit = mine[:, None, :] & (rank[:, None, :] == jnp.arange(capacity)[None, :, None])
-    slots = slots_dev + jnp.sum(jnp.where(hit, (codes % base - slots_dev)[:, None, :], 0), axis=2)
+    hit = position[:, None] == jnp.arange(total)[None, :]
+    out_slots = slots_dev + jnp.sum(
+        jnp.where(hit, (dest_block.reshape(items) - slots_dev)[:, None], 0), axis=0
+    )
+    slots = lax.all_to_all(out_slots.reshape(devices, capacity), AXES, split_axis=0, concat_axis=0, tiled=True)
     outgoing = regrid(source, regrid_weights, position, total)
     arrived = lax.all_to_all(
         outgoing.reshape(devices, capacity, fields, block_len), AXES, split_axis=0, concat_axis=0, tiled=True

time: 364 us -> 329 us (0.904)
  blocking collectives: 134 us -> 0 us
  waiting for transfers between devices: 31.6 us -> 121 us
  starting transfers between devices: 92.1 us -> 102 us
    all_gather x1 -> x0, blocking collectives: 134 us -> none  [local(): codes = lax.all_gather(target * base + dest_block.reshape(items), AXES)]
    all_to_all x1, waiting for transfers between devices: 0.01 us -> 89.8 us  [local(): lax.all_to_all(outgoing.reshape(devices, capacity, fields, block_len), AX...]
    all_to_all x0 -> x1, starting transfers between devices: none -> 11.1 us  [local(): lax.all_to_all(out_slots.reshape(devices, capacity), AXES, split_axis=0,...]
    unnamed x106 -> x101, local copies, waits for them, and re-layouts: 11.1 us -> 11 us
  transfers between devices with their start and end apart: 31 -> 32, of which waited for: 12 -> 13; matrix products, arithmetic and copies ran while one was open for 3% -> 3% of each run, Pallas kernels for 0% -> 3%
where the time goes in v2:
time: 329 us; the launch traced here: 327 us
  waiting for transfers between devices  121 us (37%)
  starting transfers between devices  102 us (31%)
  Pallas kernels  81.4 us (25%)
  local copies, waits for them, and re-layouts  17.2 us (5%)
  other arithmetic  4.75 us (1%)
    all_to_all x1, waiting for transfers between devices, local(): lax.all_to_all(outgoing.reshape(devices, capacity, fields, block_len), AX...  89.8 us
    pallas_call x2, Pallas kernels, conv(): pl.pallas_call(functools.partial(conv_kernel, last=last), grid=(face_coun...  32.3 us
    ppermute x18, starting transfers between devices, exchange(): lax.ppermute(m, AXES, pairs)  29.5 us
    ppermute x2, starting transfers between devices, exchange(): rrow = lax.ppermute(srow, AXES, plan.flip_row)  27.8 us
    pallas_call x6, Pallas kernels, whole(): pl.pallas_call(kernel, in_specs=[pl.BlockSpec(memory_space=pltpu.SMEM)] +...  23.9 us
    all_to_all x1, starting transfers between devices, local(): lax.all_to_all(out_slots.reshape(devices, capacity), AXES, split_axis=0,...  11.1 us
    unnamed x101, local copies, waits for them, and re-layouts  11 us
    ppermute x18, waiting for transfers between devices, exchange(): lax.ppermute(m, AXES, pairs)  10.9 us
  transfers between devices with their start and end apart: 32, of which 13 were waited for; matrix products, arithmetic and copies ran while one was open for 3% of the time, Pallas kernels for 3%

profile of v2, /device:TPU:0, one launch (start us, length us, event | category | flops | bytes accessed | tf_op | source)
XLA Modules:
  0.0 327.3 jit_solution(15381116904766190724)
XLA Ops:
  2.9 11.1 %all-to-all-start = ((s32[128,1,6]{2,1,0:T(1,128)}), s32[128,1,6]{2,1,0:T(1,128)S(1)}, u32[]{:S(2)}, u32[]{:S(2)}) async-start(s32[128,1,6]{2,1,0:T(1,128)} %bitcast.14), calls=%async_computation | async-start | bytes 131072 | tf_op jit(solution)/shard_map/all_to_all | solution.py:664
  14.1 10.5 %shard_map.280 = bf16[768,40,128]{2,1,0:T(8,128)(2,1)} custom-call(s32[256]{0:T(256)} %copy-done.37, bf16[40,8192]{1,0:T(8,128)(2,1)} %src_ref.1, bf16[64,4,128,128]{3,2,1,0:T(8,128)(2,1)} %w_ref.1), custom_call_target="tpu_custom_call" | custom-call | flops 335544320 | bytes 17000000 | tf_op jit(solution)/shard_map/pallas_call | solution.py:32
  24.7 10.2 %all-to-all-start.1 = ((bf16[128,6,40,128]{3,2,1,0:T(8,128)(2,1)}), bf16[128,6,40,128]{3,2,1,0:T(8,128)(2,1)}, u32[]{:S(2)}, u32[]{:S(2)}) async-start(bf16[128,6,40,128]{3,2,1,0:T(8,128)(2,1)} %bitcast.50), calls=%async_computation.1 | async-start | bytes 15728640 | tf_op jit(solution)/shard_map/all_to_all | solution.py:666
  39.4 89.8 %all-to-all-done.1 = bf16[128,6,40,128]{3,2,1,0:T(8,128)(2,1)} async-done(((bf16[128,6,40,128]{3,2,1,0:T(8,128)(2,1)}), bf16[128,6,40,128]{3,2,1,0:T(8,128)(2,1)}, u32[]{:S(2)}, u32[]{:S(2)}) %all-to-all-start.1) | async-done | bytes 7864352 | tf_op jit(solution)/shard_map/all_to_all | solution.py:666
  129.2 10.4 %shard_map.281 = (bf16[192,40,128]{2,1,0:T(8,128)(2,1)}, bf16[40,256]{1,0:T(8,128)(2,1)}, bf16[40,256]{1,0:T(8,128)(2,1)}) custom-call(s32[768]{0:T(1024)} %reshape.110.slot_ref, bf16[768,40,128]{2,1,0:T(8,128)(2,1)} %bitcast.16.in_ref), custom_call_target="tpu_custom_call" | custom-call | tf_op jit(solution)/shard_map/pallas_call | solution.py:92
  139.5 3.2 collective-permute-start.1
  145.3 2.0 shard_map.282
  147.3 5.1 %collective-permute-start.3 = (bf16[13,40,128]{2,1,0:T(8,128)(2,1)}, bf16[13,40,128]{2,1,0:T(8,128)(2,1)S(1)}, u32[]{:S(2)}, u32[]{:S(2)}) collective-permute-start(bf16[13,40,128]{2,1,0:T(8,128)(2,1)} %get-tuple-element.50.up_ref.refs_12_), channel_id=1, source_target_pairs={{4,0},{8,4},{12,8},{16,12},{20,16},{24,20},{28,24},{32,28},{36,32}... | collective-permute-start | bytes 399368 | tf_op jit(solution)/shard_map/ppermute | solution.py:600
  152.4 2.9 collective-permute-done.2.top_ref.refs_14_
  156.5 3.8 %shard_map.283 = (bf16[40,512]{1,0:T(8,128)(2,1)}, bf16[40,512]{1,0:T(8,128)(2,1)}, bf16[40,512]{1,0:T(8,128)(2,1)}, bf16[40,512]{1,0:T(8,128)(2,1)}, bf16[40,51...) custom-call(s32[54]{0:T(128)} %concatenate.17.s_ref, ...), custom_call_target="tpu_custom_call" | custom-call | tf_op jit(solution)/shard_map/pallas_call | solution.py:367
  162.2 1.9 collective-permute-start.11
  164.8 1.9 collective-permute-start.5
  168.1 1.9 collective-permute-start.6
  176.0 3.6 %collective-permute-done.8.refs_4_ = bf16[40,512]{1,0:T(8,128)(2,1)S(1)} collective-permute-done((bf16[40,512]{1,0:T(8,128)(2,1)}, bf16[40,512]{1,0:T(8,128)(2,1)S(1)}, u32[]{:S(2)}, u32[]{:S(2)}) %collective-permute-start.8) | collective-permute-done | bytes 40992 | tf_op jit(solution)/shard_map/ppermute | solution.py:608
  181.6 3.7 %shard_map.284 = (bf16[13,40,128]{2,1,0:T(8,128)(2,1)}, bf16[40,256]{1,0:T(8,128)(2,1)}) custom-call(s32[54]{0:T(128)} %concatenate.17.s_ref, bf16[40,512]{1,0:T(8,128)(2,1)} %copy-done.28, bf16[40,512]{1,0:T(8,128)(2,1)} %copy-done.29, bf16[40,512]{1,0:T(8,128)(2,1)} %copy-done.30, bf16[40,512]{1,0:T(8,128)(2,1)} %copy-done.31, bf16[40,512]{1,0:T(8,128)(2,1)} %copy-done.32, ...), custom_call_target="tpu_custom_call" | custom-call | tf_op jit(solution)/shard_map/pallas_call | solution.py:367
  185.3 14.4 %collective-permute-start.13 = (bf16[13,40,128]{2,1,0:T(8,128)(2,1)}, bf16[13,40,128]{2,1,0:T(8,128)(2,1)S(1)}, u32[]{:S(2)}, u32[]{:S(2)}) collective-permute-start(bf16[13,40,128]{2,1,0:T(8,128)(2,1)} %get-tuple-element.62.srow_ref), channel_id=1, source_target_pairs={{0,3},{1,2},{2,1},{3,0},{124,127},{125,126},{126,125},{127,124}} | collective-permute-start | bytes 399368 | tf_op jit(solution)/shard_map/ppermute | solution.py:622
  203.5 4.9 %collective-permute-done.14.rcol_ref = bf16[40,256]{1,0:T(8,128)(2,1)S(1)} collective-permute-done((bf16[40,256]{1,0:T(8,128)(2,1)}, bf16[40,256]{1,0:T(8,128)(2,1)S(1)}, u32[]{:S(2)}, u32[]{:S(2)}) %collective-permute-start.14) | collective-permute-done | bytes 20512 | tf_op jit(solution)/shard_map/ppermute | solution.py:623
  209.7 2.8 shard_map.285
  212.4 13.6 %shard_map.286 = (bf16[12,16,128,128]{3,2,1,0:T(8,128)(2,1)}, bf16[128,256]{1,0:T(8,128)(2,1)}, bf16[128,256]{1,0:T(8,128)(2,1)}) custom-call(bf16[256,512]{1,0:T(8,128)(2,1)} %bitcast.57, f32[256,1]{1,0:T(8,128)} %copy.54.b_ref, bf16[12,16,40,128]{3,2,1,0:T(8,128)(2,1)} %bitcast.53, bf16[12,40,128]{2,1,0:T(8,128)(2,1)} %get-tuple-element.64.top_ref, ...), custom_call_target="tpu_custom_call" | custom-call | tf_op jit(solution)/shard_map/pallas_call | solution.py:211
  226.1 3.2 collective-permute-start.16
  229.3 2.4 collective-permute-done.15.left_ref
  232.4 2.4 shard_map.287
  234.7 5.1 %collective-permute-start.18 = (bf16[13,128,128]{2,1,0:T(8,128)(2,1)}, bf16[13,128,128]{2,1,0:T(8,128)(2,1)S(1)}, u32[]{:S(2)}, u32[]{:S(2)}) collective-permute-start(bf16[13,128,128]{2,1,0:T(8,128)(2,1)} %get-tuple-element.71.up_ref.refs_12_), channel_id=1, source_target_pairs={{4,0},{8,4},{12,8},{16,12},{20,16},{24,20},{28,24},{32,28},{36,32}... | collective-permute-start | bytes 1277960 | tf_op jit(solution)/shard_map/ppermute | solution.py:600
  239.8 6.0 %collective-permute-done.17.top_ref.refs_14_ = bf16[13,128,128]{2,1,0:T(8,128)(2,1)S(1)} collective-permute-done((bf16[13,128,128]{2,1,0:T(8,128)(2,1)}, bf16[13,128,128]{2,1,0:T(8,128)(2,1)S(1)}, u32[]{:S(2)}, u32[]{:S(2)}) %collective-permute-start.17) | collective-permute-done | bytes 426016 | tf_op jit(solution)/shard_map/ppermute | solution.py:599
  247.5 5.7 %shard_map.288 = (bf16[128,512]{1,0:T(8,128)(2,1)}, bf16[128,512]{1,0:T(8,128)(2,1)}, bf16[128,512]{1,0:T(8,128)(2,1)}, bf16[128,512]{1,0:T(8,128)(2,1)}, bf16[1...) custom-call(s32[54]{0:T(128)} %concatenate.17.s_ref, ...), custom_call_target="tpu_custom_call" | custom-call | tf_op jit(solution)/shard_map/pallas_call | solution.py:367
  270.2 2.2 collective-permute-done.25.refs_6_
  274.6 4.9 %shard_map.289 = (bf16[13,128,128]{2,1,0:T(8,128)(2,1)}, bf16[128,256]{1,0:T(8,128)(2,1)}) custom-call(s32[54]{0:T(128)} %concatenate.17.s_ref, bf16[128,512]{1,0:T(8,128)(2,1)} %copy-done.13, bf16[128,512]{1,0:T(8,128)(2,1)} %copy-done.14, bf16[128,512]{1,0:T(8,128)(2,1)} %copy-done.15, bf16[128,512]{1,0:T(8,128)(2,1)} %copy-done.16, ...), custom_call_target="tpu_custom_call" | custom-call | tf_op jit(solution)/shard_map/pallas_call | solution.py:367
  279.5 13.3 %collective-permute-start.28 = (bf16[13,128,128]{2,1,0:T(8,128)(2,1)}, bf16[13,128,128]{2,1,0:T(8,128)(2,1)S(1)}, u32[]{:S(2)}, u32[]{:S(2)}) collective-permute-start(bf16[13,128,128]{2,1,0:T(8,128)(2,1)} %get-tuple-element.83.srow_ref), channel_id=1, source_target_pairs={{0,3},{1,2},{2,1},{3,0},{124,127},{125,126},{126,125},{127,124}} | collective-permute-start | bytes 1277960 | tf_op jit(solution)/shard_map/ppermute | solution.py:622
  294.9 5.2 %collective-permute-start.29 = (bf16[128,256]{1,0:T(8,128)(2,1)}, bf16[128,256]{1,0:T(8,128)(2,1)S(1)}, u32[]{:S(2)}, u32[]{:S(2)}) collective-permute-start(bf16[128,256]{1,0:T(8,128)(2,1)} %get-tuple-element.84.scol_ref), channel_id=1, source_target_pairs={{0,124},{3,127},{4,120},{7,123},{8,116},{11,119},{12,112},{15,115}... | collective-permute-start | bytes 196616 | tf_op jit(solution)/shard_map/ppermute | solution.py:623
  300.9 3.1 collective-permute-done.29.rcol_ref
  305.4 3.2 shard_map.290
  308.6 18.7 %shard_map.291 = bf16[128,12,16,128]{3,2,1,0:T(8,128)(2,1)} custom-call(bf16[256,1536]{1,0:T(8,128)(2,1)} %bitcast.54, f32[256,1]{1,0:T(8,128)} %copy.55.b_ref, bf16[12,16,128,128]{3,2,1,0:T(8,128)(2,1)} %get-tuple-element.68.first_ref.last_ref.x_ref, bf16[12,128,128]{2,1,0:T(8,128)(2,1)} %get-tuple-element.85.top_ref, ...), custom_call_target="tpu_custom_call" | custom-call | tf_op jit(solution)/shard_map/pallas_call | solution.py:211
  (187 shorter events, 53.3 us)
Async XLA Ops:
  2.9 21.7 %all-to-all-start = ((s32[128,1,6]{2,1,0:T(1,128)}), s32[128,1,6]{2,1,0:T(1,128)S(1)}, u32[]{:S(2)}, u32[]{:S(2)}) async-start(s32[128,1,6]{2,1,0:T(1,128)} %bitcast.14), calls=%async_computation | async-start | bytes 131072 | tf_op jit(solution)/shard_map/all_to_all | solution.py:664
  24.7 104.4 %all-to-all-start.1 = ((bf16[128,6,40,128]{3,2,1,0:T(8,128)(2,1)}), bf16[128,6,40,128]{3,2,1,0:T(8,128)(2,1)}, u32[]{:S(2)}, u32[]{:S(2)}) async-start(bf16[128,6,40,128]{3,2,1,0:T(8,128)(2,1)} %bitcast.50), calls=%async_computation.1 | async-start | bytes 15728640 | tf_op jit(solution)/shard_map/all_to_all | solution.py:666
  139.5 5.2 %collective-permute-start = (bf16[40,256]{1,0:T(8,128)(2,1)}, bf16[40,256]{1,0:T(8,128)(2,1)S(1)}, u32[]{:S(2)}, u32[]{:S(2)}) collective-permute-start(bf16[40,256]{1,0:T(8,128)(2,1)} %get-tuple-element.48.high_ref), channel_id=1, source_target_pairs={{0,1},{1,2},{2,3},{3,0},{4,5},{5,6},{6,7},{7,4},{8,9},{9,10},{10,1... | collective-permute-start | bytes 61448 | tf_op jit(solution)/shard_map/ppermute | solution.py:595
  139.5 5.2 %collective-permute-start.1 = (bf16[40,256]{1,0:T(8,128)(2,1)}, bf16[40,256]{1,0:T(8,128)(2,1)S(1)}, u32[]{:S(2)}, u32[]{:S(2)}) collective-permute-start(bf16[40,256]{1,0:T(8,128)(2,1)} %get-tuple-element.49.low_ref), channel_id=1, source_target_pairs={{1,0},{2,1},{3,2},{0,3},{5,4},{6,5},{7,6},{4,7},{9,8},{10,9},{11,1... | collective-permute-start | bytes 61448 | tf_op jit(solution)/shard_map/ppermute | solution.py:596
  147.3 7.9 %collective-permute-start.2 = (bf16[13,40,128]{2,1,0:T(8,128)(2,1)}, bf16[13,40,128]{2,1,0:T(8,128)(2,1)S(1)}, u32[]{:S(2)}, u32[]{:S(2)}) collective-permute-start(bf16[13,40,128]{2,1,0:T(8,128)(2,1)} %get-tuple-element.51.down_ref.refs_13_), channel_id=1, source_target_pairs={{0,4},{4,8},{8,12},{12,16},{16,20},{20,24},{24,28},{28,32},{32,36}... | collective-permute-start | bytes 399368 | tf_op jit(solution)/shard_map/ppermute | solution.py:599
  147.3 7.9 %collective-permute-start.3 = (bf16[13,40,128]{2,1,0:T(8,128)(2,1)}, bf16[13,40,128]{2,1,0:T(8,128)(2,1)S(1)}, u32[]{:S(2)}, u32[]{:S(2)}) collective-permute-start(bf16[13,40,128]{2,1,0:T(8,128)(2,1)} %get-tuple-element.50.up_ref.refs_12_), channel_id=1, source_target_pairs={{4,0},{8,4},{12,8},{16,12},{20,16},{24,20},{28,24},{32,28},{36,32}... | collective-permute-start | bytes 399368 | tf_op jit(solution)/shard_map/ppermute | solution.py:600
  160.3 7.8 %collective-permute-start.10 = (bf16[40,512]{1,0:T(8,128)(2,1)}, bf16[40,512]{1,0:T(8,128)(2,1)S(1)}, u32[]{:S(2)}, u32[]{:S(2)}) collective-permute-start(bf16[40,512]{1,0:T(8,128)(2,1)} %get-tuple-element.58), channel_id=1, source_target_pairs={{0,24},{24,0},{124,27},{27,124},{1,56},{56,1},{125,59},{59,125},{2... | collective-permute-start | bytes 122888 | tf_op jit(solution)/shard_map/ppermute | solution.py:608
  162.2 7.8 %collective-permute-start.11 = (bf16[40,512]{1,0:T(8,128)(2,1)}, bf16[40,512]{1,0:T(8,128)(2,1)S(1)}, u32[]{:S(2)}, u32[]{:S(2)}) collective-permute-start(bf16[40,512]{1,0:T(8,128)(2,1)} %get-tuple-element.59.refs_10_), channel_id=1, source_target_pairs={{0,28},{28,0},{124,31},{31,124},{1,60},{60,1},{125,63},{63,125},{2... | collective-permute-start | bytes 122888 | tf_op jit(solution)/shard_map/ppermute | solution.py:608
  164.2 7.8 %collective-permute-start.4 = (bf16[40,512]{1,0:T(8,128)(2,1)}, bf16[40,512]{1,0:T(8,128)(2,1)S(1)}, u32[]{:S(2)}, u32[]{:S(2)}) collective-permute-start(bf16[40,512]{1,0:T(8,128)(2,1)} %get-tuple-element.52.refs_9_), channel_id=1, source_target_pairs={{1,32},{32,1},{125,35},{35,125},{2,64},{64,2},{126,67},{67,126},{3... | collective-permute-start | bytes 122888 | tf_op jit(solution)/shard_map/ppermute | solution.py:608
  164.8 9.1 %collective-permute-start.5 = (bf16[40,512]{1,0:T(8,128)(2,1)}, bf16[40,512]{1,0:T(8,128)(2,1)S(1)}, u32[]{:S(2)}, u32[]{:S(2)}) collective-permute-start(bf16[40,512]{1,0:T(8,128)(2,1)} %get-tuple-element.53), channel_id=1, source_target_pairs={{0,4},{4,0},{124,7},{7,124},{1,36},{36,1},{125,39},{39,125},{2,68}... | collective-permute-start | bytes 122888 | tf_op jit(solution)/shard_map/ppermute | solution.py:608
  167.4 13.6 %collective-permute-start.12 = (bf16[40,1024]{1,0:T(8,128)(2,1)}, bf16[40,1024]{1,0:T(8,128)(2,1)S(1)}, u32[]{:S(2)}, u32[]{:S(2)}) collective-permute-start(bf16[40,1024]{1,0:T(8,128)(2,1)} %get-tuple-element.60), channel_id=1, source_target_pairs={{3,124},{124,3}} | collective-permute-start | bytes 245768 | tf_op jit(solution)/shard_map/ppermute | solution.py:608
  168.1 7.8 %collective-permute-start.6 = (bf16[40,512]{1,0:T(8,128)(2,1)}, bf16[40,512]{1,0:T(8,128)(2,1)S(1)}, u32[]{:S(2)}, u32[]{:S(2)}) collective-permute-start(bf16[40,512]{1,0:T(8,128)(2,1)} %get-tuple-element.54), channel_id=1, source_target_pairs={{0,8},{8,0},{124,11},{11,124},{1,40},{40,1},{125,43},{43,125},{2,7... | collective-permute-start | bytes 122888 | tf_op jit(solution)/shard_map/ppermute | solution.py:608
  170.1 5.9 %collective-permute-start.7 = (bf16[40,512]{1,0:T(8,128)(2,1)}, bf16[40,512]{1,0:T(8,128)(2,1)S(1)}, u32[]{:S(2)}, u32[]{:S(2)}) collective-permute-start(bf16[40,512]{1,0:T(8,128)(2,1)} %get-tuple-element.55), channel_id=1, source_target_pairs={{0,12},{12,0},{124,15},{15,124},{1,44},{44,1},{125,47},{47,125},{2... | collective-permute-start | bytes 122888 | tf_op jit(solution)/shard_map/ppermute | solution.py:608
  172.0 7.6 %collective-permute-start.8 = (bf16[40,512]{1,0:T(8,128)(2,1)}, bf16[40,512]{1,0:T(8,128)(2,1)S(1)}, u32[]{:S(2)}, u32[]{:S(2)}) collective-permute-start(bf16[40,512]{1,0:T(8,128)(2,1)} %get-tuple-element.56), channel_id=1, source_target_pairs={{0,16},{16,0},{124,19},{19,124},{1,48},{48,1},{125,51},{51,125},{2... | collective-permute-start | bytes 122888 | tf_op jit(solution)/shard_map/ppermute | solution.py:608
  174.0 7.0 %collective-permute-start.9 = (bf16[40,512]{1,0:T(8,128)(2,1)}, bf16[40,512]{1,0:T(8,128)(2,1)S(1)}, u32[]{:S(2)}, u32[]{:S(2)}) collective-permute-start(bf16[40,512]{1,0:T(8,128)(2,1)} %get-tuple-element.57), channel_id=1, source_target_pairs={{0,20},{20,0},{124,23},{23,124},{1,52},{52,1},{125,55},{55,125},{2... | collective-permute-start | bytes 122888 | tf_op jit(solution)/shard_map/ppermute | solution.py:608
  185.3 23.1 %collective-permute-start.13 = (bf16[13,40,128]{2,1,0:T(8,128)(2,1)}, bf16[13,40,128]{2,1,0:T(8,128)(2,1)S(1)}, u32[]{:S(2)}, u32[]{:S(2)}) collective-permute-start(bf16[13,40,128]{2,1,0:T(8,128)(2,1)} %get-tuple-element.62.srow_ref), channel_id=1, source_target_pairs={{0,3},{1,2},{2,1},{3,0},{124,127},{125,126},{126,125},{127,124}} | collective-permute-start | bytes 399368 | tf_op jit(solution)/shard_map/ppermute | solution.py:622
  199.8 8.6 %collective-permute-start.14 = (bf16[40,256]{1,0:T(8,128)(2,1)}, bf16[40,256]{1,0:T(8,128)(2,1)S(1)}, u32[]{:S(2)}, u32[]{:S(2)}) collective-permute-start(bf16[40,256]{1,0:T(8,128)(2,1)} %get-tuple-element.63.scol_ref), channel_id=1, source_target_pairs={{0,124},{3,127},{4,120},{7,123},{8,116},{11,119},{12,112},{15,115}... | collective-permute-start | bytes 61448 | tf_op jit(solution)/shard_map/ppermute | solution.py:623
  226.0 5.7 %collective-permute-start.15 = (bf16[128,256]{1,0:T(8,128)(2,1)}, bf16[128,256]{1,0:T(8,128)(2,1)S(1)}, u32[]{:S(2)}, u32[]{:S(2)}) collective-permute-start(bf16[128,256]{1,0:T(8,128)(2,1)} %get-tuple-element.69.high_ref), channel_id=1, source_target_pairs={{0,1},{1,2},{2,3},{3,0},{4,5},{5,6},{6,7},{7,4},{8,9},{9,10},{10,1... | collective-permute-start | bytes 196616 | tf_op jit(solution)/shard_map/ppermute | solution.py:595
  226.1 5.7 %collective-permute-start.16 = (bf16[128,256]{1,0:T(8,128)(2,1)}, bf16[128,256]{1,0:T(8,128)(2,1)S(1)}, u32[]{:S(2)}, u32[]{:S(2)}) collective-permute-start(bf16[128,256]{1,0:T(8,128)(2,1)} %get-tuple-element.70.low_ref), channel_id=1, source_target_pairs={{1,0},{2,1},{3,2},{0,3},{5,4},{6,5},{7,6},{4,7},{9,8},{10,9},{11,1... | collective-permute-start | bytes 196616 | tf_op jit(solution)/shard_map/ppermute | solution.py:596
  234.7 11.1 %collective-permute-start.17 = (bf16[13,128,128]{2,1,0:T(8,128)(2,1)}, bf16[13,128,128]{2,1,0:T(8,128)(2,1)S(1)}, u32[]{:S(2)}, u32[]{:S(2)}) collective-permute-start(bf16[13,128,128]{2,1,0:T(8,128)(2,1)} %get-tuple-element.72.down_ref.refs_13_), channel_id=1, source_target_pairs={{0,4},{4,8},{8,12},{12,16},{16,20},{20,24},{24,28},{28,32},{32,36}... | collective-permute-start | bytes 1277960 | tf_op jit(solution)/shard_map/ppermute | solution.py:599
  234.7 11.1 %collective-permute-start.18 = (bf16[13,128,128]{2,1,0:T(8,128)(2,1)}, bf16[13,128,128]{2,1,0:T(8,128)(2,1)S(1)}, u32[]{:S(2)}, u32[]{:S(2)}) collective-permute-start(bf16[13,128,128]{2,1,0:T(8,128)(2,1)} %get-tuple-element.71.up_ref.refs_12_), channel_id=1, source_target_pairs={{4,0},{8,4},{12,8},{16,12},{20,16},{24,20},{28,24},{32,28},{36,32}... | collective-permute-start | bytes 1277960 | tf_op jit(solution)/shard_map/ppermute | solution.py:600
  253.1 7.1 %collective-permute-start.19 = (bf16[128,512]{1,0:T(8,128)(2,1)}, bf16[128,512]{1,0:T(8,128)(2,1)S(1)}, u32[]{:S(2)}, u32[]{:S(2)}) collective-permute-start(bf16[128,512]{1,0:T(8,128)(2,1)} %get-tuple-element.73.refs_9_), channel_id=1, source_target_pairs={{1,32},{32,1},{125,35},{35,125},{2,64},{64,2},{126,67},{67,126},{3... | collective-permute-start | bytes 393224 | tf_op jit(solution)/shard_map/ppermute | solution.py:608
  253.8 8.4 %collective-permute-start.20 = (bf16[128,512]{1,0:T(8,128)(2,1)}, bf16[128,512]{1,0:T(8,128)(2,1)S(1)}, u32[]{:S(2)}, u32[]{:S(2)}) collective-permute-start(bf16[128,512]{1,0:T(8,128)(2,1)} %get-tuple-element.74), channel_id=1, source_target_pairs={{0,4},{4,0},{124,7},{7,124},{1,36},{36,1},{125,39},{39,125},{2,68}... | collective-permute-start | bytes 393224 | tf_op jit(solution)/shard_map/ppermute | solution.py:608
  255.7 8.4 %collective-permute-start.21 = (bf16[128,512]{1,0:T(8,128)(2,1)}, bf16[128,512]{1,0:T(8,128)(2,1)S(1)}, u32[]{:S(2)}, u32[]{:S(2)}) collective-permute-start(bf16[128,512]{1,0:T(8,128)(2,1)} %get-tuple-element.75), channel_id=1, source_target_pairs={{0,8},{8,0},{124,11},{11,124},{1,40},{40,1},{125,43},{43,125},{2,7... | collective-permute-start | bytes 393224 | tf_op jit(solution)/shard_map/ppermute | solution.py:608
  257.6 8.5 %collective-permute-start.22 = (bf16[128,512]{1,0:T(8,128)(2,1)}, bf16[128,512]{1,0:T(8,128)(2,1)S(1)}, u32[]{:S(2)}, u32[]{:S(2)}) collective-permute-start(bf16[128,512]{1,0:T(8,128)(2,1)} %get-tuple-element.76), channel_id=1, source_target_pairs={{0,12},{12,0},{124,15},{15,124},{1,44},{44,1},{125,47},{47,125},{2... | collective-permute-start | bytes 393224 | tf_op jit(solution)/shard_map/ppermute | solution.py:608
  259.6 14.3 %collective-permute-start.27 = (bf16[128,1024]{1,0:T(8,128)(2,1)}, bf16[128,1024]{1,0:T(8,128)(2,1)S(1)}, u32[]{:S(2)}, u32[]{:S(2)}) collective-permute-start(bf16[128,1024]{1,0:T(8,128)(2,1)} %get-tuple-element.81), channel_id=1, source_target_pairs={{3,124},{124,3}} | collective-permute-start | bytes 786440 | tf_op jit(solution)/shard_map/ppermute | solution.py:608
  260.3 8.6 %collective-permute-start.23 = (bf16[128,512]{1,0:T(8,128)(2,1)}, bf16[128,512]{1,0:T(8,128)(2,1)S(1)}, u32[]{:S(2)}, u32[]{:S(2)}) collective-permute-start(bf16[128,512]{1,0:T(8,128)(2,1)} %get-tuple-element.77), channel_id=1, source_target_pairs={{0,16},{16,0},{124,19},{19,124},{1,48},{48,1},{125,51},{51,125},{2... | collective-permute-start | bytes 393224 | tf_op jit(solution)/shard_map/ppermute | solution.py:608
  262.2 8.0 %collective-permute-start.24 = (bf16[128,512]{1,0:T(8,128)(2,1)}, bf16[128,512]{1,0:T(8,128)(2,1)S(1)}, u32[]{:S(2)}, u32[]{:S(2)}) collective-permute-start(bf16[128,512]{1,0:T(8,128)(2,1)} %get-tuple-element.78), channel_id=1, source_target_pairs={{0,20},{20,0},{124,23},{23,124},{1,52},{52,1},{125,55},{55,125},{2... | collective-permute-start | bytes 393224 | tf_op jit(solution)/shard_map/ppermute | solution.py:608
  264.2 8.3 %collective-permute-start.25 = (bf16[128,512]{1,0:T(8,128)(2,1)}, bf16[128,512]{1,0:T(8,128)(2,1)S(1)}, u32[]{:S(2)}, u32[]{:S(2)}) collective-permute-start(bf16[128,512]{1,0:T(8,128)(2,1)} %get-tuple-element.79), channel_id=1, source_target_pairs={{0,24},{24,0},{124,27},{27,124},{1,56},{56,1},{125,59},{59,125},{2... | collective-permute-start | bytes 393224 | tf_op jit(solution)/shard_map/ppermute | solution.py:608
  266.1 7.7 %collective-permute-start.26 = (bf16[128,512]{1,0:T(8,128)(2,1)}, bf16[128,512]{1,0:T(8,128)(2,1)S(1)}, u32[]{:S(2)}, u32[]{:S(2)}) collective-permute-start(bf16[128,512]{1,0:T(8,128)(2,1)} %get-tuple-element.80.refs_10_), channel_id=1, source_target_pairs={{0,28},{28,0},{124,31},{31,124},{1,60},{60,1},{125,63},{63,125},{2... | collective-permute-start | bytes 393224 | tf_op jit(solution)/shard_map/ppermute | solution.py:608
  279.5 24.5 %collective-permute-start.28 = (bf16[13,128,128]{2,1,0:T(8,128)(2,1)}, bf16[13,128,128]{2,1,0:T(8,128)(2,1)S(1)}, u32[]{:S(2)}, u32[]{:S(2)}) collective-permute-start(bf16[13,128,128]{2,1,0:T(8,128)(2,1)} %get-tuple-element.83.srow_ref), channel_id=1, source_target_pairs={{0,3},{1,2},{2,1},{3,0},{124,127},{125,126},{126,125},{127,124}} | collective-permute-start | bytes 1277960 | tf_op jit(solution)/shard_map/ppermute | solution.py:622
  294.9 9.1 %collective-permute-start.29 = (bf16[128,256]{1,0:T(8,128)(2,1)}, bf16[128,256]{1,0:T(8,128)(2,1)S(1)}, u32[]{:S(2)}, u32[]{:S(2)}) collective-permute-start(bf16[128,256]{1,0:T(8,128)(2,1)} %get-tuple-element.84.scol_ref), channel_id=1, source_target_pairs={{0,124},{3,127},{4,120},{7,123},{8,116},{11,119},{12,112},{15,115}... | collective-permute-start | bytes 196616 | tf_op jit(solution)/shard_map/ppermute | solution.py:623
  (48 other events, 812.5 us)

commit v3 on v2

--- a/solution.py
+++ b/solution.py
@@ -248,17 +248,19 @@
         self.sends = np.zeros((rounds, count), np.int32)
         self.row_from = np.full((count, per), 2, np.int32)
         self.col_round = np.full((count,), rounds, np.int32)
+        near, far = 0, last * tiles + tiles - 1
         corners = (tiles - 1, last * tiles)
-        self.pairs[per] = [corners, corners[::-1]]
+        self.pairs[0].append((near, corners[1]))
+        self.pairs[per - 1].append((far, corners[0]))
+        self.pairs[per] = [(near, corners[0]), (far, corners[1])]
+        self.sends[per, near], self.sends[per, far] = 1, 2
 
         def join(row_dev, col_dev, j):
             if row_dev in corners and col_dev in corners:
-                self.sends[per, row_dev] = 1 if j == 0 else 2
-                self.row_from[row_dev, j] = 1
+                self.row_from[row_dev, j] = 0
                 self.col_round[col_dev] = per
-                return
-            self.sends[j, row_dev] = 1
-            if row_dev != col_dev:
+            elif row_dev != col_dev:
+                self.sends[j, row_dev] = 1
                 self.pairs[j] += [(row_dev, col_dev), (col_dev, row_dev)]
                 self.row_from[row_dev, j] = 0
                 self.col_round[col_dev] = j
@@ -416,7 +418,7 @@
 
 
 def lines_kernel(s_ref, up_ref, down_ref, top_ref, bot_ref, low_ref, high_ref, left_ref, right_ref, own_ref, wrap_ref, ue_ref, *outs, bands, rows):
-    messages, both_ref, cl_ref = outs[:-2], outs[-2], outs[-1]
+    messages, extra_ref, cl_ref = outs[:-2], outs[-2], outs[-1]
     per = len(messages)
     faces, (chans, cols) = up_ref.shape[0] - 1, up_ref.shape[1:]
     span = rows + 2
@@ -439,8 +441,7 @@
     wrap = move(side_by_side(theirs, tc, bc), wrap_ref[...]).astype(BF)
     cl_ref[...] = side_by_side(pick2(first_tile, own, wrap), pick2(first_tile, wrap, own))
     on_row = jnp.logical_or(first_band, s_ref[BAND] == bands - 1)
-    both_ref[:, : 4 * cols] = cl_ref[...]
-    both_ref[:, 4 * cols :] = jnp.zeros((chans, 4 * cols), BF)
+    extra_ref[...] = jnp.zeros_like(extra_ref)
     for m in range(per):
 
         @pl.when(s_ref[SENDS + m] == 0)
@@ -470,18 +471,17 @@
                 def _(j=j, piece=pieces[j]):
                     messages[j][:, where] = piece.astype(BF)
 
-            second = slice((4 + g) * cols, (5 + g) * cols)
             for code, j in ((1, 0), (2, per - 1)):
 
                 @pl.when(s_ref[SENDS + per] == code)
                 def _(piece=pieces[j]):
-                    both_ref[:, second] = piece.astype(BF)
+                    extra_ref[:, where] = piece.astype(BF)
 
 
 def seams_kernel(s_ref, *refs, rounds, rows, bands):
     got, refs = refs[:rounds], refs[rounds:]
-    first_msg, last_msg, cl_ref, up_ref, down_ref, top_ref, bot_ref, pick_ref, srow_ref, scol_ref = refs[:10]
-    rows_ref, unit0_ref, unit7_ref, other_ref, corner_ref = refs[10:]
+    extra_ref, cl_ref, up_ref, down_ref, top_ref, bot_ref, pick_ref, srow_ref, scol_ref = refs[:9]
+    rows_ref, unit0_ref, unit7_ref, other_ref, corner_ref = refs[9:]
     faces, (chans, cols) = up_ref.shape[0] - 1, up_ref.shape[1:]
     per = rounds - 1
     span = rows + 2
@@ -492,15 +492,11 @@
 
         @pl.when(s_ref[COL_ROUND] == r)
         def _(r=r):
-            other_ref[...] = got[r][:, got[r].shape[1] - 4 * cols :]
-
-    @pl.when((s_ref[COL_ROUND] == rounds) & first_band)
+            other_ref[...] = got[r][...]
+
+    @pl.when(s_ref[COL_ROUND] == rounds)
     def _():
-        other_ref[...] = first_msg[...]
-
-    @pl.when((s_ref[COL_ROUND] == rounds) & jnp.logical_not(first_band))
-    def _():
-        other_ref[...] = last_msg[...]
+        other_ref[...] = extra_ref[...]
 
     scol_ref[...] = move(side_by_side(other_ref[...], cl_ref[...]), pick_ref[...]).astype(BF)
 
@@ -510,11 +506,11 @@
     @pl.when(on_row)
     def _():
         for code, to, normal in ((FIRST_FROM, unit0_ref, got[0]), (LAST_FROM, unit7_ref, got[per - 1])):
-            for value, src in enumerate((normal, got[per], cl_ref)):
+            for value, src in ((0, normal), (2, cl_ref)):
 
                 @pl.when(s_ref[code] == value)
                 def _(to=to, src=src):
-                    to[...] = src[:, : 4 * cols]
+                    to[...] = src[...]
 
         for f in range(faces + 1):
             rows_ref[f] = pick2(first_band, up_ref[f], bot_ref[f])
@@ -600,7 +596,7 @@
     bottom = lax.ppermute(up, "band", [(j, i) for i, j in around])
     outs = whole(
         functools.partial(lines_kernel, bands=bands, rows=rows),
-        [(chans, 4 * cols)] * plan.per + [(chans, 8 * cols), (chans, 4 * cols)],
+        [(chans, 4 * cols)] * plan.per + [(chans, 4 * cols)] * 2,
         [],
         scalars, up, down, top, bottom, low, high, left, right, own, wrap, unit_ends,
     )
@@ -617,7 +613,7 @@
             pltpu.VMEM((chans, 4 * cols), BF),
             pltpu.VMEM((chans, cols), F32),
         ],
-        scalars, *got, messages[0], messages[plan.per - 1], col_lines, up, down, top, bottom, pick,
+        scalars, *got, messages[-1], col_lines, up, down, top, bottom, pick,
     )
     rrow = lax.ppermute(srow, AXES, plan.flip_row)
     rcol = lax.ppermute(scol, AXES, plan.flip_col)

time: 329 us -> 326 us (level)
    ppermute x18, starting transfers between devices: 29.5 us -> 43.8 us  [exchange(): lax.ppermute(m, AXES, pairs)]
    ppermute x2, starting transfers between devices: 27.8 us -> 14.2 us  [exchange(): rrow = lax.ppermute(srow, AXES, plan.flip_row)]
  transfers between devices with their start and end apart: 32 -> 32, of which waited for: 13 -> 12; matrix products, arithmetic and copies ran while one was open for 3% -> 3% of each run, Pallas kernels for 3% -> 3%
where the time goes in v3:
time: 326 us; the launch traced here: 325 us
  waiting for transfers between devices  121 us (37%)
  starting transfers between devices  99.8 us (31%)
  Pallas kernels  81.7 us (25%)
  local copies, waits for them, and re-layouts  17 us (5%)
  other arithmetic  4.74 us (1%)
    all_to_all x1, waiting for transfers between devices, local(): lax.all_to_all(outgoing.reshape(devices, capacity, fields, block_len), AX...  89.8 us
    ppermute x18, starting transfers between devices, exchange(): lax.ppermute(m, AXES, pairs)  43.8 us
    pallas_call x2, Pallas kernels, conv(): pl.pallas_call(functools.partial(conv_kernel, last=last), grid=(face_coun...  32.3 us
    pallas_call x6, Pallas kernels, whole(): pl.pallas_call(kernel, in_specs=[pl.BlockSpec(memory_space=pltpu.SMEM)] +...  24.2 us
    ppermute x2, starting transfers between devices, exchange(): rrow = lax.ppermute(srow, AXES, plan.flip_row)  14.2 us
    ppermute x2, waiting for transfers between devices, exchange(): rcol = lax.ppermute(scol, AXES, plan.flip_col)  11.3 us
    all_to_all x1, starting transfers between devices, local(): lax.all_to_all(out_slots.reshape(devices, capacity), AXES, split_axis=0,...  11.1 us
    unnamed x101, local copies, waits for them, and re-layouts  10.9 us
  transfers between devices with their start and end apart: 32, of which 12 were waited for; matrix products, arithmetic and copies ran while one was open for 3% of the time, Pallas kernels for 3%

profile of v3, /device:TPU:0, one launch (start us, length us, event | category | flops | bytes accessed | tf_op | source)
XLA Modules:
  0.0 325.1 jit_solution(9232029742051175924)
XLA Ops:
  2.9 11.1 %all-to-all-start = ((s32[128,1,6]{2,1,0:T(1,128)}), s32[128,1,6]{2,1,0:T(1,128)S(1)}, u32[]{:S(2)}, u32[]{:S(2)}) async-start(s32[128,1,6]{2,1,0:T(1,128)} %bitcast.14), calls=%async_computation | async-start | bytes 131072 | tf_op jit(solution)/shard_map/all_to_all | solution.py:660
  14.1 10.5 %shard_map.280 = bf16[768,40,128]{2,1,0:T(8,128)(2,1)} custom-call(s32[256]{0:T(256)} %copy-done.37, bf16[40,8192]{1,0:T(8,128)(2,1)} %src_ref.1, bf16[64,4,128,128]{3,2,1,0:T(8,128)(2,1)} %w_ref.1), custom_call_target="tpu_custom_call" | custom-call | flops 335544320 | bytes 17000000 | tf_op jit(solution)/shard_map/pallas_call | solution.py:32
  24.7 10.2 %all-to-all-start.1 = ((bf16[128,6,40,128]{3,2,1,0:T(8,128)(2,1)}), bf16[128,6,40,128]{3,2,1,0:T(8,128)(2,1)}, u32[]{:S(2)}, u32[]{:S(2)}) async-start(bf16[128,6,40,128]{3,2,1,0:T(8,128)(2,1)} %bitcast.50), calls=%async_computation.1 | async-start | bytes 15728640 | tf_op jit(solution)/shard_map/all_to_all | solution.py:662
  39.4 89.8 %all-to-all-done.1 = bf16[128,6,40,128]{3,2,1,0:T(8,128)(2,1)} async-done(((bf16[128,6,40,128]{3,2,1,0:T(8,128)(2,1)}), bf16[128,6,40,128]{3,2,1,0:T(8,128)(2,1)}, u32[]{:S(2)}, u32[]{:S(2)}) %all-to-all-start.1) | async-done | bytes 7864352 | tf_op jit(solution)/shard_map/all_to_all | solution.py:662
  129.2 10.4 %shard_map.281 = (bf16[192,40,128]{2,1,0:T(8,128)(2,1)}, bf16[40,256]{1,0:T(8,128)(2,1)}, bf16[40,256]{1,0:T(8,128)(2,1)}) custom-call(s32[768]{0:T(1024)} %reshape.110.slot_ref, bf16[768,40,128]{2,1,0:T(8,128)(2,1)} %bitcast.16.in_ref), custom_call_target="tpu_custom_call" | custom-call | tf_op jit(solution)/shard_map/pallas_call | solution.py:92
  139.5 3.2 collective-permute-start.1
  145.4 2.0 shard_map.282
  147.3 5.1 %collective-permute-start.3 = (bf16[13,40,128]{2,1,0:T(8,128)(2,1)}, bf16[13,40,128]{2,1,0:T(8,128)(2,1)S(1)}, u32[]{:S(2)}, u32[]{:S(2)}) collective-permute-start(bf16[13,40,128]{2,1,0:T(8,128)(2,1)} %get-tuple-element.50.up_ref.refs_11_), channel_id=1, source_target_pairs={{4,0},{8,4},{12,8},{16,12},{20,16},{24,20},{28,24},{32,28},{36,32}... | collective-permute-start | bytes 399368 | tf_op jit(solution)/shard_map/ppermute | solution.py:596
  152.4 2.9 collective-permute-done.2.top_ref.refs_13_
  156.6 3.7 %shard_map.283 = (bf16[40,512]{1,0:T(8,128)(2,1)}, bf16[40,512]{1,0:T(8,128)(2,1)}, bf16[40,512]{1,0:T(8,128)(2,1)}, bf16[40,512]{1,0:T(8,128)(2,1)}, bf16[40,51...) custom-call(s32[54]{0:T(128)} %concatenate.17.s_ref, ...), custom_call_target="tpu_custom_call" | custom-call | tf_op jit(solution)/shard_map/pallas_call | solution.py:369
  162.2 1.9 collective-permute-start.11
  164.1 4.5 %collective-permute-start.12 = (bf16[40,512]{1,0:T(8,128)(2,1)}, bf16[40,512]{1,0:T(8,128)(2,1)S(1)}, u32[]{:S(2)}, u32[]{:S(2)}) collective-permute-start(bf16[40,512]{1,0:T(8,128)(2,1)} %get-tuple-element.60.refs_9_), channel_id=1, source_target_pairs={{0,3},{127,124}} | collective-permute-start | bytes 122888 | tf_op jit(solution)/shard_map/ppermute | solution.py:604
  168.7 3.1 collective-permute-start.4
  182.3 3.6 %collective-permute-done.8.refs_4_ = bf16[40,512]{1,0:T(8,128)(2,1)S(1)} collective-permute-done((bf16[40,512]{1,0:T(8,128)(2,1)}, bf16[40,512]{1,0:T(8,128)(2,1)S(1)}, u32[]{:S(2)}, u32[]{:S(2)}) %collective-permute-start.8) | collective-permute-done | bytes 40992 | tf_op jit(solution)/shard_map/ppermute | solution.py:604
  187.9 3.7 %shard_map.284 = (bf16[13,40,128]{2,1,0:T(8,128)(2,1)}, bf16[40,256]{1,0:T(8,128)(2,1)}) custom-call(s32[54]{0:T(128)} %concatenate.17.s_ref, bf16[40,512]{1,0:T(8,128)(2,1)} %copy-done.28, bf16[40,512]{1,0:T(8,128)(2,1)} %copy-done.29, bf16[40,512]{1,0:T(8,128)(2,1)} %copy-done.30, bf16[40,512]{1,0:T(8,128)(2,1)} %copy-done.31, bf16[40,512]{1,0:T(8,128)(2,1)} %copy-done.32, ...), custom_call_target="tpu_custom_call" | custom-call | tf_op jit(solution)/shard_map/pallas_call | solution.py:369
  191.6 7.0 %collective-permute-start.13 = (bf16[13,40,128]{2,1,0:T(8,128)(2,1)}, bf16[13,40,128]{2,1,0:T(8,128)(2,1)S(1)}, u32[]{:S(2)}, u32[]{:S(2)}) collective-permute-start(bf16[13,40,128]{2,1,0:T(8,128)(2,1)} %get-tuple-element.62.srow_ref), channel_id=1, source_target_pairs={{0,3},{1,2},{2,1},{3,0},{124,127},{125,126},{126,125},{127,124}} | collective-permute-start | bytes 399368 | tf_op jit(solution)/shard_map/ppermute | solution.py:618
  202.3 4.9 %collective-permute-done.14.rcol_ref = bf16[40,256]{1,0:T(8,128)(2,1)S(1)} collective-permute-done((bf16[40,256]{1,0:T(8,128)(2,1)}, bf16[40,256]{1,0:T(8,128)(2,1)S(1)}, u32[]{:S(2)}, u32[]{:S(2)}) %collective-permute-start.14) | collective-permute-done | bytes 20512 | tf_op jit(solution)/shard_map/ppermute | solution.py:619
  208.6 2.8 shard_map.285
  211.3 13.6 %shard_map.286 = (bf16[12,16,128,128]{3,2,1,0:T(8,128)(2,1)}, bf16[128,256]{1,0:T(8,128)(2,1)}, bf16[128,256]{1,0:T(8,128)(2,1)}) custom-call(bf16[256,512]{1,0:T(8,128)(2,1)} %bitcast.57, f32[256,1]{1,0:T(8,128)} %copy.54.b_ref, bf16[12,16,40,128]{3,2,1,0:T(8,128)(2,1)} %bitcast.53, bf16[12,40,128]{2,1,0:T(8,128)(2,1)} %get-tuple-element.64.top_ref, ...), custom_call_target="tpu_custom_call" | custom-call | tf_op jit(solution)/shard_map/pallas_call | solution.py:211
  224.9 3.2 collective-permute-start.16
  228.2 2.4 collective-permute-done.15.left_ref
  231.3 2.4 shard_map.287
  233.6 5.1 %collective-permute-start.18 = (bf16[13,128,128]{2,1,0:T(8,128)(2,1)}, bf16[13,128,128]{2,1,0:T(8,128)(2,1)S(1)}, u32[]{:S(2)}, u32[]{:S(2)}) collective-permute-start(bf16[13,128,128]{2,1,0:T(8,128)(2,1)} %get-tuple-element.71.up_ref.refs_11_), channel_id=1, source_target_pairs={{4,0},{8,4},{12,8},{16,12},{20,16},{24,20},{28,24},{32,28},{36,32}... | collective-permute-start | bytes 1277960 | tf_op jit(solution)/shard_map/ppermute | solution.py:596
  238.7 6.0 %collective-permute-done.17.top_ref.refs_13_ = bf16[13,128,128]{2,1,0:T(8,128)(2,1)S(1)} collective-permute-done((bf16[13,128,128]{2,1,0:T(8,128)(2,1)}, bf16[13,128,128]{2,1,0:T(8,128)(2,1)S(1)}, u32[]{:S(2)}, u32[]{:S(2)}) %collective-permute-start.17) | collective-permute-done | bytes 426016 | tf_op jit(solution)/shard_map/ppermute | solution.py:595
  246.3 5.6 %shard_map.288 = (bf16[128,512]{1,0:T(8,128)(2,1)}, bf16[128,512]{1,0:T(8,128)(2,1)}, bf16[128,512]{1,0:T(8,128)(2,1)}, bf16[128,512]{1,0:T(8,128)(2,1)}, bf16[1...) custom-call(s32[54]{0:T(128)} %concatenate.17.s_ref, ...), custom_call_target="tpu_custom_call" | custom-call | tf_op jit(solution)/shard_map/pallas_call | solution.py:369
  251.9 6.2 %collective-permute-start.19 = (bf16[128,512]{1,0:T(8,128)(2,1)}, bf16[128,512]{1,0:T(8,128)(2,1)S(1)}, u32[]{:S(2)}, u32[]{:S(2)}) collective-permute-start(bf16[128,512]{1,0:T(8,128)(2,1)} %get-tuple-element.73), channel_id=1, source_target_pairs={{0,124},{1,32},{32,1},{125,35},{35,125},{2,64},{64,2},{126,67},{67... | collective-permute-start | bytes 393224 | tf_op jit(solution)/shard_map/ppermute | solution.py:604
  271.7 3.1 collective-permute-start.27
  278.3 5.2 %shard_map.289 = (bf16[13,128,128]{2,1,0:T(8,128)(2,1)}, bf16[128,256]{1,0:T(8,128)(2,1)}) custom-call(s32[54]{0:T(128)} %concatenate.17.s_ref, bf16[128,512]{1,0:T(8,128)(2,1)} %copy-done.12, bf16[128,512]{1,0:T(8,128)(2,1)} %copy-done.13, bf16[128,512]{1,0:T(8,128)(2,1)} %copy-done.14, bf16[128,512]{1,0:T(8,128)(2,1)} %copy-done.15, ...), custom_call_target="tpu_custom_call" | custom-call | tf_op jit(solution)/shard_map/pallas_call | solution.py:369
  283.4 7.2 %collective-permute-start.28 = (bf16[13,128,128]{2,1,0:T(8,128)(2,1)}, bf16[13,128,128]{2,1,0:T(8,128)(2,1)S(1)}, u32[]{:S(2)}, u32[]{:S(2)}) collective-permute-start(bf16[13,128,128]{2,1,0:T(8,128)(2,1)} %get-tuple-element.83.srow_ref), channel_id=1, source_target_pairs={{0,3},{1,2},{2,1},{3,0},{124,127},{125,126},{126,125},{127,124}} | collective-permute-start | bytes 1277960 | tf_op jit(solution)/shard_map/ppermute | solution.py:618
  295.4 6.4 %collective-permute-done.29.rcol_ref = bf16[128,256]{1,0:T(8,128)(2,1)S(1)} collective-permute-done((bf16[128,256]{1,0:T(8,128)(2,1)}, bf16[128,256]{1,0:T(8,128)(2,1)S(1)}, u32[]{:S(2)}, u32[]{:S(2)}) %collective-permute-start.29) | collective-permute-done | bytes 65568 | tf_op jit(solution)/shard_map/ppermute | solution.py:619
  303.2 3.2 shard_map.290
  306.4 18.7 %shard_map.291 = bf16[128,12,16,128]{3,2,1,0:T(8,128)(2,1)} custom-call(bf16[256,1536]{1,0:T(8,128)(2,1)} %bitcast.54, f32[256,1]{1,0:T(8,128)} %copy.55.b_ref, bf16[12,16,128,128]{3,2,1,0:T(8,128)(2,1)} %get-tuple-element.68.first_ref.last_ref.x_ref, bf16[12,128,128]{2,1,0:T(8,128)(2,1)} %get-tuple-element.85.top_ref, ...), custom_call_target="tpu_custom_call" | custom-call | tf_op jit(solution)/shard_map/pallas_call | solution.py:211
  (187 shorter events, 55.5 us)
Async XLA Ops:
  2.9 21.7 %all-to-all-start = ((s32[128,1,6]{2,1,0:T(1,128)}), s32[128,1,6]{2,1,0:T(1,128)S(1)}, u32[]{:S(2)}, u32[]{:S(2)}) async-start(s32[128,1,6]{2,1,0:T(1,128)} %bitcast.14), calls=%async_computation | async-start | bytes 131072 | tf_op jit(solution)/shard_map/all_to_all | solution.py:660
  24.7 104.4 %all-to-all-start.1 = ((bf16[128,6,40,128]{3,2,1,0:T(8,128)(2,1)}), bf16[128,6,40,128]{3,2,1,0:T(8,128)(2,1)}, u32[]{:S(2)}, u32[]{:S(2)}) async-start(bf16[128,6,40,128]{3,2,1,0:T(8,128)(2,1)} %bitcast.50), calls=%async_computation.1 | async-start | bytes 15728640 | tf_op jit(solution)/shard_map/all_to_all | solution.py:662
  139.5 5.2 %collective-permute-start = (bf16[40,256]{1,0:T(8,128)(2,1)}, bf16[40,256]{1,0:T(8,128)(2,1)S(1)}, u32[]{:S(2)}, u32[]{:S(2)}) collective-permute-start(bf16[40,256]{1,0:T(8,128)(2,1)} %get-tuple-element.48.high_ref), channel_id=1, source_target_pairs={{0,1},{1,2},{2,3},{3,0},{4,5},{5,6},{6,7},{7,4},{8,9},{9,10},{10,1... | collective-permute-start | bytes 61448 | tf_op jit(solution)/shard_map/ppermute | solution.py:591
  139.5 5.2 %collective-permute-start.1 = (bf16[40,256]{1,0:T(8,128)(2,1)}, bf16[40,256]{1,0:T(8,128)(2,1)S(1)}, u32[]{:S(2)}, u32[]{:S(2)}) collective-permute-start(bf16[40,256]{1,0:T(8,128)(2,1)} %get-tuple-element.49.low_ref), channel_id=1, source_target_pairs={{1,0},{2,1},{3,2},{0,3},{5,4},{6,5},{7,6},{4,7},{9,8},{10,9},{11,1... | collective-permute-start | bytes 61448 | tf_op jit(solution)/shard_map/ppermute | solution.py:592
  147.3 7.9 %collective-permute-start.2 = (bf16[13,40,128]{2,1,0:T(8,128)(2,1)}, bf16[13,40,128]{2,1,0:T(8,128)(2,1)S(1)}, u32[]{:S(2)}, u32[]{:S(2)}) collective-permute-start(bf16[13,40,128]{2,1,0:T(8,128)(2,1)} %get-tuple-element.51.down_ref.refs_12_), channel_id=1, source_target_pairs={{0,4},{4,8},{8,12},{12,16},{16,20},{20,24},{24,28},{28,32},{32,36}... | collective-permute-start | bytes 399368 | tf_op jit(solution)/shard_map/ppermute | solution.py:595
  147.3 7.9 %collective-permute-start.3 = (bf16[13,40,128]{2,1,0:T(8,128)(2,1)}, bf16[13,40,128]{2,1,0:T(8,128)(2,1)S(1)}, u32[]{:S(2)}, u32[]{:S(2)}) collective-permute-start(bf16[13,40,128]{2,1,0:T(8,128)(2,1)} %get-tuple-element.50.up_ref.refs_11_), channel_id=1, source_target_pairs={{4,0},{8,4},{12,8},{16,12},{20,16},{24,20},{28,24},{32,28},{36,32}... | collective-permute-start | bytes 399368 | tf_op jit(solution)/shard_map/ppermute | solution.py:596
  160.3 14.1 %collective-permute-start.10 = (bf16[40,512]{1,0:T(8,128)(2,1)}, bf16[40,512]{1,0:T(8,128)(2,1)S(1)}, u32[]{:S(2)}, u32[]{:S(2)}) collective-permute-start(bf16[40,512]{1,0:T(8,128)(2,1)} %get-tuple-element.58), channel_id=1, source_target_pairs={{0,24},{24,0},{124,27},{27,124},{1,56},{56,1},{125,59},{59,125},{2... | collective-permute-start | bytes 122888 | tf_op jit(solution)/shard_map/ppermute | solution.py:604
  162.2 14.1 %collective-permute-start.11 = (bf16[40,512]{1,0:T(8,128)(2,1)}, bf16[40,512]{1,0:T(8,128)(2,1)S(1)}, u32[]{:S(2)}, u32[]{:S(2)}) collective-permute-start(bf16[40,512]{1,0:T(8,128)(2,1)} %get-tuple-element.59), channel_id=1, source_target_pairs={{127,3},{0,28},{28,0},{124,31},{31,124},{1,60},{60,1},{125,63},{63... | collective-permute-start | bytes 122888 | tf_op jit(solution)/shard_map/ppermute | solution.py:604
  164.1 14.1 %collective-permute-start.12 = (bf16[40,512]{1,0:T(8,128)(2,1)}, bf16[40,512]{1,0:T(8,128)(2,1)S(1)}, u32[]{:S(2)}, u32[]{:S(2)}) collective-permute-start(bf16[40,512]{1,0:T(8,128)(2,1)} %get-tuple-element.60.refs_9_), channel_id=1, source_target_pairs={{0,3},{127,124}} | collective-permute-start | bytes 122888 | tf_op jit(solution)/shard_map/ppermute | solution.py:604
  168.7 11.6 %collective-permute-start.4 = (bf16[40,512]{1,0:T(8,128)(2,1)}, bf16[40,512]{1,0:T(8,128)(2,1)S(1)}, u32[]{:S(2)}, u32[]{:S(2)}) collective-permute-start(bf16[40,512]{1,0:T(8,128)(2,1)} %get-tuple-element.52), channel_id=1, source_target_pairs={{0,124},{1,32},{32,1},{125,35},{35,125},{2,64},{64,2},{126,67},{67... | collective-permute-start | bytes 122888 | tf_op jit(solution)/shard_map/ppermute | solution.py:604
  172.4 9.8 %collective-permute-start.5 = (bf16[40,512]{1,0:T(8,128)(2,1)}, bf16[40,512]{1,0:T(8,128)(2,1)S(1)}, u32[]{:S(2)}, u32[]{:S(2)}) collective-permute-start(bf16[40,512]{1,0:T(8,128)(2,1)} %get-tuple-element.53), channel_id=1, source_target_pairs={{0,4},{4,0},{124,7},{7,124},{1,36},{36,1},{125,39},{39,125},{2,68}... | collective-permute-start | bytes 122888 | tf_op jit(solution)/shard_map/ppermute | solution.py:604
  174.4 7.8 %collective-permute-start.6 = (bf16[40,512]{1,0:T(8,128)(2,1)}, bf16[40,512]{1,0:T(8,128)(2,1)S(1)}, u32[]{:S(2)}, u32[]{:S(2)}) collective-permute-start(bf16[40,512]{1,0:T(8,128)(2,1)} %get-tuple-element.54), channel_id=1, source_target_pairs={{0,8},{8,0},{124,11},{11,124},{1,40},{40,1},{125,43},{43,125},{2,7... | collective-permute-start | bytes 122888 | tf_op jit(solution)/shard_map/ppermute | solution.py:604
  176.3 5.9 %collective-permute-start.7 = (bf16[40,512]{1,0:T(8,128)(2,1)}, bf16[40,512]{1,0:T(8,128)(2,1)S(1)}, u32[]{:S(2)}, u32[]{:S(2)}) collective-permute-start(bf16[40,512]{1,0:T(8,128)(2,1)} %get-tuple-element.55), channel_id=1, source_target_pairs={{0,12},{12,0},{124,15},{15,124},{1,44},{44,1},{125,47},{47,125},{2... | collective-permute-start | bytes 122888 | tf_op jit(solution)/shard_map/ppermute | solution.py:604
  178.3 7.6 %collective-permute-start.8 = (bf16[40,512]{1,0:T(8,128)(2,1)}, bf16[40,512]{1,0:T(8,128)(2,1)S(1)}, u32[]{:S(2)}, u32[]{:S(2)}) collective-permute-start(bf16[40,512]{1,0:T(8,128)(2,1)} %get-tuple-element.56), channel_id=1, source_target_pairs={{0,16},{16,0},{124,19},{19,124},{1,48},{48,1},{125,51},{51,125},{2... | collective-permute-start | bytes 122888 | tf_op jit(solution)/shard_map/ppermute | solution.py:604
  180.2 7.0 %collective-permute-start.9 = (bf16[40,512]{1,0:T(8,128)(2,1)}, bf16[40,512]{1,0:T(8,128)(2,1)S(1)}, u32[]{:S(2)}, u32[]{:S(2)}) collective-permute-start(bf16[40,512]{1,0:T(8,128)(2,1)} %get-tuple-element.57), channel_id=1, source_target_pairs={{0,20},{20,0},{124,23},{23,124},{1,52},{52,1},{125,55},{55,125},{2... | collective-permute-start | bytes 122888 | tf_op jit(solution)/shard_map/ppermute | solution.py:604
  191.6 15.7 %collective-permute-start.13 = (bf16[13,40,128]{2,1,0:T(8,128)(2,1)}, bf16[13,40,128]{2,1,0:T(8,128)(2,1)S(1)}, u32[]{:S(2)}, u32[]{:S(2)}) collective-permute-start(bf16[13,40,128]{2,1,0:T(8,128)(2,1)} %get-tuple-element.62.srow_ref), channel_id=1, source_target_pairs={{0,3},{1,2},{2,1},{3,0},{124,127},{125,126},{126,125},{127,124}} | collective-permute-start | bytes 399368 | tf_op jit(solution)/shard_map/ppermute | solution.py:618
  198.7 8.6 %collective-permute-start.14 = (bf16[40,256]{1,0:T(8,128)(2,1)}, bf16[40,256]{1,0:T(8,128)(2,1)S(1)}, u32[]{:S(2)}, u32[]{:S(2)}) collective-permute-start(bf16[40,256]{1,0:T(8,128)(2,1)} %get-tuple-element.63.scol_ref), channel_id=1, source_target_pairs={{0,124},{3,127},{4,120},{7,123},{8,116},{11,119},{12,112},{15,115}... | collective-permute-start | bytes 61448 | tf_op jit(solution)/shard_map/ppermute | solution.py:619
  224.9 5.7 %collective-permute-start.15 = (bf16[128,256]{1,0:T(8,128)(2,1)}, bf16[128,256]{1,0:T(8,128)(2,1)S(1)}, u32[]{:S(2)}, u32[]{:S(2)}) collective-permute-start(bf16[128,256]{1,0:T(8,128)(2,1)} %get-tuple-element.69.high_ref), channel_id=1, source_target_pairs={{0,1},{1,2},{2,3},{3,0},{4,5},{5,6},{6,7},{7,4},{8,9},{9,10},{10,1... | collective-permute-start | bytes 196616 | tf_op jit(solution)/shard_map/ppermute | solution.py:591
  224.9 5.7 %collective-permute-start.16 = (bf16[128,256]{1,0:T(8,128)(2,1)}, bf16[128,256]{1,0:T(8,128)(2,1)S(1)}, u32[]{:S(2)}, u32[]{:S(2)}) collective-permute-start(bf16[128,256]{1,0:T(8,128)(2,1)} %get-tuple-element.70.low_ref), channel_id=1, source_target_pairs={{1,0},{2,1},{3,2},{0,3},{5,4},{6,5},{7,6},{4,7},{9,8},{10,9},{11,1... | collective-permute-start | bytes 196616 | tf_op jit(solution)/shard_map/ppermute | solution.py:592
  233.6 11.1 %collective-permute-start.17 = (bf16[13,128,128]{2,1,0:T(8,128)(2,1)}, bf16[13,128,128]{2,1,0:T(8,128)(2,1)S(1)}, u32[]{:S(2)}, u32[]{:S(2)}) collective-permute-start(bf16[13,128,128]{2,1,0:T(8,128)(2,1)} %get-tuple-element.72.down_ref.refs_12_), channel_id=1, source_target_pairs={{0,4},{4,8},{8,12},{12,16},{16,20},{20,24},{24,28},{28,32},{32,36}... | collective-permute-start | bytes 1277960 | tf_op jit(solution)/shard_map/ppermute | solution.py:595
  233.6 11.1 %collective-permute-start.18 = (bf16[13,128,128]{2,1,0:T(8,128)(2,1)}, bf16[13,128,128]{2,1,0:T(8,128)(2,1)S(1)}, u32[]{:S(2)}, u32[]{:S(2)}) collective-permute-start(bf16[13,128,128]{2,1,0:T(8,128)(2,1)} %get-tuple-element.71.up_ref.refs_11_), channel_id=1, source_target_pairs={{4,0},{8,4},{12,8},{16,12},{20,16},{24,20},{28,24},{32,28},{36,32}... | collective-permute-start | bytes 1277960 | tf_op jit(solution)/shard_map/ppermute | solution.py:596
  251.9 13.9 %collective-permute-start.19 = (bf16[128,512]{1,0:T(8,128)(2,1)}, bf16[128,512]{1,0:T(8,128)(2,1)S(1)}, u32[]{:S(2)}, u32[]{:S(2)}) collective-permute-start(bf16[128,512]{1,0:T(8,128)(2,1)} %get-tuple-element.73), channel_id=1, source_target_pairs={{0,124},{1,32},{32,1},{125,35},{35,125},{2,64},{64,2},{126,67},{67... | collective-permute-start | bytes 393224 | tf_op jit(solution)/shard_map/ppermute | solution.py:604
  258.1 9.7 %collective-permute-start.20 = (bf16[128,512]{1,0:T(8,128)(2,1)}, bf16[128,512]{1,0:T(8,128)(2,1)S(1)}, u32[]{:S(2)}, u32[]{:S(2)}) collective-permute-start(bf16[128,512]{1,0:T(8,128)(2,1)} %get-tuple-element.74), channel_id=1, source_target_pairs={{0,4},{4,0},{124,7},{7,124},{1,36},{36,1},{125,39},{39,125},{2,68}... | collective-permute-start | bytes 393224 | tf_op jit(solution)/shard_map/ppermute | solution.py:604
  260.0 9.7 %collective-permute-start.21 = (bf16[128,512]{1,0:T(8,128)(2,1)}, bf16[128,512]{1,0:T(8,128)(2,1)S(1)}, u32[]{:S(2)}, u32[]{:S(2)}) collective-permute-start(bf16[128,512]{1,0:T(8,128)(2,1)} %get-tuple-element.75), channel_id=1, source_target_pairs={{0,8},{8,0},{124,11},{11,124},{1,40},{40,1},{125,43},{43,125},{2,7... | collective-permute-start | bytes 393224 | tf_op jit(solution)/shard_map/ppermute | solution.py:604
  261.9 9.7 %collective-permute-start.22 = (bf16[128,512]{1,0:T(8,128)(2,1)}, bf16[128,512]{1,0:T(8,128)(2,1)S(1)}, u32[]{:S(2)}, u32[]{:S(2)}) collective-permute-start(bf16[128,512]{1,0:T(8,128)(2,1)} %get-tuple-element.76), channel_id=1, source_target_pairs={{0,12},{12,0},{124,15},{15,124},{1,44},{44,1},{125,47},{47,125},{2... | collective-permute-start | bytes 393224 | tf_op jit(solution)/shard_map/ppermute | solution.py:604
  263.9 10.9 %collective-permute-start.23 = (bf16[128,512]{1,0:T(8,128)(2,1)}, bf16[128,512]{1,0:T(8,128)(2,1)S(1)}, u32[]{:S(2)}, u32[]{:S(2)}) collective-permute-start(bf16[128,512]{1,0:T(8,128)(2,1)} %get-tuple-element.77), channel_id=1, source_target_pairs={{0,16},{16,0},{124,19},{19,124},{1,48},{48,1},{125,51},{51,125},{2... | collective-permute-start | bytes 393224 | tf_op jit(solution)/shard_map/ppermute | solution.py:604
  265.8 9.0 %collective-permute-start.24 = (bf16[128,512]{1,0:T(8,128)(2,1)}, bf16[128,512]{1,0:T(8,128)(2,1)S(1)}, u32[]{:S(2)}, u32[]{:S(2)}) collective-permute-start(bf16[128,512]{1,0:T(8,128)(2,1)} %get-tuple-element.78), channel_id=1, source_target_pairs={{0,20},{20,0},{124,23},{23,124},{1,52},{52,1},{125,55},{55,125},{2... | collective-permute-start | bytes 393224 | tf_op jit(solution)/shard_map/ppermute | solution.py:604
  267.8 8.3 %collective-permute-start.25 = (bf16[128,512]{1,0:T(8,128)(2,1)}, bf16[128,512]{1,0:T(8,128)(2,1)S(1)}, u32[]{:S(2)}, u32[]{:S(2)}) collective-permute-start(bf16[128,512]{1,0:T(8,128)(2,1)} %get-tuple-element.79), channel_id=1, source_target_pairs={{0,24},{24,0},{124,27},{27,124},{1,56},{56,1},{125,59},{59,125},{2... | collective-permute-start | bytes 393224 | tf_op jit(solution)/shard_map/ppermute | solution.py:604
  269.7 7.7 %collective-permute-start.26 = (bf16[128,512]{1,0:T(8,128)(2,1)}, bf16[128,512]{1,0:T(8,128)(2,1)S(1)}, u32[]{:S(2)}, u32[]{:S(2)}) collective-permute-start(bf16[128,512]{1,0:T(8,128)(2,1)} %get-tuple-element.80), channel_id=1, source_target_pairs={{127,3},{0,28},{28,0},{124,31},{31,124},{1,60},{60,1},{125,63},{63... | collective-permute-start | bytes 393224 | tf_op jit(solution)/shard_map/ppermute | solution.py:604
  271.7 6.0 %collective-permute-start.27 = (bf16[128,512]{1,0:T(8,128)(2,1)}, bf16[128,512]{1,0:T(8,128)(2,1)S(1)}, u32[]{:S(2)}, u32[]{:S(2)}) collective-permute-start(bf16[128,512]{1,0:T(8,128)(2,1)} %get-tuple-element.81.refs_9_), channel_id=1, source_target_pairs={{0,3},{127,124}} | collective-permute-start | bytes 393224 | tf_op jit(solution)/shard_map/ppermute | solution.py:604
  283.4 18.4 %collective-permute-start.28 = (bf16[13,128,128]{2,1,0:T(8,128)(2,1)}, bf16[13,128,128]{2,1,0:T(8,128)(2,1)S(1)}, u32[]{:S(2)}, u32[]{:S(2)}) collective-permute-start(bf16[13,128,128]{2,1,0:T(8,128)(2,1)} %get-tuple-element.83.srow_ref), channel_id=1, source_target_pairs={{0,3},{1,2},{2,1},{3,0},{124,127},{125,126},{126,125},{127,124}} | collective-permute-start | bytes 1277960 | tf_op jit(solution)/shard_map/ppermute | solution.py:618
  292.7 9.1 %collective-permute-start.29 = (bf16[128,256]{1,0:T(8,128)(2,1)}, bf16[128,256]{1,0:T(8,128)(2,1)S(1)}, u32[]{:S(2)}, u32[]{:S(2)}) collective-permute-start(bf16[128,256]{1,0:T(8,128)(2,1)} %get-tuple-element.84.scol_ref), channel_id=1, source_target_pairs={{0,124},{3,127},{4,120},{7,123},{8,116},{11,119},{12,112},{15,115}... | collective-permute-start | bytes 196616 | tf_op jit(solution)/shard_map/ppermute | solution.py:619
  (48 other events, 805.0 us)

commit v4 on v3

--- a/solution.py
+++ b/solution.py
@@ -14,21 +14,30 @@
 VMEM_LIMIT = 56 * 1024 * 1024
 
 
-def regrid_kernel(pos_ref, src_ref, w_ref, out_ref, *, blocks, top, length):
+def regrid_kernel(pos_ref, src_ref, w_ref, slot_ref, out_ref, *, blocks, top, length):
     step = pl.program_id(0)
+    fields = src_ref.shape[0]
+    count = pl.num_programs(0) * blocks * top
+
+    @pl.when(step == 0)
+    def _():
+        out_ref[:, out_ref.shape[1] - 1] = slot_ref[...]
+
     for s in range(blocks):
         lhs = src_ref[:, s * length : (s + 1) * length]
         rhs = jnp.concatenate([w_ref[s, k] for k in range(top)], axis=1)
-        val = jnp.dot(lhs, rhs, preferred_element_type=F32).astype(BF)
+        val = jnp.dot(lhs, rhs, preferred_element_type=F32)
         for k in range(top):
-            where = pos_ref[(step * blocks + s) * top + k]
-            out_ref[where] = val[:, k * length : (k + 1) * length]
-
-
-def regrid(source, weights, position, slots):
+            item = (step * blocks + s) * top + k
+            piece = val[:, k * length : (k + 1) * length].reshape(fields // 8, 8, length)
+            out_ref[pos_ref[item], pl.ds(pos_ref[count + item], fields // 8)] = piece.astype(BF)
+
+
+def regrid(source, weights, position, slots, capacity):
     fields = source.shape[0]
     count, top, length = weights.shape[0], weights.shape[1], weights.shape[2]
     blocks = 8
+    shape = (slots.shape[0], capacity * fields // 8 + 1, 8, length)
     return pl.pallas_call(
         functools.partial(regrid_kernel, blocks=blocks, top=top, length=length),
         grid_spec=pltpu.PrefetchScalarGridSpec(
@@ -37,15 +46,16 @@
             in_specs=[
                 pl.BlockSpec((fields, blocks * length), lambda i, p: (0, i)),
                 pl.BlockSpec((blocks, top, length, length), lambda i, p: (i, 0, 0, 0)),
+                pl.BlockSpec(slots.shape, lambda i, p: (0, 0, 0)),
             ],
-            out_specs=pl.BlockSpec((slots, fields, length), lambda i, p: (0, 0, 0)),
+            out_specs=pl.BlockSpec(shape, lambda i, p: (0, 0, 0, 0)),
         ),
-        out_shape=jax.ShapeDtypeStruct((slots, fields, length), BF),
+        out_shape=jax.ShapeDtypeStruct(shape, BF),
         compiler_params=pltpu.CompilerParams(vmem_limit_bytes=VMEM_LIMIT),
         cost_estimate=pl.CostEstimate(
             flops=2 * count * top * length * length * fields, bytes_accessed=17_000_000, transcendentals=0
         ),
-    )(position, source, weights)
+    )(position, source, weights, slots)
 
 
 def edge_columns(piece, lane, at, low, high):
@@ -58,6 +68,8 @@
 
 def place_kernel(slot_ref, in_ref, out_ref, low_ref, high_ref, acc_ref, acc2_ref, *, chunk):
     step = pl.program_id(0)
+    tiles = acc_ref.shape[1]
+    capacity = in_ref.shape[1] // tiles
 
     @pl.when(step == 0)
     def _():
@@ -65,12 +77,13 @@
         acc2_ref[...] = jnp.zeros_like(acc2_ref)
 
     def body(i, carry):
-        for j, ref in ((2 * i, acc_ref), (2 * i + 1, acc2_ref)):
-            where = slot_ref[step * chunk + j]
-            ref[where] += in_ref[j].astype(F32)
+        for r in range(capacity):
+            ref = acc_ref if r % 2 == 0 else acc2_ref
+            where = slot_ref[(step * chunk + i) * capacity + r]
+            ref[where] += in_ref[i, r * tiles : (r + 1) * tiles].astype(F32)
         return carry
 
-    lax.fori_loop(0, chunk // 2, body, 0, unroll=8)
+    lax.fori_loop(0, chunk, body, 0, unroll=2)
 
     @pl.when(step == pl.num_programs(0) - 1)
     def _():
@@ -79,7 +92,7 @@
         for half in range(2):
             low = high = jnp.zeros((chans, cols), F32)
             for at in range(min(cols, count - half * cols)):
-                piece = acc_ref[half * cols + at] + acc2_ref[half * cols + at]
+                piece = (acc_ref[half * cols + at] + acc2_ref[half * cols + at]).reshape(chans, cols)
                 out_ref[half * cols + at] = piece.astype(BF)
                 low, high = edge_columns(piece, lane, at, low, high)
             low_ref[:, half * cols : (half + 1) * cols] = low.astype(BF)
@@ -87,20 +100,21 @@
 
 
 def place(arrived, slots, count):
-    items, fields, length = arrived.shape
-    chunk = 96
+    senders, size, eight, length = arrived.shape
+    chunk = 16
+    fields = size // (slots.shape[0] // senders) * eight
     return pl.pallas_call(
         functools.partial(place_kernel, chunk=chunk),
         grid_spec=pltpu.PrefetchScalarGridSpec(
             num_scalar_prefetch=1,
-            grid=(items // chunk,),
-            in_specs=[pl.BlockSpec((chunk, fields, length), lambda i, p: (i, 0, 0))],
+            grid=(senders // chunk,),
+            in_specs=[pl.BlockSpec((chunk, size, eight, length), lambda i, p: (i, 0, 0, 0))],
             out_specs=[
                 pl.BlockSpec((count, fields, length), lambda i, p: (0, 0, 0)),
                 pl.BlockSpec((fields, 2 * length), lambda i, p: (0, 0)),
                 pl.BlockSpec((fields, 2 * length), lambda i, p: (0, 0)),
             ],
-            scratch_shapes=[pltpu.VMEM((count + 1, fields, length), F32)] * 2,
+            scratch_shapes=[pltpu.VMEM((count + 1, fields // 8, 8, length), F32)] * 2,
         ),
         out_shape=[
             jax.ShapeDtypeStruct((count, fields, length), BF),
@@ -652,17 +666,21 @@
     target = dest_group.reshape(items)
     order = jnp.arange(items)
     same = (target[:, None] == target[None, :]) & (order[None, :] < order[:, None])
-    position = target * capacity + jnp.sum(same.astype(jnp.int32), axis=1)
+    rank = jnp.sum(same.astype(jnp.int32), axis=1)
+    position = target * capacity + rank
     hit = position[:, None] == jnp.arange(total)[None, :]
     out_slots = slots_dev + jnp.sum(
         jnp.where(hit, (dest_block.reshape(items) - slots_dev)[:, None], 0), axis=0
     )
-    slots = lax.all_to_all(out_slots.reshape(devices, capacity), AXES, split_axis=0, concat_axis=0, tiled=True)
-    outgoing = regrid(source, regrid_weights, position, total)
-    arrived = lax.all_to_all(
-        outgoing.reshape(devices, capacity, fields, block_len), AXES, split_axis=0, concat_axis=0, tiled=True
-    )
-    regridded, low, high = place(arrived.reshape(total, fields, block_len), slots.reshape(total), slots_dev)
+    out_slots = jnp.pad(
+        out_slots.reshape(devices, 1, capacity).astype(BF), ((0, 0), (0, 7), (0, block_len - capacity))
+    )
+    outgoing = regrid(
+        source, regrid_weights, jnp.concatenate([target, rank * (fields // 8)]), out_slots, capacity
+    )
+    arrived = lax.all_to_all(outgoing, AXES, split_axis=0, concat_axis=0, tiled=True)
+    slots = arrived[:, -1, 0, :capacity].astype(jnp.int32).reshape(total)
+    regridded, low, high = place(arrived, slots, slots_dev)
     regridded = regridded.reshape(faces, rows, fields, block_len)
 
     plan = Plan(bands, tiles)

time: 326 us -> 322 us (0.988)
  starting transfers between devices: 99.8 us -> 90.6 us
  waiting for transfers between devices: 121 us -> 125 us
    all_to_all x2 -> x1, starting transfers between devices: 21.4 us -> 11.6 us  [local(): lax.all_to_all(outgoing, AXES, split_axis=0, concat_axis=0, tiled=True)]
    all_to_all x2 -> x1, waiting for transfers between devices: 89.8 us -> 94.6 us  [local(): lax.all_to_all(outgoing, AXES, split_axis=0, concat_axis=0, tiled=True)]
    unnamed x101 -> x99, local copies, waits for them, and re-layouts: 10.9 us -> 10.9 us
  transfers between devices with their start and end apart: 32 -> 31, of which waited for: 12 -> 12; matrix products, arithmetic and copies ran while one was open for 3% -> 3% of each run, Pallas kernels for 3% -> 0%
where the time goes in v4:
time: 322 us; the launch traced here: 320 us
  waiting for transfers between devices  125 us (39%)
  starting transfers between devices  90.6 us (28%)
  Pallas kernels  80.8 us (25%)
  local copies, waits for them, and re-layouts  16.7 us (5%)
  other arithmetic  5.73 us (2%)
    all_to_all x1, waiting for transfers between devices, local(): lax.all_to_all(outgoing, AXES, split_axis=0, concat_axis=0, tiled=True)  94.6 us
    ppermute x18, starting transfers between devices, exchange(): lax.ppermute(m, AXES, pairs)  43.8 us
    pallas_call x2, Pallas kernels, conv(): pl.pallas_call(functools.partial(conv_kernel, last=last), grid=(face_coun...  32.3 us
    pallas_call x6, Pallas kernels, whole(): pl.pallas_call(kernel, in_specs=[pl.BlockSpec(memory_space=pltpu.SMEM)] +...  23.1 us
    ppermute x2, starting transfers between devices, exchange(): rrow = lax.ppermute(srow, AXES, plan.flip_row)  14.2 us
    all_to_all x1, starting transfers between devices, local(): lax.all_to_all(outgoing, AXES, split_axis=0, concat_axis=0, tiled=True)  11.6 us
    ppermute x2, waiting for transfers between devices, exchange(): rcol = lax.ppermute(scol, AXES, plan.flip_col)  11 us
    unnamed x99, local copies, waits for them, and re-layouts  10.9 us
  transfers between devices with their start and end apart: 31, of which 12 were waited for; matrix products, arithmetic and copies ran while one was open for 3% of the time, Pallas kernels for 0%

profile of v4, /device:TPU:0, one launch (start us, length us, event | category | flops | bytes accessed | tf_op | source)
XLA Modules:
  0.0 320.1 jit_solution(6121524698741396018)
XLA Ops:
  3.7 10.8 %shard_map.280 = bf16[128,31,8,128]{3,2,1,0:T(8,128)(2,1)} custom-call(s32[512]{0:T(512)} %pad_add_fusion.pos_ref, bf16[40,8192]{1,0:T(8,128)(2,1)} %src_ref.1, bf16[64,4,128,128]{3,2,1,0:T(8,128)(2,1)} %w_ref.1, bf16[128,8,128]{2,1,0:T(8,128)(2,1)} %pad.29.slot_ref), custom_call_target="tpu_custom_call" | custom-call | flops 335544320 | bytes 17000000 | tf_op jit(solution)/shard_map/pallas_call | solution.py:41
  14.5 11.6 %all-to-all-start = ((bf16[128,31,8,128]{3,2,1,0:T(8,128)(2,1)}), bf16[128,31,8,128]{3,2,1,0:T(8,128)(2,1)}, u32[]{:S(2)}, u32[]{:S(2)}) async-start(bf16[128,31,8,128]{3,2,1,0:T(8,128)(2,1)} %shard_map.280), calls=%async_computation | async-start | bytes 16252928 | tf_op jit(solution)/shard_map/all_to_all | solution.py:681
  28.5 94.6 %all-to-all-done.in_ref = bf16[128,31,8,128]{3,2,1,0:T(8,128)(2,1)} async-done(((bf16[128,31,8,128]{3,2,1,0:T(8,128)(2,1)}), bf16[128,31,8,128]{3,2,1,0:T(8,128)(2,1)}, u32[]{:S(2)}, u32[]{:S(2)}) %all-to-all-start) | async-done | bytes 8126496 | tf_op jit(solution)/shard_map/all_to_all | solution.py:681
  125.1 10.4 %shard_map.281 = (bf16[192,40,128]{2,1,0:T(8,128)(2,1)}, bf16[40,256]{1,0:T(8,128)(2,1)}, bf16[40,256]{1,0:T(8,128)(2,1)}) custom-call(s32[768]{0:T(1024)} %reshape.109.slot_ref, bf16[128,31,8,128]{3,2,1,0:T(8,128)(2,1)} %all-to-all-done.in_ref), custom_call_target="tpu_custom_call" | custom-call | tf_op jit(solution)/shard_map/pallas_call | solution.py:106
  135.4 3.2 %collective-permute-start.1 = (bf16[40,256]{1,0:T(8,128)(2,1)}, bf16[40,256]{1,0:T(8,128)(2,1)S(1)}, u32[]{:S(2)}, u32[]{:S(2)}) collective-permute-start(bf16[40,256]{1,0:T(8,128)(2,1)} %get-tuple-element.49.low_ref), channel_id=1, source_target_pairs={{1,0},{2,1},{3,2},{0,3},{5,4},{6,5},{7,6},{4,7},{9,8},{10,9},{11,1... | collective-permute-start | bytes 61448 | tf_op jit(solution)/shard_map/ppermute | solution.py:606
  141.3 2.0 shard_map.282
  143.2 5.1 %collective-permute-start.3 = (bf16[13,40,128]{2,1,0:T(8,128)(2,1)}, bf16[13,40,128]{2,1,0:T(8,128)(2,1)S(1)}, u32[]{:S(2)}, u32[]{:S(2)}) collective-permute-start(bf16[13,40,128]{2,1,0:T(8,128)(2,1)} %get-tuple-element.50.up_ref.refs_11_), channel_id=1, source_target_pairs={{4,0},{8,4},{12,8},{16,12},{20,16},{24,20},{28,24},{32,28},{36,32}... | collective-permute-start | bytes 399368 | tf_op jit(solution)/shard_map/ppermute | solution.py:610
  148.3 2.9 collective-permute-done.2.top_ref.refs_13_
  152.5 3.7 %shard_map.283 = (bf16[40,512]{1,0:T(8,128)(2,1)}, bf16[40,512]{1,0:T(8,128)(2,1)}, bf16[40,512]{1,0:T(8,128)(2,1)}, bf16[40,512]{1,0:T(8,128)(2,1)}, bf16[40,51...) custom-call(s32[54]{0:T(128)} %concatenate.21.s_ref, ...), custom_call_target="tpu_custom_call" | custom-call | tf_op jit(solution)/shard_map/pallas_call | solution.py:383
  156.2 1.9 collective-permute-start.10
  160.1 4.5 %collective-permute-start.12 = (bf16[40,512]{1,0:T(8,128)(2,1)}, bf16[40,512]{1,0:T(8,128)(2,1)S(1)}, u32[]{:S(2)}, u32[]{:S(2)}) collective-permute-start(bf16[40,512]{1,0:T(8,128)(2,1)} %get-tuple-element.60.refs_9_), channel_id=1, source_target_pairs={{0,3},{127,124}} | collective-permute-start | bytes 122888 | tf_op jit(solution)/shard_map/ppermute | solution.py:618
  164.6 3.1 collective-permute-start.4
  178.2 3.6 %collective-permute-done.8.refs_4_ = bf16[40,512]{1,0:T(8,128)(2,1)S(1)} collective-permute-done((bf16[40,512]{1,0:T(8,128)(2,1)}, bf16[40,512]{1,0:T(8,128)(2,1)S(1)}, u32[]{:S(2)}, u32[]{:S(2)}) %collective-permute-start.8) | collective-permute-done | bytes 40992 | tf_op jit(solution)/shard_map/ppermute | solution.py:618
  183.8 3.5 %shard_map.284 = (bf16[13,40,128]{2,1,0:T(8,128)(2,1)}, bf16[40,256]{1,0:T(8,128)(2,1)}) custom-call(s32[54]{0:T(128)} %concatenate.21.s_ref, bf16[40,512]{1,0:T(8,128)(2,1)} %copy-done.28, bf16[40,512]{1,0:T(8,128)(2,1)} %copy-done.29, bf16[40,512]{1,0:T(8,128)(2,1)} %copy-done.30, bf16[40,512]{1,0:T(8,128)(2,1)} %copy-done.31, bf16[40,512]{1,0:T(8,128)(2,1)} %copy-done.32, ...), custom_call_target="tpu_custom_call" | custom-call | tf_op jit(solution)/shard_map/pallas_call | solution.py:383
  187.3 7.0 %collective-permute-start.13 = (bf16[13,40,128]{2,1,0:T(8,128)(2,1)}, bf16[13,40,128]{2,1,0:T(8,128)(2,1)S(1)}, u32[]{:S(2)}, u32[]{:S(2)}) collective-permute-start(bf16[13,40,128]{2,1,0:T(8,128)(2,1)} %get-tuple-element.62.srow_ref), channel_id=1, source_target_pairs={{0,3},{1,2},{2,1},{3,0},{124,127},{125,126},{126,125},{127,124}} | collective-permute-start | bytes 399368 | tf_op jit(solution)/shard_map/ppermute | solution.py:632
  198.1 5.0 %collective-permute-done.14.rcol_ref = bf16[40,256]{1,0:T(8,128)(2,1)S(1)} collective-permute-done((bf16[40,256]{1,0:T(8,128)(2,1)}, bf16[40,256]{1,0:T(8,128)(2,1)S(1)}, u32[]{:S(2)}, u32[]{:S(2)}) %collective-permute-start.14) | collective-permute-done | bytes 20512 | tf_op jit(solution)/shard_map/ppermute | solution.py:633
  204.3 2.6 shard_map.285
  206.8 13.6 %shard_map.286 = (bf16[12,16,128,128]{3,2,1,0:T(8,128)(2,1)}, bf16[128,256]{1,0:T(8,128)(2,1)}, bf16[128,256]{1,0:T(8,128)(2,1)}) custom-call(bf16[256,512]{1,0:T(8,128)(2,1)} %bitcast.53, f32[256,1]{1,0:T(8,128)} %copy.47.b_ref, bf16[12,16,40,128]{3,2,1,0:T(8,128)(2,1)} %bitcast.49, bf16[12,40,128]{2,1,0:T(8,128)(2,1)} %get-tuple-element.64.top_ref, ...), custom_call_target="tpu_custom_call" | custom-call | tf_op jit(solution)/shard_map/pallas_call | solution.py:225
  220.7 3.2 %collective-permute-start.16 = (bf16[128,256]{1,0:T(8,128)(2,1)}, bf16[128,256]{1,0:T(8,128)(2,1)S(1)}, u32[]{:S(2)}, u32[]{:S(2)}) collective-permute-start(bf16[128,256]{1,0:T(8,128)(2,1)} %get-tuple-element.70.low_ref), channel_id=1, source_target_pairs={{1,0},{2,1},{3,2},{0,3},{5,4},{6,5},{7,6},{4,7},{9,8},{10,9},{11,1... | collective-permute-start | bytes 196616 | tf_op jit(solution)/shard_map/ppermute | solution.py:606
  223.9 2.4 collective-permute-done.15.left_ref
  227.0 2.4 shard_map.287
  229.4 5.1 %collective-permute-start.18 = (bf16[13,128,128]{2,1,0:T(8,128)(2,1)}, bf16[13,128,128]{2,1,0:T(8,128)(2,1)S(1)}, u32[]{:S(2)}, u32[]{:S(2)}) collective-permute-start(bf16[13,128,128]{2,1,0:T(8,128)(2,1)} %get-tuple-element.71.up_ref.refs_11_), channel_id=1, source_target_pairs={{4,0},{8,4},{12,8},{16,12},{20,16},{24,20},{28,24},{32,28},{36,32}... | collective-permute-start | bytes 1277960 | tf_op jit(solution)/shard_map/ppermute | solution.py:610
  234.4 6.0 %collective-permute-done.17.top_ref.refs_13_ = bf16[13,128,128]{2,1,0:T(8,128)(2,1)S(1)} collective-permute-done((bf16[13,128,128]{2,1,0:T(8,128)(2,1)}, bf16[13,128,128]{2,1,0:T(8,128)(2,1)S(1)}, u32[]{:S(2)}, u32[]{:S(2)}) %collective-permute-start.17) | collective-permute-done | bytes 426016 | tf_op jit(solution)/shard_map/ppermute | solution.py:609
  242.1 5.6 %shard_map.288 = (bf16[128,512]{1,0:T(8,128)(2,1)}, bf16[128,512]{1,0:T(8,128)(2,1)}, bf16[128,512]{1,0:T(8,128)(2,1)}, bf16[128,512]{1,0:T(8,128)(2,1)}, bf16[1...) custom-call(s32[54]{0:T(128)} %concatenate.21.s_ref, ...), custom_call_target="tpu_custom_call" | custom-call | tf_op jit(solution)/shard_map/pallas_call | solution.py:383
  247.7 6.2 %collective-permute-start.19 = (bf16[128,512]{1,0:T(8,128)(2,1)}, bf16[128,512]{1,0:T(8,128)(2,1)S(1)}, u32[]{:S(2)}, u32[]{:S(2)}) collective-permute-start(bf16[128,512]{1,0:T(8,128)(2,1)} %get-tuple-element.73), channel_id=1, source_target_pairs={{0,124},{1,32},{32,1},{125,35},{35,125},{2,64},{64,2},{126,67},{67... | collective-permute-start | bytes 393224 | tf_op jit(solution)/shard_map/ppermute | solution.py:618
  267.4 3.1 collective-permute-start.27
  274.0 4.7 %shard_map.289 = (bf16[13,128,128]{2,1,0:T(8,128)(2,1)}, bf16[128,256]{1,0:T(8,128)(2,1)}) custom-call(s32[54]{0:T(128)} %concatenate.21.s_ref, bf16[128,512]{1,0:T(8,128)(2,1)} %copy-done.12, bf16[128,512]{1,0:T(8,128)(2,1)} %copy-done.13, bf16[128,512]{1,0:T(8,128)(2,1)} %copy-done.14, bf16[128,512]{1,0:T(8,128)(2,1)} %copy-done.15, ...), custom_call_target="tpu_custom_call" | custom-call | tf_op jit(solution)/shard_map/pallas_call | solution.py:383
  278.7 7.2 %collective-permute-start.28 = (bf16[13,128,128]{2,1,0:T(8,128)(2,1)}, bf16[13,128,128]{2,1,0:T(8,128)(2,1)S(1)}, u32[]{:S(2)}, u32[]{:S(2)}) collective-permute-start(bf16[13,128,128]{2,1,0:T(8,128)(2,1)} %get-tuple-element.83.srow_ref), channel_id=1, source_target_pairs={{0,3},{1,2},{2,1},{3,0},{124,127},{125,126},{126,125},{127,124}} | collective-permute-start | bytes 1277960 | tf_op jit(solution)/shard_map/ppermute | solution.py:632
  288.0 2.2 collective-permute-start.29
  291.0 6.1 %collective-permute-done.29.rcol_ref = bf16[128,256]{1,0:T(8,128)(2,1)S(1)} collective-permute-done((bf16[128,256]{1,0:T(8,128)(2,1)}, bf16[128,256]{1,0:T(8,128)(2,1)S(1)}, u32[]{:S(2)}, u32[]{:S(2)}) %collective-permute-start.29) | collective-permute-done | bytes 65568 | tf_op jit(solution)/shard_map/ppermute | solution.py:633
  298.4 2.9 shard_map.290
  301.4 18.7 %shard_map.291 = bf16[128,12,16,128]{3,2,1,0:T(8,128)(2,1)} custom-call(bf16[256,1536]{1,0:T(8,128)(2,1)} %bitcast.50, f32[256,1]{1,0:T(8,128)} %copy.48.b_ref, bf16[12,16,128,128]{3,2,1,0:T(8,128)(2,1)} %get-tuple-element.68.first_ref.last_ref.x_ref, bf16[12,128,128]{2,1,0:T(8,128)(2,1)} %get-tuple-element.85.top_ref, ...), custom_call_target="tpu_custom_call" | custom-call | tf_op jit(solution)/shard_map/pallas_call | solution.py:225
  (184 shorter events, 54.4 us)
Async XLA Ops:
  14.5 108.6 %all-to-all-start = ((bf16[128,31,8,128]{3,2,1,0:T(8,128)(2,1)}), bf16[128,31,8,128]{3,2,1,0:T(8,128)(2,1)}, u32[]{:S(2)}, u32[]{:S(2)}) async-start(bf16[128,31,8,128]{3,2,1,0:T(8,128)(2,1)} %shard_map.280), calls=%async_computation | async-start | bytes 16252928 | tf_op jit(solution)/shard_map/all_to_all | solution.py:681
  26.2 142.2 %copy-start.21 = (bf16[9,128,40]{1,2,0:T(8,128)(2,1)S(1)}, bf16[9,128,40]{1,2,0:T(8,128)(2,1)}, u32[]{:S(2)}) copy-start(bf16[9,128,40]{1,2,0:T(8,128)(2,1)} %param.35) | copy-start | bytes 276484
  135.4 5.2 %collective-permute-start = (bf16[40,256]{1,0:T(8,128)(2,1)}, bf16[40,256]{1,0:T(8,128)(2,1)S(1)}, u32[]{:S(2)}, u32[]{:S(2)}) collective-permute-start(bf16[40,256]{1,0:T(8,128)(2,1)} %get-tuple-element.48.high_ref), channel_id=1, source_target_pairs={{0,1},{1,2},{2,3},{3,0},{4,5},{5,6},{6,7},{7,4},{8,9},{9,10},{10,1... | collective-permute-start | bytes 61448 | tf_op jit(solution)/shard_map/ppermute | solution.py:605
  135.4 5.2 %collective-permute-start.1 = (bf16[40,256]{1,0:T(8,128)(2,1)}, bf16[40,256]{1,0:T(8,128)(2,1)S(1)}, u32[]{:S(2)}, u32[]{:S(2)}) collective-permute-start(bf16[40,256]{1,0:T(8,128)(2,1)} %get-tuple-element.49.low_ref), channel_id=1, source_target_pairs={{1,0},{2,1},{3,2},{0,3},{5,4},{6,5},{7,6},{4,7},{9,8},{10,9},{11,1... | collective-permute-start | bytes 61448 | tf_op jit(solution)/shard_map/ppermute | solution.py:606
  143.2 7.9 %collective-permute-start.2 = (bf16[13,40,128]{2,1,0:T(8,128)(2,1)}, bf16[13,40,128]{2,1,0:T(8,128)(2,1)S(1)}, u32[]{:S(2)}, u32[]{:S(2)}) collective-permute-start(bf16[13,40,128]{2,1,0:T(8,128)(2,1)} %get-tuple-element.51.down_ref.refs_12_), channel_id=1, source_target_pairs={{0,4},{4,8},{8,12},{12,16},{16,20},{20,24},{24,28},{28,32},{32,36}... | collective-permute-start | bytes 399368 | tf_op jit(solution)/shard_map/ppermute | solution.py:609
  143.2 7.9 %collective-permute-start.3 = (bf16[13,40,128]{2,1,0:T(8,128)(2,1)}, bf16[13,40,128]{2,1,0:T(8,128)(2,1)S(1)}, u32[]{:S(2)}, u32[]{:S(2)}) collective-permute-start(bf16[13,40,128]{2,1,0:T(8,128)(2,1)} %get-tuple-element.50.up_ref.refs_11_), channel_id=1, source_target_pairs={{4,0},{8,4},{12,8},{16,12},{20,16},{24,20},{28,24},{32,28},{36,32}... | collective-permute-start | bytes 399368 | tf_op jit(solution)/shard_map/ppermute | solution.py:610
  156.2 14.1 %collective-permute-start.10 = (bf16[40,512]{1,0:T(8,128)(2,1)}, bf16[40,512]{1,0:T(8,128)(2,1)S(1)}, u32[]{:S(2)}, u32[]{:S(2)}) collective-permute-start(bf16[40,512]{1,0:T(8,128)(2,1)} %get-tuple-element.58), channel_id=1, source_target_pairs={{0,24},{24,0},{124,27},{27,124},{1,56},{56,1},{125,59},{59,125},{2... | collective-permute-start | bytes 122888 | tf_op jit(solution)/shard_map/ppermute | solution.py:618
  158.1 14.1 %collective-permute-start.11 = (bf16[40,512]{1,0:T(8,128)(2,1)}, bf16[40,512]{1,0:T(8,128)(2,1)S(1)}, u32[]{:S(2)}, u32[]{:S(2)}) collective-permute-start(bf16[40,512]{1,0:T(8,128)(2,1)} %get-tuple-element.59), channel_id=1, source_target_pairs={{127,3},{0,28},{28,0},{124,31},{31,124},{1,60},{60,1},{125,63},{63... | collective-permute-start | bytes 122888 | tf_op jit(solution)/shard_map/ppermute | solution.py:618
  160.1 14.1 %collective-permute-start.12 = (bf16[40,512]{1,0:T(8,128)(2,1)}, bf16[40,512]{1,0:T(8,128)(2,1)S(1)}, u32[]{:S(2)}, u32[]{:S(2)}) collective-permute-start(bf16[40,512]{1,0:T(8,128)(2,1)} %get-tuple-element.60.refs_9_), channel_id=1, source_target_pairs={{0,3},{127,124}} | collective-permute-start | bytes 122888 | tf_op jit(solution)/shard_map/ppermute | solution.py:618
  164.6 11.6 %collective-permute-start.4 = (bf16[40,512]{1,0:T(8,128)(2,1)}, bf16[40,512]{1,0:T(8,128)(2,1)S(1)}, u32[]{:S(2)}, u32[]{:S(2)}) collective-permute-start(bf16[40,512]{1,0:T(8,128)(2,1)} %get-tuple-element.52), channel_id=1, source_target_pairs={{0,124},{1,32},{32,1},{125,35},{35,125},{2,64},{64,2},{126,67},{67... | collective-permute-start | bytes 122888 | tf_op jit(solution)/shard_map/ppermute | solution.py:618
  168.4 9.8 %collective-permute-start.5 = (bf16[40,512]{1,0:T(8,128)(2,1)}, bf16[40,512]{1,0:T(8,128)(2,1)S(1)}, u32[]{:S(2)}, u32[]{:S(2)}) collective-permute-start(bf16[40,512]{1,0:T(8,128)(2,1)} %get-tuple-element.53), channel_id=1, source_target_pairs={{0,4},{4,0},{124,7},{7,124},{1,36},{36,1},{125,39},{39,125},{2,68}... | collective-permute-start | bytes 122888 | tf_op jit(solution)/shard_map/ppermute | solution.py:618
  170.3 7.8 %collective-permute-start.6 = (bf16[40,512]{1,0:T(8,128)(2,1)}, bf16[40,512]{1,0:T(8,128)(2,1)S(1)}, u32[]{:S(2)}, u32[]{:S(2)}) collective-permute-start(bf16[40,512]{1,0:T(8,128)(2,1)} %get-tuple-element.54), channel_id=1, source_target_pairs={{0,8},{8,0},{124,11},{11,124},{1,40},{40,1},{125,43},{43,125},{2,7... | collective-permute-start | bytes 122888 | tf_op jit(solution)/shard_map/ppermute | solution.py:618
  172.3 5.9 %collective-permute-start.7 = (bf16[40,512]{1,0:T(8,128)(2,1)}, bf16[40,512]{1,0:T(8,128)(2,1)S(1)}, u32[]{:S(2)}, u32[]{:S(2)}) collective-permute-start(bf16[40,512]{1,0:T(8,128)(2,1)} %get-tuple-element.55), channel_id=1, source_target_pairs={{0,12},{12,0},{124,15},{15,124},{1,44},{44,1},{125,47},{47,125},{2... | collective-permute-start | bytes 122888 | tf_op jit(solution)/shard_map/ppermute | solution.py:618
  174.2 7.6 %collective-permute-start.8 = (bf16[40,512]{1,0:T(8,128)(2,1)}, bf16[40,512]{1,0:T(8,128)(2,1)S(1)}, u32[]{:S(2)}, u32[]{:S(2)}) collective-permute-start(bf16[40,512]{1,0:T(8,128)(2,1)} %get-tuple-element.56), channel_id=1, source_target_pairs={{0,16},{16,0},{124,19},{19,124},{1,48},{48,1},{125,51},{51,125},{2... | collective-permute-start | bytes 122888 | tf_op jit(solution)/shard_map/ppermute | solution.py:618
  176.1 7.0 %collective-permute-start.9 = (bf16[40,512]{1,0:T(8,128)(2,1)}, bf16[40,512]{1,0:T(8,128)(2,1)S(1)}, u32[]{:S(2)}, u32[]{:S(2)}) collective-permute-start(bf16[40,512]{1,0:T(8,128)(2,1)} %get-tuple-element.57), channel_id=1, source_target_pairs={{0,20},{20,0},{124,23},{23,124},{1,52},{52,1},{125,55},{55,125},{2... | collective-permute-start | bytes 122888 | tf_op jit(solution)/shard_map/ppermute | solution.py:618
  187.3 15.7 %collective-permute-start.13 = (bf16[13,40,128]{2,1,0:T(8,128)(2,1)}, bf16[13,40,128]{2,1,0:T(8,128)(2,1)S(1)}, u32[]{:S(2)}, u32[]{:S(2)}) collective-permute-start(bf16[13,40,128]{2,1,0:T(8,128)(2,1)} %get-tuple-element.62.srow_ref), channel_id=1, source_target_pairs={{0,3},{1,2},{2,1},{3,0},{124,127},{125,126},{126,125},{127,124}} | collective-permute-start | bytes 399368 | tf_op jit(solution)/shard_map/ppermute | solution.py:632
  194.4 8.6 %collective-permute-start.14 = (bf16[40,256]{1,0:T(8,128)(2,1)}, bf16[40,256]{1,0:T(8,128)(2,1)S(1)}, u32[]{:S(2)}, u32[]{:S(2)}) collective-permute-start(bf16[40,256]{1,0:T(8,128)(2,1)} %get-tuple-element.63.scol_ref), channel_id=1, source_target_pairs={{0,124},{3,127},{4,120},{7,123},{8,116},{11,119},{12,112},{15,115}... | collective-permute-start | bytes 61448 | tf_op jit(solution)/shard_map/ppermute | solution.py:633
  220.4 5.9 %collective-permute-start.15 = (bf16[128,256]{1,0:T(8,128)(2,1)}, bf16[128,256]{1,0:T(8,128)(2,1)S(1)}, u32[]{:S(2)}, u32[]{:S(2)}) collective-permute-start(bf16[128,256]{1,0:T(8,128)(2,1)} %get-tuple-element.69.high_ref), channel_id=1, source_target_pairs={{0,1},{1,2},{2,3},{3,0},{4,5},{5,6},{6,7},{7,4},{8,9},{9,10},{10,1... | collective-permute-start | bytes 196616 | tf_op jit(solution)/shard_map/ppermute | solution.py:605
  220.7 5.7 %collective-permute-start.16 = (bf16[128,256]{1,0:T(8,128)(2,1)}, bf16[128,256]{1,0:T(8,128)(2,1)S(1)}, u32[]{:S(2)}, u32[]{:S(2)}) collective-permute-start(bf16[128,256]{1,0:T(8,128)(2,1)} %get-tuple-element.70.low_ref), channel_id=1, source_target_pairs={{1,0},{2,1},{3,2},{0,3},{5,4},{6,5},{7,6},{4,7},{9,8},{10,9},{11,1... | collective-permute-start | bytes 196616 | tf_op jit(solution)/shard_map/ppermute | solution.py:606
  229.3 11.1 %collective-permute-start.17 = (bf16[13,128,128]{2,1,0:T(8,128)(2,1)}, bf16[13,128,128]{2,1,0:T(8,128)(2,1)S(1)}, u32[]{:S(2)}, u32[]{:S(2)}) collective-permute-start(bf16[13,128,128]{2,1,0:T(8,128)(2,1)} %get-tuple-element.72.down_ref.refs_12_), channel_id=1, source_target_pairs={{0,4},{4,8},{8,12},{12,16},{16,20},{20,24},{24,28},{28,32},{32,36}... | collective-permute-start | bytes 1277960 | tf_op jit(solution)/shard_map/ppermute | solution.py:609
  229.4 11.1 %collective-permute-start.18 = (bf16[13,128,128]{2,1,0:T(8,128)(2,1)}, bf16[13,128,128]{2,1,0:T(8,128)(2,1)S(1)}, u32[]{:S(2)}, u32[]{:S(2)}) collective-permute-start(bf16[13,128,128]{2,1,0:T(8,128)(2,1)} %get-tuple-element.71.up_ref.refs_11_), channel_id=1, source_target_pairs={{4,0},{8,4},{12,8},{16,12},{20,16},{24,20},{28,24},{32,28},{36,32}... | collective-permute-start | bytes 1277960 | tf_op jit(solution)/shard_map/ppermute | solution.py:610
  247.7 13.9 %collective-permute-start.19 = (bf16[128,512]{1,0:T(8,128)(2,1)}, bf16[128,512]{1,0:T(8,128)(2,1)S(1)}, u32[]{:S(2)}, u32[]{:S(2)}) collective-permute-start(bf16[128,512]{1,0:T(8,128)(2,1)} %get-tuple-element.73), channel_id=1, source_target_pairs={{0,124},{1,32},{32,1},{125,35},{35,125},{2,64},{64,2},{126,67},{67... | collective-permute-start | bytes 393224 | tf_op jit(solution)/shard_map/ppermute | solution.py:618
  253.8 9.7 %collective-permute-start.20 = (bf16[128,512]{1,0:T(8,128)(2,1)}, bf16[128,512]{1,0:T(8,128)(2,1)S(1)}, u32[]{:S(2)}, u32[]{:S(2)}) collective-permute-start(bf16[128,512]{1,0:T(8,128)(2,1)} %get-tuple-element.74), channel_id=1, source_target_pairs={{0,4},{4,0},{124,7},{7,124},{1,36},{36,1},{125,39},{39,125},{2,68}... | collective-permute-start | bytes 393224 | tf_op jit(solution)/shard_map/ppermute | solution.py:618
  255.8 9.7 %collective-permute-start.21 = (bf16[128,512]{1,0:T(8,128)(2,1)}, bf16[128,512]{1,0:T(8,128)(2,1)S(1)}, u32[]{:S(2)}, u32[]{:S(2)}) collective-permute-start(bf16[128,512]{1,0:T(8,128)(2,1)} %get-tuple-element.75), channel_id=1, source_target_pairs={{0,8},{8,0},{124,11},{11,124},{1,40},{40,1},{125,43},{43,125},{2,7... | collective-permute-start | bytes 393224 | tf_op jit(solution)/shard_map/ppermute | solution.py:618
  257.7 9.7 %collective-permute-start.22 = (bf16[128,512]{1,0:T(8,128)(2,1)}, bf16[128,512]{1,0:T(8,128)(2,1)S(1)}, u32[]{:S(2)}, u32[]{:S(2)}) collective-permute-start(bf16[128,512]{1,0:T(8,128)(2,1)} %get-tuple-element.76), channel_id=1, source_target_pairs={{0,12},{12,0},{124,15},{15,124},{1,44},{44,1},{125,47},{47,125},{2... | collective-permute-start | bytes 393224 | tf_op jit(solution)/shard_map/ppermute | solution.py:618
  259.6 10.9 %collective-permute-start.23 = (bf16[128,512]{1,0:T(8,128)(2,1)}, bf16[128,512]{1,0:T(8,128)(2,1)S(1)}, u32[]{:S(2)}, u32[]{:S(2)}) collective-permute-start(bf16[128,512]{1,0:T(8,128)(2,1)} %get-tuple-element.77), channel_id=1, source_target_pairs={{0,16},{16,0},{124,19},{19,124},{1,48},{48,1},{125,51},{51,125},{2... | collective-permute-start | bytes 393224 | tf_op jit(solution)/shard_map/ppermute | solution.py:618
  261.6 9.0 %collective-permute-start.24 = (bf16[128,512]{1,0:T(8,128)(2,1)}, bf16[128,512]{1,0:T(8,128)(2,1)S(1)}, u32[]{:S(2)}, u32[]{:S(2)}) collective-permute-start(bf16[128,512]{1,0:T(8,128)(2,1)} %get-tuple-element.78), channel_id=1, source_target_pairs={{0,20},{20,0},{124,23},{23,124},{1,52},{52,1},{125,55},{55,125},{2... | collective-permute-start | bytes 393224 | tf_op jit(solution)/shard_map/ppermute | solution.py:618
  263.5 8.3 %collective-permute-start.25 = (bf16[128,512]{1,0:T(8,128)(2,1)}, bf16[128,512]{1,0:T(8,128)(2,1)S(1)}, u32[]{:S(2)}, u32[]{:S(2)}) collective-permute-start(bf16[128,512]{1,0:T(8,128)(2,1)} %get-tuple-element.79), channel_id=1, source_target_pairs={{0,24},{24,0},{124,27},{27,124},{1,56},{56,1},{125,59},{59,125},{2... | collective-permute-start | bytes 393224 | tf_op jit(solution)/shard_map/ppermute | solution.py:618
  265.5 7.7 %collective-permute-start.26 = (bf16[128,512]{1,0:T(8,128)(2,1)}, bf16[128,512]{1,0:T(8,128)(2,1)S(1)}, u32[]{:S(2)}, u32[]{:S(2)}) collective-permute-start(bf16[128,512]{1,0:T(8,128)(2,1)} %get-tuple-element.80), channel_id=1, source_target_pairs={{127,3},{0,28},{28,0},{124,31},{31,124},{1,60},{60,1},{125,63},{63... | collective-permute-start | bytes 393224 | tf_op jit(solution)/shard_map/ppermute | solution.py:618
  267.4 6.0 %collective-permute-start.27 = (bf16[128,512]{1,0:T(8,128)(2,1)}, bf16[128,512]{1,0:T(8,128)(2,1)S(1)}, u32[]{:S(2)}, u32[]{:S(2)}) collective-permute-start(bf16[128,512]{1,0:T(8,128)(2,1)} %get-tuple-element.81.refs_9_), channel_id=1, source_target_pairs={{0,3},{127,124}} | collective-permute-start | bytes 393224 | tf_op jit(solution)/shard_map/ppermute | solution.py:618
  278.7 18.3 %collective-permute-start.28 = (bf16[13,128,128]{2,1,0:T(8,128)(2,1)}, bf16[13,128,128]{2,1,0:T(8,128)(2,1)S(1)}, u32[]{:S(2)}, u32[]{:S(2)}) collective-permute-start(bf16[13,128,128]{2,1,0:T(8,128)(2,1)} %get-tuple-element.83.srow_ref), channel_id=1, source_target_pairs={{0,3},{1,2},{2,1},{3,0},{124,127},{125,126},{126,125},{127,124}} | collective-permute-start | bytes 1277960 | tf_op jit(solution)/shard_map/ppermute | solution.py:632
  288.0 9.1 %collective-permute-start.29 = (bf16[128,256]{1,0:T(8,128)(2,1)}, bf16[128,256]{1,0:T(8,128)(2,1)S(1)}, u32[]{:S(2)}, u32[]{:S(2)}) collective-permute-start(bf16[128,256]{1,0:T(8,128)(2,1)} %get-tuple-element.84.scol_ref), channel_id=1, source_target_pairs={{0,124},{3,127},{4,120},{7,123},{8,116},{11,119},{12,112},{15,115}... | collective-permute-start | bytes 196616 | tf_op jit(solution)/shard_map/ppermute | solution.py:633
  (46 other events, 678.6 us)
